TPU v7x, 1024 devices: a whole 8x8x8 slice. The times are simulated.
1024 devices in a mesh: dp: 128 (over x_lo, y, z), expert: 8 (over x_hi, core).
Axes of the slice: x: 8 (x_hi: 4, x_lo: 2; x = x_hi * 2 + x_lo), y: 8, z: 8, core: 2. Of those that a mesh axis runs over, the one named last changes fastest.
Arguments:
- cotangent: bfloat16 [131072, 4096], P(('dp', 'expert')), may hold values from -6 to 6
- gate_up: bfloat16 [131072, 1, 1536], P(('dp', 'expert')), may hold values from -6 to 6
- route_probs: bfloat16 [131072, 1], P(('dp', 'expert')), may hold values from 0.049804688 to 0.59765625
- routes: int32 [131072, 1], P(('dp', 'expert')), may hold values from 0 to 7; in each aligned block of 128 rows (0 to 127, 128 to 255, ...) at most 20 rows name the same one
- down_weight: bfloat16 [8, 4096, 768], P('expert', 'dp'), may hold values from -0.09375 to 0.09375
Outputs:
- grad_gate_up: bfloat16 [131072, 1, 1536], P(('dp', 'expert'))
- grad_probs: bfloat16 [131072, 1], P(('dp', 'expert'))
Inputs may be any that keep to these rules, and one draw needn't show every extreme that they name: `routes`: each token names exactly one expert; among the 128 tokens of one device no expert is named by more than 20 tokens, and on some device some expert is named by exactly 20.
All inputs are finite; a program needn't handle non-finite values.
Results may differ from a plain program's by a relative error of at most 0.015.
Values may be sent and summed in bfloat16 or wider, within the bound.
No kernel may reach another device: no remote copies, remote signals or barrier semaphores. Data moves between devices by JAX's collectives and lax.ppermute only.
A program may use at most 32 MiB of HBM per device.

v0:
```python
import jax
import jax.numpy as jnp
from jax import lax
from jax.sharding import PartitionSpec as P

D = 4096
FFW = 768
TOP_WIN = 1


def activation(pre_act):
    gate_pre = pre_act[..., :FFW].astype(jnp.float32)
    up_value = pre_act[..., FFW:].astype(jnp.float32)
    squash = jax.nn.sigmoid(gate_pre)
    return (gate_pre, up_value, squash)


def backward_gates(back_hidden, row_scale, gate_pre, up_value, squash):
    scaled = row_scale[:, None] * back_hidden
    grad_gate = scaled * up_value * squash * (1.0 + gate_pre * (1.0 - squash))
    grad_up = scaled * gate_pre * squash
    return jnp.concatenate([grad_gate, grad_up], axis=-1).astype(jnp.bfloat16)


def body(cotangent, gate_up, route_probs, routes, down_weight):
    tokens = cotangent.shape[0]
    groups = lax.axis_size("expert")
    capacity = tokens * TOP_WIN // groups + tokens // 32
    slot_count = groups * capacity
    route_rows = tokens * TOP_WIN
    flat_routes = routes.reshape(route_rows)
    member = (flat_routes[:, None] == jnp.arange(groups, dtype=jnp.int32)[None, :]).astype(
        jnp.int32
    )
    order_rank = jnp.sum(jnp.cumsum(member, axis=0) * member, axis=1) - 1
    target = flat_routes * capacity + order_rank
    placing = jnp.arange(slot_count, dtype=jnp.int32)[:, None] == target[None, :]
    placing_rows = placing.astype(jnp.bfloat16)
    placing_tokens = jnp.sum(
        placing.reshape(slot_count, tokens, TOP_WIN).astype(jnp.int32), axis=2
    ).astype(jnp.bfloat16)
    rows_cot = (
        jnp.dot(placing_tokens, cotangent, preferred_element_type=jnp.float32)
        .astype(jnp.bfloat16)
        .reshape(groups, capacity, D)
    )
    back_dims = (((0,), (0,)), ((), ()))
    flat_pre = gate_up.reshape(route_rows, 2 * FFW)
    rows_pre = (
        jnp.dot(placing_rows, flat_pre, preferred_element_type=jnp.float32)
        .astype(jnp.bfloat16)
        .reshape(groups, capacity, 2 * FFW)
    )
    rows_prob = (
        jnp.dot(placing_rows, route_probs, preferred_element_type=jnp.float32)
        .astype(jnp.bfloat16)
        .reshape(groups, capacity)
    )
    slot_cot, slot_pre, slot_prob = (
        lax.all_to_all(rows_cot, "expert", split_axis=0, concat_axis=0, tiled=True),
        lax.all_to_all(rows_pre, "expert", split_axis=0, concat_axis=0, tiled=True),
        lax.all_to_all(rows_prob, "expert", split_axis=0, concat_axis=0, tiled=True),
    )
    slot_rows = slot_cot.reshape(slot_count, D)
    gate_pre, up_value, squash = activation(slot_pre.reshape(slot_count, 2 * FFW))
    hidden = (gate_pre * squash * up_value).astype(jnp.bfloat16)
    weight_rows = lax.all_gather(down_weight, "dp", axis=1, tiled=True)[0]
    back_hidden = jnp.dot(slot_rows, weight_rows, preferred_element_type=jnp.float32)
    inner = jnp.sum(hidden.astype(jnp.float32) * back_hidden, axis=1)
    slot_scale = slot_prob.reshape(slot_count).astype(jnp.float32)
    slot_grads = backward_gates(back_hidden, slot_scale, gate_pre, up_value, squash).reshape(
        groups, capacity, 2 * FFW
    )
    prob_grads = inner.astype(jnp.bfloat16).reshape(groups, capacity)
    came_grads, came_probs = (
        lax.all_to_all(slot_grads, "expert", split_axis=0, concat_axis=0, tiled=True),
        lax.all_to_all(prob_grads, "expert", split_axis=0, concat_axis=0, tiled=True),
    )
    grad_rows = lax.dot_general(
        placing_rows,
        came_grads.reshape(slot_count, 2 * FFW),
        back_dims,
        preferred_element_type=jnp.float32,
    ).astype(jnp.bfloat16)
    prob_rows = lax.dot_general(
        placing_rows,
        came_probs.reshape(slot_count, 1),
        back_dims,
        preferred_element_type=jnp.float32,
    )
    grad_probs = prob_rows.astype(jnp.bfloat16)
    return (grad_rows.reshape(tokens, TOP_WIN, 2 * FFW), grad_probs)


def solution(mesh):
    placed = (
        P(("dp", "expert"), None),
        P(("dp", "expert"), None, None),
        P(("dp", "expert"), None),
        P(("dp", "expert"), None),
        P("expert", "dp", None),
    )
    return jax.shard_map(
        body,
        mesh=mesh,
        in_specs=placed,
        out_specs=(P(("dp", "expert"), None, None), P(("dp", "expert"), None)),
        check_vma=False,
    )
```

profile of v0, /device:TPU:1, one launch (start us, length us, event | category | flops | bytes accessed | tf_op | source)
XLA Modules:
  0.0 679.9 jit_solution(9290463952741847470)
XLA Ops:
  7.2 0.7 all-gather.2.cloned.1.call-update
  7.9 0.7 fusion.17
  8.7 0.2 reduce_window_sum.11
  8.8 0.8 select_reduce_fusion
  9.7 0.7 add_add_fusion
  10.3 0.8 fusion.16
  11.1 0.7 all_to_all.25
  11.8 17.4 %all-to-all-start = ((bf16[8,1,20]{2,1,0:T(2,128)(2,1)}), bf16[8,1,20]{2,1,0:T(2,128)(2,1)S(1)}, u32[]{:S(2)}, u32[]{:S(2)}) async-start(bf16[8,1,20]{2,1,0:T(2,128)(2,1)} %all_to_all.25), calls=%async_computation | async-start | bytes 8192 | tf_op jit(solution)/shard_map/all_to_all | solution.py:62
  29.2 1.3 convolution_convert_fusion.1
  30.5 1.0 reshape.104
  31.4 4.7 all-to-all-done
  36.1 4.1 all-to-all-start.2
  40.3 0.5 convolution_convert_fusion
  40.8 1.3 reshape.101
  42.1 12.2 %all-to-all-done.2 = bf16[8,20,1536]{2,1,0:T(8,128)(2,1)S(1)} async-done(((bf16[8,20,1536]{2,1,0:T(8,128)(2,1)}), bf16[8,20,1536]{2,1,0:T(8,128)(2,1)S(1)}, u32[]{:S(2)}, u32[]{:S(2)}) %all-to-all-start.2) | async-done | bytes 491552 | tf_op jit(solution)/shard_map/all_to_all | solution.py:61
  54.3 6.6 all-to-all-start.1
  60.9 0.1 reshape.109
  61.0 0.9 reshape.105
  61.9 36.2 %all-to-all-done.1 = bf16[8,20,4096]{2,1,0:T(8,128)(2,1)S(1)} async-done(((bf16[8,20,4096]{2,1,0:T(8,128)(2,1)}), bf16[8,20,4096]{2,1,0:T(8,128)(2,1)S(1)}, u32[]{:S(2)}, u32[]{:S(2)}) %all-to-all-start.1) | async-done | bytes 1310752 | tf_op jit(solution)/shard_map/all_to_all | solution.py:60
  98.2 1.2 reshape.102
  99.4 449.8 %all-gather.2.cloned.1.call-done = bf16[1,4096,768]{2,1,0:T(8,128)(2,1)} async-done(((bf16[1,32,768]{2,1,0:T(8,128)(2,1)}), bf16[1,4096,768]{2,1,0:T(8,128)(2,1)}) %all-gather.2.cloned.1.call-update) | async-done | bytes 6291472 | tf_op jit(solution)/shard_map/all_gather | solution.py:67
  549.2 4.7 fusion.7
  554.0 0.7 convert_element_type.88
  554.7 91.1 %all-to-all-start.4 = ((bf16[8,1,20]{2,1,0:T(2,128)(2,1)}), bf16[8,1,20]{2,1,0:T(2,128)(2,1)S(1)}, u32[]{:S(2)}, u32[]{:S(2)}) async-start(bf16[8,1,20]{2,1,0:T(2,128)(2,1)} %convert_element_type.88), calls=%async_computation.4 | async-start | bytes 8192 | tf_op jit(solution)/shard_map/all_to_all | solution.py:77
  645.7 0.9 pad_maximum_fusion
  646.6 6.1 all-to-all-done.4
  652.7 4.1 all-to-all-start.3
  656.8 0.1 reshape.112
  656.9 0.7 fusion.4
  657.6 14.4 %all-to-all-done.3 = bf16[8,20,1536]{2,1,0:T(8,128)(2,1)S(1)} async-done(((bf16[8,20,1536]{2,1,0:T(8,128)(2,1)}), bf16[8,20,1536]{2,1,0:T(8,128)(2,1)S(1)}, u32[]{:S(2)}, u32[]{:S(2)}) %all-to-all-start.3) | async-done | bytes 491552 | tf_op jit(solution)/shard_map/all_to_all | solution.py:76
  671.9 0.1 reshape.106
  672.0 1.1 fusion.2
  (10 shorter events, 0.2 us)
Async XLA Ops:
  7.2 33.1 %copy-start = (bf16[128,4096]{1,0:T(8,128)(2,1)S(1)}, bf16[128,4096]{1,0:T(8,128)(2,1)}, u32[]{:S(2)}) copy-start(bf16[128,4096]{1,0:T(8,128)(2,1)} %param.5) | copy-start | bytes 3145732
  7.2 542.0 %all-gather.2.cloned.1.call-start = ((), (), s32[]{:S(2)}) async-start(), calls=%async_computation.5 | async-start | bytes 6340608 | tf_op jit(solution)/shard_map/all_gather | solution.py:67
  11.8 24.3 %all-to-all-start = ((bf16[8,1,20]{2,1,0:T(2,128)(2,1)}), bf16[8,1,20]{2,1,0:T(2,128)(2,1)S(1)}, u32[]{:S(2)}, u32[]{:S(2)}) async-start(bf16[8,1,20]{2,1,0:T(2,128)(2,1)} %all_to_all.25), calls=%async_computation | async-start | bytes 8192 | tf_op jit(solution)/shard_map/all_to_all | solution.py:62
  36.1 18.2 %all-to-all-start.2 = ((bf16[8,20,1536]{2,1,0:T(8,128)(2,1)}), bf16[8,20,1536]{2,1,0:T(8,128)(2,1)S(1)}, u32[]{:S(2)}, u32[]{:S(2)}) async-start(bf16[8,20,1536]{2,1,0:T(8,128)(2,1)} %reshape.104), calls=%async_computation.2 | async-start | bytes 1179648 | tf_op jit(solution)/shard_map/all_to_all | solution.py:61
  54.3 43.8 %all-to-all-start.1 = ((bf16[8,20,4096]{2,1,0:T(8,128)(2,1)}), bf16[8,20,4096]{2,1,0:T(8,128)(2,1)S(1)}, u32[]{:S(2)}, u32[]{:S(2)}) async-start(bf16[8,20,4096]{2,1,0:T(8,128)(2,1)} %reshape.101), calls=%async_computation.1 | async-start | bytes 3145728 | tf_op jit(solution)/shard_map/all_to_all | solution.py:60
  61.9 487.3 %copy-start.1 = (bf16[160,1536]{1,0:T(8,128)(2,1)S(1)}, bf16[160,1536]{1,0:T(8,128)(2,1)}, u32[]{:S(2)}) copy-start(bf16[160,1536]{1,0:T(8,128)(2,1)} %reshape.105) | copy-start | bytes 1474564
  554.7 98.0 %all-to-all-start.4 = ((bf16[8,1,20]{2,1,0:T(2,128)(2,1)}), bf16[8,1,20]{2,1,0:T(2,128)(2,1)S(1)}, u32[]{:S(2)}, u32[]{:S(2)}) async-start(bf16[8,1,20]{2,1,0:T(2,128)(2,1)} %convert_element_type.88), calls=%async_computation.4 | async-start | bytes 8192 | tf_op jit(solution)/shard_map/all_to_all | solution.py:77
  652.7 19.3 %all-to-all-start.3 = ((bf16[8,20,1536]{2,1,0:T(8,128)(2,1)}), bf16[8,20,1536]{2,1,0:T(8,128)(2,1)S(1)}, u32[]{:S(2)}, u32[]{:S(2)}) async-start(bf16[8,20,1536]{2,1,0:T(8,128)(2,1)} %pad_maximum_fusion), calls=%async_computation.3 | async-start | bytes 1179648 | tf_op jit(solution)/shard_map/all_to_all | solution.py:76
Sparse Core Ops, SparseCore 0:
  10.7 538.4 all-gather.1
where the time goes:
time: 683 us; the launch traced here: 680 us
  waiting for transfers between devices  524 us (77%)
  starting transfers between devices  123 us (18%)
  between operations  14.1 us (2%)
  matrix products  8.93 us (1%)
    all_gather x1, waiting for transfers between devices, body(): weight_rows = lax.all_gather(down_weight, 'dp', axis=1, tiled=True)[0]  450 us
    all_to_all x1, starting transfers between devices, body(): lax.all_to_all(prob_grads, 'expert', split_axis=0, concat_axis=0, tiled=T...  91.1 us
    all_to_all x1, waiting for transfers between devices, body(): lax.all_to_all(rows_cot, 'expert', split_axis=0, concat_axis=0, tiled=True)  36.2 us
    all_to_all x1, starting transfers between devices, body(): lax.all_to_all(rows_prob, 'expert', split_axis=0, concat_axis=0, tiled=True)  17.4 us
    all_to_all x1, waiting for transfers between devices, body(): lax.all_to_all(slot_grads, 'expert', split_axis=0, concat_axis=0, tiled=T...  14.4 us
  transfers between devices with their start and end apart: 6, of which 6 were waited for; matrix products, arithmetic and copies ran while one was open for 2% of the time, Pallas kernels for 0%

commit v1 on v0

v1 whole, which is shorter than its diff:
```python
import jax
import jax.numpy as jnp
from jax import lax
from jax.sharding import Mesh, PartitionSpec as P

D = 4096
FFW = 768

AXES = ("xl", "y", "z", "xh", "core")
EXPERT = ("xh", "core")


def body(cotangent, gate_up, route_probs, routes, down_weight):
    tokens = cotangent.shape[0]
    groups = 8
    capacity = tokens // groups + tokens // 32
    slot_count = groups * capacity

    pair = lax.all_gather(down_weight[0], "xl", axis=0, tiled=False)
    weight = lax.all_gather(pair, ("y", "z"), axis=1, tiled=True).reshape(D, FFW)

    flat_routes = routes.reshape(tokens)
    member = (flat_routes[:, None] == jnp.arange(groups, dtype=jnp.int32)[None, :]).astype(jnp.int32)
    rank = jnp.sum(jnp.cumsum(member, axis=0) * member, axis=1) - 1
    target = flat_routes * capacity + rank
    placing = (jnp.arange(slot_count, dtype=jnp.int32)[:, None] == target[None, :]).astype(jnp.bfloat16)

    rows_cot = (
        jnp.dot(placing, cotangent, preferred_element_type=jnp.float32)
        .astype(jnp.bfloat16)
        .reshape(groups, capacity, D)
    )
    slot_rows = lax.all_to_all(rows_cot, EXPERT, split_axis=0, concat_axis=0, tiled=True)

    back = jnp.dot(slot_rows.reshape(slot_count, D), weight, preferred_element_type=jnp.float32)
    back = back.astype(jnp.bfloat16).reshape(groups, capacity, FFW)
    came = lax.all_to_all(back, EXPERT, split_axis=0, concat_axis=0, tiled=True)
    back_hidden = lax.dot_general(
        placing,
        came.reshape(slot_count, FFW),
        (((0,), (0,)), ((), ())),
        preferred_element_type=jnp.float32,
    )

    flat_pre = gate_up.reshape(tokens, 2 * FFW)
    gate = flat_pre[:, :FFW].astype(jnp.float32)
    up = flat_pre[:, FFW:].astype(jnp.float32)
    squash = jax.nn.sigmoid(gate)
    hidden = (gate * squash * up).astype(jnp.bfloat16).astype(jnp.float32)
    grad_probs = jnp.sum(hidden * back_hidden, axis=1, keepdims=True).astype(jnp.bfloat16)
    scaled = route_probs.astype(jnp.float32) * back_hidden
    grad_gate = scaled * up * squash * (1.0 + gate * (1.0 - squash))
    grad_up = scaled * gate * squash
    grads = jnp.concatenate([grad_gate, grad_up], axis=-1).astype(jnp.bfloat16)
    return grads.reshape(tokens, 1, 2 * FFW), grad_probs


def solution(mesh):
    named = Mesh(mesh.devices.reshape(2, 8, 8, 4, 2), AXES)
    dp = ("xl", "y", "z")
    return jax.shard_map(
        body,
        mesh=named,
        in_specs=(
            P(AXES, None),
            P(AXES, None, None),
            P(AXES, None),
            P(AXES, None),
            P(EXPERT, dp, None),
        ),
        out_specs=(P(AXES, None, None), P(AXES, None)),
        check_vma=False,
    )
```

time: 683 us -> 155 us (0.23)
  waiting for transfers between devices: 524 us -> 65.2 us
  starting transfers between devices: 123 us -> 8.08 us
  blocking collectives: 0 us -> 54 us
    all_gather x1, waiting for transfers between devices: 450 us -> 54.1 us  [body(): lax.all_gather(pair, ('y', 'z'), axis=1, tiled=True).reshape(D, FFW)]
    all_to_all x5 -> x1, starting transfers between devices: 123 us -> 8.04 us  [body(): came = lax.all_to_all(back, EXPERT, split_axis=0, concat_axis=0, tiled=True)]
    all_to_all x5 -> x1, waiting for transfers between devices: 73.6 us -> 11.1 us  [body(): came = lax.all_to_all(back, EXPERT, split_axis=0, concat_axis=0, tiled=True)]
    all_to_all x0 -> x1, blocking collectives: none -> 48 us  [body(): lax.all_to_all(rows_cot, EXPERT, split_axis=0, concat_axis=0, tiled=True)]
  transfers between devices with their start and end apart: 6 -> 2, of which waited for: 6 -> 2; matrix products, arithmetic and copies ran while one was open for 2% -> 4% of each run, Pallas kernels for 0% -> 0%
where the time goes in v1:
time: 155 us
  waiting for transfers between devices  65.2 us (42%)
  blocking collectives  54 us (35%)
  between operations  14.1 us (9%)
  starting transfers between devices  8.08 us (5%)
  matrix products  6.56 us (4%)
  local copies, waits for them, and re-layouts  3.79 us (2%)
  other arithmetic  3.17 us (2%)
    all_gather x1, waiting for transfers between devices, body(): lax.all_gather(pair, ('y', 'z'), axis=1, tiled=True).reshape(D, FFW)  54.1 us
    all_to_all x1, blocking collectives, body(): lax.all_to_all(rows_cot, EXPERT, split_axis=0, concat_axis=0, tiled=True)  48 us
    all_to_all x1, waiting for transfers between devices, body(): came = lax.all_to_all(back, EXPERT, split_axis=0, concat_axis=0, tiled=True)  11.1 us
    all_to_all x1, starting transfers between devices, body(): came = lax.all_to_all(back, EXPERT, split_axis=0, concat_axis=0, tiled=True)  8.04 us
    all_gather x1, blocking collectives, body(): pair = lax.all_gather(down_weight[0], 'xl', axis=0, tiled=False)  6.02 us
    dot_general x1, matrix products, body(): jnp.dot(slot_rows.reshape(slot_count, D), weight, preferred_element_type=...  3.98 us
  transfers between devices with their start and end apart: 2, of which 2 were waited for; matrix products, arithmetic and copies ran while one was open for 4% of the time, Pallas kernels for 0%

profile of v1, /device:TPU:1, one launch (start us, length us, event | category | flops | bytes accessed | tf_op | source)
XLA Modules:
  0.0 154.9 jit_solution(6126083290809938284)
XLA Ops:
  7.2 0.0 copy-start
  7.2 0.0 all-gather.2.cloned.1.call-start
  7.2 6.0 %all_gather.6 = bf16[2,32,768]{2,1,0:T(8,128)(2,1)} all-gather(bf16[1,32,768]{2,1,0:T(8,128)(2,1)} %param.9), channel_id=1, replica_groups=mesh['xl'=2,'y'=8,'z'=8,'xh'=4,'core'=2] {'xl'}, dimensions={0}, use_global_device_ids=true | all-gather | bytes 147456 | tf_op jit(solution)/shard_map/all_gather | solution.py:19
  13.2 0.0 all-gather.2.cloned.1.call-update
  13.3 0.7 fusion.13
  14.0 0.2 reduce_window_sum.11
  14.2 0.8 select_reduce_fusion
  15.0 0.7 add_add_fusion
  15.7 0.0 copy-done
  15.7 1.6 %convolution_convert_fusion = bf16[160,4096]{1,0:T(8,128)(2,1)} fusion(bf16[128,4096]{1,0:T(8,128)(2,1)S(1)} %copy-done, s32[128]{0:T(128)S(1)} %add_add_fusion), kind=kOutput, calls=%fused_computation | convolution fusion | flops 168448000 | bytes 2359808 | tf_op jit(solution)/shard_map/dot_general | solution.py:29
  17.3 1.4 reshape.76
  18.7 48.0 %all_to_all.10 = bf16[8,20,4096]{2,1,0:T(8,128)(2,1)} all-to-all(bf16[8,20,4096]{2,1,0:T(8,128)(2,1)S(1)} %reshape.76), channel_id=1, replica_groups=mesh['xl'=2,'y'=8,'z'=8,'xh'=4,'core'=2] {'xh','core'}, dimensions={0} | all-to-all | bytes 2621440 | tf_op jit(solution)/shard_map/all_to_all | solution.py:33
  66.7 1.5 reshape.77
  68.2 54.1 %all-gather.2.cloned.1.call-done = bf16[2,2048,768]{2,1,0:T(8,128)(2,1)} async-done(((bf16[2,32,768]{2,1,0:T(8,128)(2,1)}), bf16[2,2048,768]{2,1,0:T(8,128)(2,1)}) %all-gather.2.cloned.1.call-update) | async-done | bytes 6291472 | tf_op jit(solution)/shard_map/all_gather | solution.py:20
  122.3 0.0 copy-start.2
  122.3 4.0 %convolution_convert_fusion.1 = bf16[160,768]{1,0:T(8,128)(2,1)S(1)} fusion(bf16[160,4096]{1,0:T(8,128)(2,1)S(1)} %reshape.77, bf16[4096,768]{1,0:T(8,128)(2,1)} %bitcast.18), kind=kOutput, calls=%fused_computation.1 | convolution fusion | flops 1006755840 | bytes 7847936 | tf_op jit(solution)/shard_map/dot_general | solution.py:35
  126.3 0.0 copy-start.1
  126.3 0.8 reshape.79
  127.1 8.0 %all-to-all-start.1 = ((bf16[8,20,768]{2,1,0:T(8,128)(2,1)}), bf16[8,20,768]{2,1,0:T(8,128)(2,1)S(1)}, u32[]{:S(2)}, u32[]{:S(2)}) async-start(bf16[8,20,768]{2,1,0:T(8,128)(2,1)} %reshape.79), calls=%async_computation.1 | async-start | bytes 589824 | tf_op jit(solution)/shard_map/all_to_all | solution.py:37
  135.1 0.0 copy-done.2
  135.2 11.1 %all-to-all-done.1 = bf16[8,20,768]{2,1,0:T(8,128)(2,1)S(1)} async-done(((bf16[8,20,768]{2,1,0:T(8,128)(2,1)}), bf16[8,20,768]{2,1,0:T(8,128)(2,1)S(1)}, u32[]{:S(2)}, u32[]{:S(2)}) %all-to-all-start.1) | async-done | bytes 245792 | tf_op jit(solution)/shard_map/all_to_all | solution.py:37
  146.2 0.1 reshape.80
  146.3 0.0 copy-done.1
  146.3 1.0 fusion.11
  147.3 0.8 pad_maximum_fusion
  (1 shorter events, 0.0 us)
Async XLA Ops:
  7.2 8.5 %copy-start = (bf16[128,4096]{1,0:T(8,128)(2,1)S(1)}, bf16[128,4096]{1,0:T(8,128)(2,1)}, u32[]{:S(2)}) copy-start(bf16[128,4096]{1,0:T(8,128)(2,1)} %param.5) | copy-start | bytes 3145732
  7.2 115.2 %all-gather.2.cloned.1.call-start = ((), (), s32[]{:S(2)}) async-start(), calls=%async_computation.2 | async-start | bytes 6389760 | tf_op jit(solution)/shard_map/all_gather | solution.py:20
  122.3 12.8 %copy-start.2 = (bf16[128,1]{0,1:T(2,128)(2,1)S(1)}, bf16[128,1]{0,1:T(2,128)(2,1)}, u32[]{:S(2)}) copy-start(bf16[128,1]{0,1:T(2,128)(2,1)} %param.7) | copy-start | bytes 772
  126.3 20.0 %copy-start.1 = (bf16[128,1,1536]{2,0,1:T(8,128)(2,1)S(1)}, bf16[128,1,1536]{2,0,1:T(8,128)(2,1)}, u32[]{:S(2)}) copy-start(bf16[128,1,1536]{2,0,1:T(8,128)(2,1)} %param.6) | copy-start | bytes 1179652
  127.1 19.1 %all-to-all-start.1 = ((bf16[8,20,768]{2,1,0:T(8,128)(2,1)}), bf16[8,20,768]{2,1,0:T(8,128)(2,1)S(1)}, u32[]{:S(2)}, u32[]{:S(2)}) async-start(bf16[8,20,768]{2,1,0:T(8,128)(2,1)} %reshape.79), calls=%async_computation.1 | async-start | bytes 589824 | tf_op jit(solution)/shard_map/all_to_all | solution.py:37
Sparse Core Ops, SparseCore 0:
  13.4 108.8 all-gather.1

commit v2 on v1

v2 whole, which is shorter than its diff:
```python
import jax
import jax.numpy as jnp
from jax import lax
from jax.sharding import Mesh, PartitionSpec as P

D = 4096
FFW = 768
HALF = D // 2
QUART = D // 4
EXPERTS = 8
CAP = 20
PEERS = 16

AXES = ("xl", "y", "z", "xh", "core")
SHARE = ("xl", "xh", "core")


def onehot(index, rows):
    return (jnp.arange(rows, dtype=jnp.int32)[:, None] == index[None, :]).astype(jnp.bfloat16)


def body(cotangent, gate_up, route_probs, routes, down_weight):
    tokens = cotangent.shape[0]

    weight = lax.all_gather(down_weight[0], ("y", "z"), axis=0, tiled=True)

    flat_routes = routes.reshape(tokens)
    member = (flat_routes[:, None] == jnp.arange(EXPERTS, dtype=jnp.int32)[None, :]).astype(jnp.int32)
    rank = jnp.sum(jnp.cumsum(member, axis=0) * member, axis=1) - 1
    first = flat_routes * (2 * CAP) + rank
    both = jnp.concatenate([first, first + CAP])
    placing = onehot(both, EXPERTS * 2 * CAP)
    quarters = [cotangent[:, i * QUART : (i + 1) * QUART] for i in range(4)]
    sent = jnp.stack(
        [
            jnp.dot(
                placing,
                jnp.concatenate([quarters[2 * h], quarters[2 * h + 1]], axis=0),
                preferred_element_type=jnp.float32,
            ).astype(jnp.bfloat16)
            for h in range(2)
        ]
    ).reshape(PEERS, 2 * CAP, QUART)
    got = lax.all_to_all(sent, SHARE, split_axis=0, concat_axis=0, tiled=True)

    count = PEERS * 2 * CAP
    order = jnp.arange(count, dtype=jnp.int32)
    order = (order % (count // 2)) // CAP * (2 * CAP) + order // (count // 2) * CAP + order % CAP
    swap = onehot(order, count)
    rows = lax.dot_general(
        swap, got.reshape(count, QUART), (((0,), (0,)), ((), ())), preferred_element_type=jnp.float32
    ).astype(jnp.bfloat16)
    back = jnp.dot(rows[: count // 2], weight[:QUART], preferred_element_type=jnp.float32) + jnp.dot(
        rows[count // 2 :], weight[QUART:], preferred_element_type=jnp.float32
    )
    back = back.astype(jnp.bfloat16)
    back = jnp.concatenate([back[:, : FFW // 2], back[:, FFW // 2 :]], axis=0)
    back = jnp.dot(swap, back, preferred_element_type=jnp.float32).astype(jnp.bfloat16)
    came = lax.all_to_all(
        back.reshape(PEERS, 2 * CAP, FFW // 2), SHARE, split_axis=0, concat_axis=0, tiled=True
    ).reshape(count, FFW // 2)

    place = jnp.arange(count, dtype=jnp.int32) % (count // 2)
    back_hidden = jnp.concatenate(
        [
            jnp.dot(
                (place[None, :] == (first + c * CAP)[:, None]).astype(jnp.bfloat16),
                came,
                preferred_element_type=jnp.float32,
            )
            for c in range(2)
        ],
        axis=1,
    )

    flat_pre = gate_up.reshape(tokens, 2 * FFW)
    gate = flat_pre[:, :FFW].astype(jnp.float32)
    up = flat_pre[:, FFW:].astype(jnp.float32)
    squash = jax.nn.sigmoid(gate)
    hidden = (gate * squash * up).astype(jnp.bfloat16).astype(jnp.float32)
    grad_probs = jnp.sum(hidden * back_hidden, axis=1, keepdims=True).astype(jnp.bfloat16)
    scaled = route_probs.astype(jnp.float32) * back_hidden
    grad_gate = scaled * up * squash * (1.0 + gate * (1.0 - squash))
    grad_up = scaled * gate * squash
    grads = jnp.concatenate([grad_gate, grad_up], axis=-1).astype(jnp.bfloat16)
    return grads.reshape(tokens, 1, 2 * FFW), grad_probs


def solution(mesh):
    named = Mesh(mesh.devices.reshape(2, 8, 8, 4, 2), AXES)
    return jax.shard_map(
        body,
        mesh=named,
        in_specs=(
            P(AXES, None),
            P(AXES, None, None),
            P(AXES, None),
            P(AXES, None),
            P(("xh", "core"), ("xl", "y", "z"), None),
        ),
        out_specs=(P(AXES, None, None), P(AXES, None)),
        check_vma=False,
    )
```

time: 155 us -> 155 us (level)
  blocking collectives: 54 us -> 0 us
  waiting for transfers between devices: 65.2 us -> 98.6 us
  starting transfers between devices: 8.08 us -> 28.8 us
  local copies, waits for them, and re-layouts: 3.79 us -> 1.45 us
  other arithmetic: 3.17 us -> 5.24 us
    all_to_all x1 -> x0, blocking collectives: 48 us -> none  [body(): lax.all_to_all(rows_cot, EXPERT, split_axis=0, concat_axis=0, tiled=True)]
    all_to_all x1 -> x2, waiting for transfers between devices: 11.1 us -> 48.3 us  [the longest x1 31.7 us: body(): got = lax.all_to_all(sent, SHARE, split_axis=0, concat_axis=0, tiled=True)]
    all_to_all x1 -> x2, starting transfers between devices: 8.04 us -> 28.8 us  [the longest x1 17.6 us: body(): got = lax.all_to_all(sent, SHARE, split_axis=0, concat_axis=0, tiled=True)]
    all_gather x1 -> x0, blocking collectives: 6.02 us -> none  [body(): pair = lax.all_gather(down_weight[0], 'xl', axis=0, tiled=False)]
    all_gather x1, waiting for transfers between devices: 54.1 us -> 49.7 us  [body(): weight = lax.all_gather(down_weight[0], ('y', 'z'), axis=0, tiled=True)]
    reshape x4 -> x0, local copies, waits for them, and re-layouts: 3.77 us -> none  [the longest x1 1.52 us: body(): slot_rows.reshape(slot_count, D)]
    dot_general x3 -> x8, matrix products: 6.56 us -> 6.85 us  [the longest x1 2.24 us: body(): jnp.dot(rows[count // 2:], weight[QUART:], preferred_element_type=jnp.flo...]
  transfers between devices with their start and end apart: 2 -> 3, of which waited for: 2 -> 3; matrix products, arithmetic and copies ran while one was open for 4% -> 4% of each run, Pallas kernels for 0% -> 0%
where the time goes in v2:
time: 155 us
  waiting for transfers between devices  98.6 us (64%)
  starting transfers between devices  28.8 us (19%)
  between operations  14.2 us (9%)
  matrix products  6.85 us (4%)
  other arithmetic  5.24 us (3%)
    all_gather x1, waiting for transfers between devices, body(): weight = lax.all_gather(down_weight[0], ('y', 'z'), axis=0, tiled=True)  49.7 us
    all_to_all x1, waiting for transfers between devices, body(): got = lax.all_to_all(sent, SHARE, split_axis=0, concat_axis=0, tiled=True)  31.7 us
    all_to_all x1, starting transfers between devices, body(): got = lax.all_to_all(sent, SHARE, split_axis=0, concat_axis=0, tiled=True)  17.6 us
    all_to_all x1, waiting for transfers between devices, body(): lax.all_to_all(back.reshape(PEERS, 2 * CAP, FFW // 2), SHARE, split_axis=...  16.6 us
    all_to_all x1, starting transfers between devices, body(): lax.all_to_all(back.reshape(PEERS, 2 * CAP, FFW // 2), SHARE, split_axis=...  11.1 us
  transfers between devices with their start and end apart: 3, of which 3 were waited for; matrix products, arithmetic and copies ran while one was open for 4% of the time, Pallas kernels for 0%

profile of v2, /device:TPU:1, one launch (start us, length us, event | category | flops | bytes accessed | tf_op | source)
XLA Modules:
  0.0 155.1 jit_solution(5743232288695104756)
XLA Ops:
  7.2 0.0 all-gather.3.cloned.1.call-start
  7.2 0.7 all-gather.3.cloned.1.call-update
  7.9 0.7 fusion.45
  8.6 0.2 reduce_window_sum.11
  8.8 0.8 select_reduce_fusion
  9.6 0.7 broadcast_add_fusion
  10.3 1.3 fusion.65
  11.6 0.3 fusion.8
  12.0 0.3 fusion.9
  12.3 1.2 pad_maximum_fusion
  13.5 17.6 %all-to-all-start = ((bf16[16,40,1024]{2,1,0:T(8,128)(2,1)}), bf16[16,40,1024]{2,1,0:T(8,128)(2,1)S(1)}, u32[]{:S(2)}, u32[]{:S(2)}) async-start(bf16[16,40,1024]{2,1,0:T(8,128)(2,1)} %bitcast.6), calls=%async_computation | async-start | bytes 2621440 | tf_op jit(solution)/shard_map/all_to_all | solution.py:44
  31.1 31.7 %all-to-all-done = bf16[16,40,1024]{2,1,0:T(8,128)(2,1)S(1)} async-done(((bf16[16,40,1024]{2,1,0:T(8,128)(2,1)}), bf16[16,40,1024]{2,1,0:T(8,128)(2,1)S(1)}, u32[]{:S(2)}, u32[]{:S(2)}) %all-to-all-start) | async-done | bytes 1310752 | tf_op jit(solution)/shard_map/all_to_all | solution.py:44
  62.8 1.2 fusion.2
  64.0 49.7 %all-gather.3.cloned.1.call-done = bf16[1,2048,768]{2,1,0:T(8,128)(2,1)} async-done(((bf16[1,32,768]{2,1,0:T(8,128)(2,1)}), bf16[1,2048,768]{2,1,0:T(8,128)(2,1)}) %all-gather.3.cloned.1.call-update) | async-done | bytes 3145744 | tf_op jit(solution)/shard_map/all_gather | solution.py:25
  113.7 0.0 copy-start.2
  113.7 2.2 %fusion.3 = f32[320,768]{1,0:T(8,128)S(1)} fusion(bf16[1,2048,768]{2,1,0:T(8,128)(2,1)} %all-gather.3.cloned.1.call-done, bf16[640,1024]{1,0:T(8,128)(2,1)S(1)} %fusion.2), kind=kOutput, calls=%fused_computation.5 | convolution fusion | flops 503316480 | bytes 3211264 | tf_op jit(solution)/shard_map/dot_general | solution.py:53
  116.0 0.1 copy-done.2
  116.1 0.7 fusion.6
  116.8 0.1 fusion.66
  116.9 0.0 copy-start.3
  116.9 0.0 copy-start.1
  116.9 1.4 fusion.7
  118.3 0.0 copy-start
  118.3 11.1 %all-to-all-start.1 = ((bf16[16,40,384]{2,1,0:T(8,128)(2,1)}), bf16[16,40,384]{2,1,0:T(8,128)(2,1)S(1)}, u32[]{:S(2)}, u32[]{:S(2)}) async-start(bf16[16,40,384]{2,1,0:T(8,128)(2,1)} %bitcast.10), calls=%async_computation.1 | async-start | bytes 983040 | tf_op jit(solution)/shard_map/all_to_all | solution.py:59
  129.4 0.0 copy-done.3
  129.4 0.0 copy-done.1
  129.4 16.6 %all-to-all-done.1 = bf16[16,40,384]{2,1,0:T(8,128)(2,1)S(1)} async-done(((bf16[16,40,384]{2,1,0:T(8,128)(2,1)}), bf16[16,40,384]{2,1,0:T(8,128)(2,1)S(1)}, u32[]{:S(2)}, u32[]{:S(2)}) %all-to-all-start.1) | async-done | bytes 491552 | tf_op jit(solution)/shard_map/all_to_all | solution.py:59
  146.0 0.3 fusion.35
  146.3 0.3 fusion.33
  146.7 0.0 copy-done
  146.7 0.8 fusion.38
  147.5 0.8 pad_maximum_fusion.2
  (5 shorter events, 0.1 us)
Async XLA Ops:
  7.2 106.6 %all-gather.3.cloned.1.call-start = ((), (), s32[]{:S(2)}) async-start(), calls=%async_computation.2 | async-start | bytes 3194880 | tf_op jit(solution)/shard_map/all_gather | solution.py:25
  13.5 49.3 %all-to-all-start = ((bf16[16,40,1024]{2,1,0:T(8,128)(2,1)}), bf16[16,40,1024]{2,1,0:T(8,128)(2,1)S(1)}, u32[]{:S(2)}, u32[]{:S(2)}) async-start(bf16[16,40,1024]{2,1,0:T(8,128)(2,1)} %bitcast.6), calls=%async_computation | async-start | bytes 2621440 | tf_op jit(solution)/shard_map/all_to_all | solution.py:44
  113.7 2.4 %copy-start.2 = (bf16[1,2048,768]{2,1,0:T(8,128)(2,1)S(1)}, bf16[1,2048,768]{2,1,0:T(8,128)(2,1)}, u32[]{:S(2)}) copy-start(bf16[1,2048,768]{2,1,0:T(8,128)(2,1)} %all-gather.3.cloned.1.call-done) | copy-start | bytes 9437188
  116.9 12.5 %copy-start.3 = (bf16[128,1]{0,1:T(2,128)(2,1)S(1)}, bf16[128,1]{0,1:T(2,128)(2,1)}, u32[]{:S(2)}) copy-start(bf16[128,1]{0,1:T(2,128)(2,1)} %param.7) | copy-start | bytes 772
  116.9 12.5 %copy-start.1 = (s32[128,1]{0,1:T(1,128)S(1)}, s32[128,1]{0,1:T(1,128)}, u32[]{:S(2)}) copy-start(s32[128,1]{0,1:T(1,128)} %param.8) | copy-start | bytes 1540
  118.3 28.4 %copy-start = (bf16[128,1,1536]{2,0,1:T(8,128)(2,1)S(1)}, bf16[128,1,1536]{2,0,1:T(8,128)(2,1)}, u32[]{:S(2)}) copy-start(bf16[128,1,1536]{2,0,1:T(8,128)(2,1)} %param.6) | copy-start | bytes 1179652
  118.3 27.8 %all-to-all-start.1 = ((bf16[16,40,384]{2,1,0:T(8,128)(2,1)}), bf16[16,40,384]{2,1,0:T(8,128)(2,1)S(1)}, u32[]{:S(2)}, u32[]{:S(2)}) async-start(bf16[16,40,384]{2,1,0:T(8,128)(2,1)} %bitcast.10), calls=%async_computation.1 | async-start | bytes 983040 | tf_op jit(solution)/shard_map/all_to_all | solution.py:59
Sparse Core Ops, SparseCore 0:
  12.2 101.4 all-gather.2

commit v3 on v2

--- a/solution.py
+++ b/solution.py
@@ -1,6 +1,8 @@
 import jax
 import jax.numpy as jnp
 from jax import lax
+from jax.experimental import pallas as pl
+from jax.experimental.pallas import tpu as pltpu
 from jax.sharding import Mesh, PartitionSpec as P
 
 D = 4096
@@ -14,6 +16,66 @@
 AXES = ("xl", "y", "z", "xh", "core")
 SHARE = ("xl", "xh", "core")
 
+TORUS = ("y", "z", "xh", "core")
+RING = 8
+LINES = [(h, c) for h in range(4) for c in range(2)]
+COUNT = PEERS * 2 * CAP
+
+
+def place_of(y, z, h, c):
+    return (((y % RING) * RING + z % RING) * 4 + h) * 2 + c
+
+
+def first_groups():
+    return [
+        [place_of(k, i, h, c) if c == 0 else place_of(i, k, h, c) for i in range(RING)]
+        for h, c in LINES
+        for k in range(RING)
+    ]
+
+
+def second_shift(step):
+    return [
+        (place_of(y, z, h, c), place_of(y + step, z, h, c) if c == 0 else place_of(y, z + step, h, c))
+        for y in range(RING)
+        for z in range(RING)
+        for h, c in LINES
+    ]
+
+
+def product(got_ref, *refs):
+    parts, out_ref, weight_ref = refs[:RING], refs[RING], refs[RING + 1]
+    y, z, core = lax.axis_index("y"), lax.axis_index("z"), lax.axis_index("core")
+    mine = jnp.where(core == 0, y, z)
+    outer = jnp.where(core == 0, RING, 1)
+    inner = jnp.where(core == 0, 1, RING)
+    for step in range(RING):
+        source = lax.rem(mine + RING - step, RING)
+        for i in range(RING):
+            weight_ref[source * outer + i * inner] = parts[step][i]
+
+    def order(shape, axis):
+        i = lax.broadcasted_iota(jnp.int32, shape, axis)
+        piece = (i >= COUNT // 2).astype(jnp.int32)
+        j = i - piece * (COUNT // 2)
+        source = (j * 3277) >> 16
+        return source * (2 * CAP) + piece * CAP + j - source * CAP
+
+    square = (COUNT, COUNT)
+    take = (lax.broadcasted_iota(jnp.int32, square, 1) == order((COUNT, 1), 0)).astype(jnp.bfloat16)
+    give = (lax.broadcasted_iota(jnp.int32, square, 0) == order((1, COUNT), 1)).astype(jnp.bfloat16)
+    rows = jnp.dot(take, got_ref[...], preferred_element_type=jnp.float32).astype(jnp.bfloat16)
+    half = RING * RING // 2
+    width = weight_ref.shape[1] * half
+    back = jnp.dot(
+        rows[: COUNT // 2], weight_ref[:half].reshape(width, FFW), preferred_element_type=jnp.float32
+    ) + jnp.dot(
+        rows[COUNT // 2 :], weight_ref[half:].reshape(width, FFW), preferred_element_type=jnp.float32
+    )
+    back = back.astype(jnp.bfloat16)
+    back = jnp.concatenate([back[:, : FFW // 2], back[:, FFW // 2 :]], axis=0)
+    out_ref[...] = jnp.dot(give, back, preferred_element_type=jnp.float32).astype(jnp.bfloat16)
+
 
 def onehot(index, rows):
     return (jnp.arange(rows, dtype=jnp.int32)[:, None] == index[None, :]).astype(jnp.bfloat16)
@@ -22,7 +84,16 @@
 def body(cotangent, gate_up, route_probs, routes, down_weight):
     tokens = cotangent.shape[0]
 
-    weight = lax.all_gather(down_weight[0], ("y", "z"), axis=0, tiled=True)
+    own = down_weight[0]
+    line = lax.all_to_all(
+        jnp.broadcast_to(own[None], (RING,) + own.shape),
+        TORUS,
+        split_axis=0,
+        concat_axis=0,
+        axis_index_groups=first_groups(),
+        tiled=True,
+    )
+    parts = [line] + [lax.ppermute(line, TORUS, second_shift(step)) for step in range(1, RING)]
 
     flat_routes = routes.reshape(tokens)
     member = (flat_routes[:, None] == jnp.arange(EXPERTS, dtype=jnp.int32)[None, :]).astype(jnp.int32)
@@ -43,24 +114,20 @@
     ).reshape(PEERS, 2 * CAP, QUART)
     got = lax.all_to_all(sent, SHARE, split_axis=0, concat_axis=0, tiled=True)
 
-    count = PEERS * 2 * CAP
-    order = jnp.arange(count, dtype=jnp.int32)
-    order = (order % (count // 2)) // CAP * (2 * CAP) + order // (count // 2) * CAP + order % CAP
-    swap = onehot(order, count)
-    rows = lax.dot_general(
-        swap, got.reshape(count, QUART), (((0,), (0,)), ((), ())), preferred_element_type=jnp.float32
-    ).astype(jnp.bfloat16)
-    back = jnp.dot(rows[: count // 2], weight[:QUART], preferred_element_type=jnp.float32) + jnp.dot(
-        rows[count // 2 :], weight[QUART:], preferred_element_type=jnp.float32
-    )
-    back = back.astype(jnp.bfloat16)
-    back = jnp.concatenate([back[:, : FFW // 2], back[:, FFW // 2 :]], axis=0)
-    back = jnp.dot(swap, back, preferred_element_type=jnp.float32).astype(jnp.bfloat16)
+    back = pl.pallas_call(
+        product,
+        out_shape=jax.ShapeDtypeStruct((COUNT, FFW // 2), jnp.bfloat16),
+        in_specs=[pl.BlockSpec(memory_space=pltpu.VMEM)] * (RING + 1),
+        out_specs=pl.BlockSpec(memory_space=pltpu.VMEM),
+        scratch_shapes=[pltpu.VMEM((RING * RING,) + own.shape, jnp.bfloat16)],
+        compiler_params=pltpu.CompilerParams(vmem_limit_bytes=20 * 2**20),
+        cost_estimate=pl.CostEstimate(flops=2 * 10**9, bytes_accessed=10**7, transcendentals=0),
+    )(got.reshape(COUNT, QUART), *parts)
     came = lax.all_to_all(
         back.reshape(PEERS, 2 * CAP, FFW // 2), SHARE, split_axis=0, concat_axis=0, tiled=True
-    ).reshape(count, FFW // 2)
+    ).reshape(COUNT, FFW // 2)
 
-    place = jnp.arange(count, dtype=jnp.int32) % (count // 2)
+    place = jnp.arange(COUNT, dtype=jnp.int32) % (COUNT // 2)
     back_hidden = jnp.concatenate(
         [
             jnp.dot(

time: 155 us -> 129 us (0.83); the launches traced: 155 us -> 127 us
  waiting for transfers between devices: 98.6 us -> 47.4 us
  starting transfers between devices: 28.8 us -> 62.7 us
  between operations: 14.2 us -> 0.84 us
  local copies, waits for them, and re-layouts: 1.45 us -> 7.03 us
  matrix products: 6.85 us -> 1.31 us
  Pallas kernels: 0 us -> 4.23 us
    all_gather x1 -> x0, waiting for transfers between devices: 49.7 us -> none  [body(): weight = lax.all_gather(down_weight[0], ('y', 'z'), axis=0, tiled=True)]
    all_to_all x1, waiting for transfers between devices: 31.7 us -> 0.01 us  [body(): got = lax.all_to_all(sent, SHARE, split_axis=0, concat_axis=0, tiled=True)]
    ppermute x0 -> x7, starting transfers between devices: none -> 25.4 us  [body(): lax.ppermute(line, TORUS, second_shift(step))]
    ppermute x0 -> x7, waiting for transfers between devices: none -> 23.2 us  [body(): lax.ppermute(line, TORUS, second_shift(step))]
    all_to_all x0 -> x1, starting transfers between devices: none -> 8.11 us  [body(): lax.all_to_all(jnp.broadcast_to(own[None], (RING,) + own.shape), TORUS, s...]
    all_to_all x0 -> x1, waiting for transfers between devices: none -> 7.6 us  [body(): lax.all_to_all(jnp.broadcast_to(own[None], (RING,) + own.shape), TORUS, s...]
    dot_general x4 -> x0, matrix products: 5.55 us -> none  [the longest x1 2.24 us: body(): jnp.dot(rows[count // 2:], weight[QUART:], preferred_element_type=jnp.flo...]
    unnamed x8 -> x20, local copies, waits for them, and re-layouts: 0.13 us -> 5.29 us
  transfers between devices with their start and end apart: 3 -> 10, of which waited for: 3 -> 6; matrix products, arithmetic and copies ran while one was open for 4% -> 2% of each run, Pallas kernels for 0% -> 0%
where the time goes in v3:
time: 129 us; the launch traced here: 127 us
  starting transfers between devices  62.7 us (49%)
  waiting for transfers between devices  47.4 us (37%)
  local copies, waits for them, and re-layouts  7.03 us (5%)
  Pallas kernels  4.23 us (3%)
  other arithmetic  3.93 us (3%)
  matrix products  1.31 us (1%)
    ppermute x7, starting transfers between devices, body(): lax.ppermute(line, TORUS, second_shift(step))  25.4 us
    ppermute x7, waiting for transfers between devices, body(): lax.ppermute(line, TORUS, second_shift(step))  23.2 us
    all_to_all x1, starting transfers between devices, body(): got = lax.all_to_all(sent, SHARE, split_axis=0, concat_axis=0, tiled=True)  18 us
    all_to_all x1, waiting for transfers between devices, body(): lax.all_to_all(back.reshape(PEERS, 2 * CAP, FFW // 2), SHARE, split_axis=...  16.6 us
    all_to_all x1, starting transfers between devices, body(): lax.all_to_all(back.reshape(PEERS, 2 * CAP, FFW // 2), SHARE, split_axis=...  11.2 us
    all_to_all x1, starting transfers between devices, body(): lax.all_to_all(jnp.broadcast_to(own[None], (RING,) + own.shape), TORUS, s...  8.11 us
    all_to_all x1, waiting for transfers between devices, body(): lax.all_to_all(jnp.broadcast_to(own[None], (RING,) + own.shape), TORUS, s...  7.6 us
    unnamed x20, local copies, waits for them, and re-layouts  5.29 us
  transfers between devices with their start and end apart: 10, of which 6 were waited for; matrix products, arithmetic and copies ran while one was open for 2% of the time, Pallas kernels for 0%

profile of v3, /device:TPU:1, one launch (start us, length us, event | category | flops | bytes accessed | tf_op | source)
XLA Modules:
  0.0 127.4 jit_solution(4587481775439966690)
XLA Ops:
  0.7 1.7 %broadcast_in_dim.5 = bf16[8,32,768]{2,1,0:T(8,128)(2,1)} broadcast(bf16[32,768]{1,0:T(8,128)(2,1)} %bitcast.39), dimensions={1,2} | broadcast | bytes 442368 | tf_op jit(solution)/shard_map/broadcast_in_dim | solution.py:89
  2.3 8.1 %all-to-all-start.1 = ((bf16[8,32,768]{2,1,0:T(8,128)(2,1)}), bf16[8,32,768]{2,1,0:T(8,128)(2,1)S(1)}, u32[]{:S(2)}, u32[]{:S(2)}) async-start(bf16[8,32,768]{2,1,0:T(8,128)(2,1)} %broadcast_in_dim.5), calls=%async_computation.1 | async-start | bytes 786432 | tf_op jit(solution)/shard_map/all_to_all | solution.py:88
  10.4 0.7 fusion.30
  11.6 0.3 fusion
  12.0 0.3 fusion.1
  12.3 1.2 pad_maximum_fusion
  13.6 7.6 %all-to-all-done.1.refs_0_ = bf16[8,32,768]{2,1,0:T(8,128)(2,1)S(1)} async-done(((bf16[8,32,768]{2,1,0:T(8,128)(2,1)}), bf16[8,32,768]{2,1,0:T(8,128)(2,1)S(1)}, u32[]{:S(2)}, u32[]{:S(2)}) %all-to-all-start.1) | async-done | bytes 393248 | tf_op jit(solution)/shard_map/all_to_all | solution.py:88
  21.2 18.0 %all-to-all-start = ((bf16[16,40,1024]{2,1,0:T(8,128)(2,1)}), bf16[16,40,1024]{2,1,0:T(8,128)(2,1)S(1)}, u32[]{:S(2)}, u32[]{:S(2)}) async-start(bf16[16,40,1024]{2,1,0:T(8,128)(2,1)} %bitcast.6), calls=%async_computation | async-start | bytes 2621440 | tf_op jit(solution)/shard_map/all_to_all | solution.py:115
  39.2 2.2 %collective-permute-start = (bf16[8,32,768]{2,1,0:T(8,128)(2,1)S(1)}, bf16[8,32,768]{2,1,0:T(8,128)(2,1)S(1)}, u32[]{:S(2)}, u32[]{:S(2)}) collective-permute-start(bf16[8,32,768]{2,1,0:T(8,128)(2,1)S(1)} %all-to-all-done.1.refs_0_), channel_id=1, source_target_pairs={{0,64},{1,9},{2,66},{3,11},{4,68},{5,13},{6,70},{7,15},{8,72},{9,1... | collective-permute-start | bytes 1179656 | tf_op jit(solution)/shard_map/ppermute | solution.py:96
  41.4 2.0 %collective-permute-start.1 = (bf16[8,32,768]{2,1,0:T(8,128)(2,1)S(1)}, bf16[8,32,768]{2,1,0:T(8,128)(2,1)S(1)}, u32[]{:S(2)}, u32[]{:S(2)}) collective-permute-start(bf16[8,32,768]{2,1,0:T(8,128)(2,1)S(1)} %all-to-all-done.1.refs_0_), channel_id=1, source_target_pairs={{0,128},{1,17},{2,130},{3,19},{4,132},{5,21},{6,134},{7,23},{8,136... | collective-permute-start | bytes 1179656 | tf_op jit(solution)/shard_map/ppermute | solution.py:96
  43.4 6.9 %collective-permute-start.2 = (bf16[8,32,768]{2,1,0:T(8,128)(2,1)S(1)}, bf16[8,32,768]{2,1,0:T(8,128)(2,1)S(1)}, u32[]{:S(2)}, u32[]{:S(2)}) collective-permute-start(bf16[8,32,768]{2,1,0:T(8,128)(2,1)S(1)} %all-to-all-done.1.refs_0_), channel_id=1, source_target_pairs={{0,192},{1,25},{2,194},{3,27},{4,196},{5,29},{6,198},{7,31},{8,200... | collective-permute-start | bytes 1179656 | tf_op jit(solution)/shard_map/ppermute | solution.py:96
  50.4 3.7 %collective-permute-start.3 = (bf16[8,32,768]{2,1,0:T(8,128)(2,1)S(1)}, bf16[8,32,768]{2,1,0:T(8,128)(2,1)S(1)}, u32[]{:S(2)}, u32[]{:S(2)}) collective-permute-start(bf16[8,32,768]{2,1,0:T(8,128)(2,1)S(1)} %all-to-all-done.1.refs_0_), channel_id=1, source_target_pairs={{0,256},{1,33},{2,258},{3,35},{4,260},{5,37},{6,262},{7,39},{8,264... | collective-permute-start | bytes 1179656 | tf_op jit(solution)/shard_map/ppermute | solution.py:96
  54.1 6.4 %collective-permute-start.4 = (bf16[8,32,768]{2,1,0:T(8,128)(2,1)S(1)}, bf16[8,32,768]{2,1,0:T(8,128)(2,1)S(1)}, u32[]{:S(2)}, u32[]{:S(2)}) collective-permute-start(bf16[8,32,768]{2,1,0:T(8,128)(2,1)S(1)} %all-to-all-done.1.refs_0_), channel_id=1, source_target_pairs={{0,320},{1,41},{2,322},{3,43},{4,324},{5,45},{6,326},{7,47},{8,328... | collective-permute-start | bytes 1179656 | tf_op jit(solution)/shard_map/ppermute | solution.py:96
  60.5 1.9 %collective-permute-start.5 = (bf16[8,32,768]{2,1,0:T(8,128)(2,1)S(1)}, bf16[8,32,768]{2,1,0:T(8,128)(2,1)S(1)}, u32[]{:S(2)}, u32[]{:S(2)}) collective-permute-start(bf16[8,32,768]{2,1,0:T(8,128)(2,1)S(1)} %all-to-all-done.1.refs_0_), channel_id=1, source_target_pairs={{0,384},{1,49},{2,386},{3,51},{4,388},{5,53},{6,390},{7,55},{8,392... | collective-permute-start | bytes 1179656 | tf_op jit(solution)/shard_map/ppermute | solution.py:96
  62.4 2.2 %collective-permute-start.6 = (bf16[8,32,768]{2,1,0:T(8,128)(2,1)S(1)}, bf16[8,32,768]{2,1,0:T(8,128)(2,1)S(1)}, u32[]{:S(2)}, u32[]{:S(2)}) collective-permute-start(bf16[8,32,768]{2,1,0:T(8,128)(2,1)S(1)} %all-to-all-done.1.refs_0_), channel_id=1, source_target_pairs={{0,448},{1,57},{2,450},{3,59},{4,452},{5,61},{6,454},{7,63},{8,456... | collective-permute-start | bytes 1179656 | tf_op jit(solution)/shard_map/ppermute | solution.py:96
  64.6 8.8 %collective-permute-done.2.refs_3_ = bf16[8,32,768]{2,1,0:T(8,128)(2,1)S(1)} collective-permute-done((bf16[8,32,768]{2,1,0:T(8,128)(2,1)S(1)}, bf16[8,32,768]{2,1,0:T(8,128)(2,1)S(1)}, u32[]{:S(2)}, u32[]{:S(2)}) %collective-permute-start.2) | collective-permute-done | bytes 393248 | tf_op jit(solution)/shard_map/ppermute | solution.py:96
  73.4 2.7 %collective-permute-done.3.refs_4_ = bf16[8,32,768]{2,1,0:T(8,128)(2,1)S(1)} collective-permute-done((bf16[8,32,768]{2,1,0:T(8,128)(2,1)S(1)}, bf16[8,32,768]{2,1,0:T(8,128)(2,1)S(1)}, u32[]{:S(2)}, u32[]{:S(2)}) %collective-permute-start.3) | collective-permute-done | bytes 393248 | tf_op jit(solution)/shard_map/ppermute | solution.py:96
  76.1 0.7 copy-done
  76.8 9.8 %collective-permute-done.5.refs_6_ = bf16[8,32,768]{2,1,0:T(8,128)(2,1)S(1)} collective-permute-done((bf16[8,32,768]{2,1,0:T(8,128)(2,1)S(1)}, bf16[8,32,768]{2,1,0:T(8,128)(2,1)S(1)}, u32[]{:S(2)}, u32[]{:S(2)}) %collective-permute-start.5) | collective-permute-done | bytes 393248 | tf_op jit(solution)/shard_map/ppermute | solution.py:96
  86.7 0.8 copy-done.2
  87.4 1.9 %collective-permute-done.6.refs_7_ = bf16[8,32,768]{2,1,0:T(8,128)(2,1)S(1)} collective-permute-done((bf16[8,32,768]{2,1,0:T(8,128)(2,1)S(1)}, bf16[8,32,768]{2,1,0:T(8,128)(2,1)S(1)}, u32[]{:S(2)}, u32[]{:S(2)}) %collective-permute-start.6) | collective-permute-done | bytes 393248 | tf_op jit(solution)/shard_map/ppermute | solution.py:96
  89.3 0.8 copy-done.4
  90.1 1.0 copy-done.1
  91.1 1.0 copy-done.3
  92.1 1.0 copy-done.5
  93.1 4.2 %shard_map.68 = bf16[640,384]{1,0:T(8,128)(2,1)} custom-call(bf16[640,1024]{1,0:T(8,128)(2,1)S(1)} %bitcast.35, bf16[8,32,768]{2,1,0:T(8,128)(2,1)S(1)} %all-to-all-done.1.refs_0_, bf16[8,32,768]{2,1,0:T(8,128)(2,1)S(1)} %collective-permute-done.refs_1_, bf16[8,32,768]{2,1,0:T(8,128)(2,1)S(1)} %collective-permute-done.1.refs_2_, ...), custom_call_target="tpu_custom_call" | custom-call | flops 2000000000 | bytes 10000000 | tf_op jit(solution)/shard_map/pallas_call | solution.py:117
  97.3 11.2 %all-to-all-start.2 = ((bf16[16,40,384]{2,1,0:T(8,128)(2,1)}), bf16[16,40,384]{2,1,0:T(8,128)(2,1)S(1)}, u32[]{:S(2)}, u32[]{:S(2)}) async-start(bf16[16,40,384]{2,1,0:T(8,128)(2,1)} %bitcast.9), calls=%async_computation.2 | async-start | bytes 983040 | tf_op jit(solution)/shard_map/all_to_all | solution.py:126
  108.6 16.6 %all-to-all-done.2 = bf16[16,40,384]{2,1,0:T(8,128)(2,1)S(1)} async-done(((bf16[16,40,384]{2,1,0:T(8,128)(2,1)}), bf16[16,40,384]{2,1,0:T(8,128)(2,1)S(1)}, u32[]{:S(2)}, u32[]{:S(2)}) %all-to-all-start.2) | async-done | bytes 491552 | tf_op jit(solution)/shard_map/all_to_all | solution.py:126
  125.2 0.3 fusion.20
  125.5 0.3 fusion.18
  125.8 0.8 fusion.23
  126.7 0.8 pad_maximum_fusion.2
  (26 shorter events, 0.5 us)
Async XLA Ops:
  0.6 10.7 %copy-start.8 = (s32[128,1]{0,1:T(1,128)S(1)}, s32[128,1]{0,1:T(1,128)}, u32[]{:S(2)}) copy-start(s32[128,1]{0,1:T(1,128)} %param.8) | copy-start | bytes 1540
  0.6 10.9 %copy-start.6 = (bf16[128,4096]{1,0:T(8,128)(2,1)S(1)}, bf16[128,4096]{1,0:T(8,128)(2,1)}, u32[]{:S(2)}) copy-start(bf16[128,4096]{1,0:T(8,128)(2,1)} %param.5) | copy-start | bytes 3145732
  2.3 18.8 %all-to-all-start.1 = ((bf16[8,32,768]{2,1,0:T(8,128)(2,1)}), bf16[8,32,768]{2,1,0:T(8,128)(2,1)S(1)}, u32[]{:S(2)}, u32[]{:S(2)}) async-start(bf16[8,32,768]{2,1,0:T(8,128)(2,1)} %broadcast_in_dim.5), calls=%async_computation.1 | async-start | bytes 786432 | tf_op jit(solution)/shard_map/all_to_all | solution.py:88
  21.2 68.9 %all-to-all-start = ((bf16[16,40,1024]{2,1,0:T(8,128)(2,1)}), bf16[16,40,1024]{2,1,0:T(8,128)(2,1)S(1)}, u32[]{:S(2)}, u32[]{:S(2)}) async-start(bf16[16,40,1024]{2,1,0:T(8,128)(2,1)} %bitcast.6), calls=%async_computation | async-start | bytes 2621440 | tf_op jit(solution)/shard_map/all_to_all | solution.py:115
  39.2 21.3 %collective-permute-start = (bf16[8,32,768]{2,1,0:T(8,128)(2,1)S(1)}, bf16[8,32,768]{2,1,0:T(8,128)(2,1)S(1)}, u32[]{:S(2)}, u32[]{:S(2)}) collective-permute-start(bf16[8,32,768]{2,1,0:T(8,128)(2,1)S(1)} %all-to-all-done.1.refs_0_), channel_id=1, source_target_pairs={{0,64},{1,9},{2,66},{3,11},{4,68},{5,13},{6,70},{7,15},{8,72},{9,1... | collective-permute-start | bytes 1179656 | tf_op jit(solution)/shard_map/ppermute | solution.py:96
  41.4 21.1 %collective-permute-start.1 = (bf16[8,32,768]{2,1,0:T(8,128)(2,1)S(1)}, bf16[8,32,768]{2,1,0:T(8,128)(2,1)S(1)}, u32[]{:S(2)}, u32[]{:S(2)}) collective-permute-start(bf16[8,32,768]{2,1,0:T(8,128)(2,1)S(1)} %all-to-all-done.1.refs_0_), channel_id=1, source_target_pairs={{0,128},{1,17},{2,130},{3,19},{4,132},{5,21},{6,134},{7,23},{8,136... | collective-permute-start | bytes 1179656 | tf_op jit(solution)/shard_map/ppermute | solution.py:96
  43.4 30.0 %collective-permute-start.2 = (bf16[8,32,768]{2,1,0:T(8,128)(2,1)S(1)}, bf16[8,32,768]{2,1,0:T(8,128)(2,1)S(1)}, u32[]{:S(2)}, u32[]{:S(2)}) collective-permute-start(bf16[8,32,768]{2,1,0:T(8,128)(2,1)S(1)} %all-to-all-done.1.refs_0_), channel_id=1, source_target_pairs={{0,192},{1,25},{2,194},{3,27},{4,196},{5,29},{6,198},{7,31},{8,200... | collective-permute-start | bytes 1179656 | tf_op jit(solution)/shard_map/ppermute | solution.py:96
  50.4 25.7 %collective-permute-start.3 = (bf16[8,32,768]{2,1,0:T(8,128)(2,1)S(1)}, bf16[8,32,768]{2,1,0:T(8,128)(2,1)S(1)}, u32[]{:S(2)}, u32[]{:S(2)}) collective-permute-start(bf16[8,32,768]{2,1,0:T(8,128)(2,1)S(1)} %all-to-all-done.1.refs_0_), channel_id=1, source_target_pairs={{0,256},{1,33},{2,258},{3,35},{4,260},{5,37},{6,262},{7,39},{8,264... | collective-permute-start | bytes 1179656 | tf_op jit(solution)/shard_map/ppermute | solution.py:96
  54.1 22.0 %collective-permute-start.4 = (bf16[8,32,768]{2,1,0:T(8,128)(2,1)S(1)}, bf16[8,32,768]{2,1,0:T(8,128)(2,1)S(1)}, u32[]{:S(2)}, u32[]{:S(2)}) collective-permute-start(bf16[8,32,768]{2,1,0:T(8,128)(2,1)S(1)} %all-to-all-done.1.refs_0_), channel_id=1, source_target_pairs={{0,320},{1,41},{2,322},{3,43},{4,324},{5,45},{6,326},{7,47},{8,328... | collective-permute-start | bytes 1179656 | tf_op jit(solution)/shard_map/ppermute | solution.py:96
  60.5 26.2 %collective-permute-start.5 = (bf16[8,32,768]{2,1,0:T(8,128)(2,1)S(1)}, bf16[8,32,768]{2,1,0:T(8,128)(2,1)S(1)}, u32[]{:S(2)}, u32[]{:S(2)}) collective-permute-start(bf16[8,32,768]{2,1,0:T(8,128)(2,1)S(1)} %all-to-all-done.1.refs_0_), channel_id=1, source_target_pairs={{0,384},{1,49},{2,386},{3,51},{4,388},{5,53},{6,390},{7,55},{8,392... | collective-permute-start | bytes 1179656 | tf_op jit(solution)/shard_map/ppermute | solution.py:96
  62.4 26.9 %collective-permute-start.6 = (bf16[8,32,768]{2,1,0:T(8,128)(2,1)S(1)}, bf16[8,32,768]{2,1,0:T(8,128)(2,1)S(1)}, u32[]{:S(2)}, u32[]{:S(2)}) collective-permute-start(bf16[8,32,768]{2,1,0:T(8,128)(2,1)S(1)} %all-to-all-done.1.refs_0_), channel_id=1, source_target_pairs={{0,448},{1,57},{2,450},{3,59},{4,452},{5,61},{6,454},{7,63},{8,456... | collective-permute-start | bytes 1179656 | tf_op jit(solution)/shard_map/ppermute | solution.py:96
  76.1 0.7 copy-start
  86.7 0.8 copy-start.2
  89.3 0.8 copy-start.4
  90.1 1.0 copy-start.1
  91.1 1.0 copy-start.3
  92.1 1.0 copy-start.5
  93.1 15.5 %copy-start.9 = (bf16[128,1]{0,1:T(2,128)(2,1)S(1)}, bf16[128,1]{0,1:T(2,128)(2,1)}, u32[]{:S(2)}) copy-start(bf16[128,1]{0,1:T(2,128)(2,1)} %param.7) | copy-start | bytes 772
  97.3 28.5 %copy-start.7 = (bf16[128,1,1536]{2,0,1:T(8,128)(2,1)S(1)}, bf16[128,1,1536]{2,0,1:T(8,128)(2,1)}, u32[]{:S(2)}) copy-start(bf16[128,1,1536]{2,0,1:T(8,128)(2,1)} %param.6) | copy-start | bytes 1179652
  97.3 27.9 %all-to-all-start.2 = ((bf16[16,40,384]{2,1,0:T(8,128)(2,1)}), bf16[16,40,384]{2,1,0:T(8,128)(2,1)S(1)}, u32[]{:S(2)}, u32[]{:S(2)}) async-start(bf16[16,40,384]{2,1,0:T(8,128)(2,1)} %bitcast.9), calls=%async_computation.2 | async-start | bytes 983040 | tf_op jit(solution)/shard_map/all_to_all | solution.py:126

commit v4 on v3

--- a/solution.py
+++ b/solution.py
@@ -43,16 +43,42 @@
     ]
 
 
+HALF_RING = RING // 2
+PIECES = (
+    (0, 0, RING, 0, 0),
+    (1, 0, RING, 3, 0),
+    (2, 0, RING, -3, 0),
+    (3, 0, RING, -1, 0),
+    (3, RING, RING, 2, 0),
+    (3, 2 * RING, HALF_RING, 4, 0),
+    (4, 0, RING, 1, 0),
+    (4, RING, RING, -2, 0),
+    (4, 2 * RING, HALF_RING, 4, HALF_RING),
+)
+ARRAYS = 5
+
+
 def product(got_ref, *refs):
-    parts, out_ref, weight_ref = refs[:RING], refs[RING], refs[RING + 1]
+    parts, out_ref, weight_ref, sems = refs[:ARRAYS], refs[ARRAYS], refs[ARRAYS + 1], refs[ARRAYS + 2]
     y, z, core = lax.axis_index("y"), lax.axis_index("z"), lax.axis_index("core")
-    mine = jnp.where(core == 0, y, z)
-    outer = jnp.where(core == 0, RING, 1)
-    inner = jnp.where(core == 0, 1, RING)
-    for step in range(RING):
-        source = lax.rem(mine + RING - step, RING)
-        for i in range(RING):
-            weight_ref[source * outer + i * inner] = parts[step][i]
+
+    def copies(along_y):
+        out = []
+        for n, (which, first, blocks, offset, at) in enumerate(PIECES):
+            source = lax.rem((y if along_y else z) + offset + RING, RING)
+            dst = weight_ref.at[source, at : at + blocks] if along_y else weight_ref.at[at : at + blocks, source]
+            out.append(pltpu.make_async_copy(parts[which].at[first : first + blocks], dst, sems.at[n]))
+        return out
+
+    @pl.when(core == 0)
+    def _():
+        for copy in copies(True):
+            copy.start()
+
+    @pl.when(core != 0)
+    def _():
+        for copy in copies(False):
+            copy.start()
 
     def order(shape, axis):
         i = lax.broadcasted_iota(jnp.int32, shape, axis)
@@ -65,8 +91,19 @@
     take = (lax.broadcasted_iota(jnp.int32, square, 1) == order((COUNT, 1), 0)).astype(jnp.bfloat16)
     give = (lax.broadcasted_iota(jnp.int32, square, 0) == order((1, COUNT), 1)).astype(jnp.bfloat16)
     rows = jnp.dot(take, got_ref[...], preferred_element_type=jnp.float32).astype(jnp.bfloat16)
-    half = RING * RING // 2
-    width = weight_ref.shape[1] * half
+
+    @pl.when(core == 0)
+    def _():
+        for copy in copies(True):
+            copy.wait()
+
+    @pl.when(core != 0)
+    def _():
+        for copy in copies(False):
+            copy.wait()
+
+    half = RING // 2
+    width = weight_ref.shape[2] * RING * half
     back = jnp.dot(
         rows[: COUNT // 2], weight_ref[:half].reshape(width, FFW), preferred_element_type=jnp.float32
     ) + jnp.dot(
@@ -93,7 +130,11 @@
         axis_index_groups=first_groups(),
         tiled=True,
     )
-    parts = [line] + [lax.ppermute(line, TORUS, second_shift(step)) for step in range(1, RING)]
+    ahead = lax.ppermute(line, TORUS, second_shift(-3))
+    behind = lax.ppermute(line, TORUS, second_shift(3))
+    up = jnp.concatenate([line, ahead, behind[:HALF_RING]], axis=0)
+    down = jnp.concatenate([line, behind, ahead[HALF_RING:]], axis=0)
+    parts = [line, ahead, behind, lax.ppermute(up, TORUS, second_shift(1)), lax.ppermute(down, TORUS, second_shift(-1))]
 
     flat_routes = routes.reshape(tokens)
     member = (flat_routes[:, None] == jnp.arange(EXPERTS, dtype=jnp.int32)[None, :]).astype(jnp.int32)
@@ -117,9 +158,12 @@
     back = pl.pallas_call(
         product,
         out_shape=jax.ShapeDtypeStruct((COUNT, FFW // 2), jnp.bfloat16),
-        in_specs=[pl.BlockSpec(memory_space=pltpu.VMEM)] * (RING + 1),
+        in_specs=[pl.BlockSpec(memory_space=pltpu.VMEM)] + [pl.BlockSpec(memory_space=pl.ANY)] * ARRAYS,
         out_specs=pl.BlockSpec(memory_space=pltpu.VMEM),
-        scratch_shapes=[pltpu.VMEM((RING * RING,) + own.shape, jnp.bfloat16)],
+        scratch_shapes=[
+            pltpu.VMEM((RING, RING) + own.shape, jnp.bfloat16),
+            pltpu.SemaphoreType.DMA((len(PIECES),)),
+        ],
         compiler_params=pltpu.CompilerParams(vmem_limit_bytes=20 * 2**20),
         cost_estimate=pl.CostEstimate(flops=2 * 10**9, bytes_accessed=10**7, transcendentals=0),
     )(got.reshape(COUNT, QUART), *parts)

time: 129 us -> 121 us (0.938)
  starting transfers between devices: 62.7 us -> 55.5 us
  local copies, waits for them, and re-layouts: 7.03 us -> 3.94 us
  waiting for transfers between devices: 47.4 us -> 49.8 us
    ppermute x7 -> x4, starting transfers between devices: 25.4 us -> 14.8 us  [the longest x1 6.25 us: body(): ahead = lax.ppermute(line, TORUS, second_shift(-3))]
    all_to_all x1, starting transfers between devices: 11.2 us -> 14.7 us  [body(): lax.all_to_all(back.reshape(PEERS, 2 * CAP, FFW // 2), SHARE, split_axis=...]
    unnamed x20 -> x12, local copies, waits for them, and re-layouts: 5.29 us -> 2.16 us
    ppermute x7 -> x4, waiting for transfers between devices: 23.2 us -> 25.6 us  [the longest x1 9.97 us: body(): behind = lax.ppermute(line, TORUS, second_shift(3))]
  transfers between devices with their start and end apart: 10 -> 7, of which waited for: 6 -> 6; matrix products, arithmetic and copies ran while one was open for 2% -> 3% of each run, Pallas kernels for 0% -> 0%
where the time goes in v4:
time: 121 us
  starting transfers between devices  55.5 us (46%)
  waiting for transfers between devices  49.8 us (41%)
  Pallas kernels  4.98 us (4%)
  other arithmetic  4.11 us (3%)
  local copies, waits for them, and re-layouts  3.94 us (3%)
  matrix products  1.31 us (1%)
    all_to_all x1, starting transfers between devices, body(): got = lax.all_to_all(sent, SHARE, split_axis=0, concat_axis=0, tiled=True)  18 us
    all_to_all x1, waiting for transfers between devices, body(): lax.all_to_all(back.reshape(PEERS, 2 * CAP, FFW // 2), SHARE, split_axis=...  16.6 us
    all_to_all x1, starting transfers between devices, body(): lax.all_to_all(back.reshape(PEERS, 2 * CAP, FFW // 2), SHARE, split_axis=...  14.7 us
    ppermute x1, waiting for transfers between devices, body(): behind = lax.ppermute(line, TORUS, second_shift(3))  9.97 us
    ppermute x1, waiting for transfers between devices, body(): lax.ppermute(up, TORUS, second_shift(1))  9.54 us
    all_to_all x1, starting transfers between devices, body(): lax.all_to_all(jnp.broadcast_to(own[None], (RING,) + own.shape), TORUS, s...  8.11 us
    all_to_all x1, waiting for transfers between devices, body(): lax.all_to_all(jnp.broadcast_to(own[None], (RING,) + own.shape), TORUS, s...  7.61 us
    ppermute x1, starting transfers between devices, body(): ahead = lax.ppermute(line, TORUS, second_shift(-3))  6.25 us
  transfers between devices with their start and end apart: 7, of which 6 were waited for; matrix products, arithmetic and copies ran while one was open for 3% of the time, Pallas kernels for 0%

profile of v4, /device:TPU:1, one launch (start us, length us, event | category | flops | bytes accessed | tf_op | source)
XLA Modules:
  0.0 120.5 jit_solution(11768344493878283112)
XLA Ops:
  0.6 0.0 copy-start.4
  0.7 1.7 %broadcast_in_dim.5 = bf16[8,32,768]{2,1,0:T(8,128)(2,1)} broadcast(bf16[32,768]{1,0:T(8,128)(2,1)} %bitcast.39), dimensions={1,2} | broadcast | bytes 442368 | tf_op jit(solution)/shard_map/broadcast_in_dim | solution.py:126
  2.3 8.1 %all-to-all-start.1 = ((bf16[8,32,768]{2,1,0:T(8,128)(2,1)}), bf16[8,32,768]{2,1,0:T(8,128)(2,1)S(1)}, u32[]{:S(2)}, u32[]{:S(2)}) async-start(bf16[8,32,768]{2,1,0:T(8,128)(2,1)} %broadcast_in_dim.5), calls=%async_computation.1 | async-start | bytes 786432 | tf_op jit(solution)/shard_map/all_to_all | solution.py:125
  10.4 0.7 fusion.32
  11.2 0.2 reduce_window_sum.11
  11.3 0.2 select_reduce_fusion
  11.6 0.1 fusion.39
  11.6 0.3 fusion
  12.0 0.3 fusion.1
  12.3 1.2 pad_maximum_fusion
  13.5 7.6 %all-to-all-done.1.refs_0_ = bf16[8,32,768]{2,1,0:T(8,128)(2,1)S(1)} async-done(((bf16[8,32,768]{2,1,0:T(8,128)(2,1)}), bf16[8,32,768]{2,1,0:T(8,128)(2,1)S(1)}, u32[]{:S(2)}, u32[]{:S(2)}) %all-to-all-start.1) | async-done | bytes 393248 | tf_op jit(solution)/shard_map/all_to_all | solution.py:125
  21.2 18.0 %all-to-all-start = ((bf16[16,40,1024]{2,1,0:T(8,128)(2,1)}), bf16[16,40,1024]{2,1,0:T(8,128)(2,1)S(1)}, u32[]{:S(2)}, u32[]{:S(2)}) async-start(bf16[16,40,1024]{2,1,0:T(8,128)(2,1)} %bitcast.6), calls=%async_computation | async-start | bytes 2621440 | tf_op jit(solution)/shard_map/all_to_all | solution.py:156
  39.2 2.0 %collective-permute-start.1 = (bf16[8,32,768]{2,1,0:T(8,128)(2,1)S(1)}, bf16[8,32,768]{2,1,0:T(8,128)(2,1)S(1)}, u32[]{:S(2)}, u32[]{:S(2)}) collective-permute-start(bf16[8,32,768]{2,1,0:T(8,128)(2,1)S(1)} %all-to-all-done.1.refs_0_), channel_id=1, source_target_pairs={{0,192},{1,25},{2,194},{3,27},{4,196},{5,29},{6,198},{7,31},{8,200... | collective-permute-start | bytes 1179656 | tf_op jit(solution)/shard_map/ppermute | solution.py:134
  41.2 6.2 %collective-permute-start = (bf16[8,32,768]{2,1,0:T(8,128)(2,1)S(1)}, bf16[8,32,768]{2,1,0:T(8,128)(2,1)S(1)}, u32[]{:S(2)}, u32[]{:S(2)}) collective-permute-start(bf16[8,32,768]{2,1,0:T(8,128)(2,1)S(1)} %all-to-all-done.1.refs_0_), channel_id=1, source_target_pairs={{0,320},{1,41},{2,322},{3,43},{4,324},{5,45},{6,326},{7,47},{8,328... | collective-permute-start | bytes 1179656 | tf_op jit(solution)/shard_map/ppermute | solution.py:133
  47.5 10.0 %collective-permute-done.1.refs_2_ = bf16[8,32,768]{2,1,0:T(8,128)(2,1)S(1)} collective-permute-done((bf16[8,32,768]{2,1,0:T(8,128)(2,1)S(1)}, bf16[8,32,768]{2,1,0:T(8,128)(2,1)S(1)}, u32[]{:S(2)}, u32[]{:S(2)}) %collective-permute-start.1) | collective-permute-done | bytes 393248 | tf_op jit(solution)/shard_map/ppermute | solution.py:134
  57.4 4.6 %collective-permute-done.refs_1_ = bf16[8,32,768]{2,1,0:T(8,128)(2,1)S(1)} collective-permute-done((bf16[8,32,768]{2,1,0:T(8,128)(2,1)S(1)}, bf16[8,32,768]{2,1,0:T(8,128)(2,1)S(1)}, u32[]{:S(2)}, u32[]{:S(2)}) %collective-permute-start) | collective-permute-done | bytes 393248 | tf_op jit(solution)/shard_map/ppermute | solution.py:133
  62.1 0.2 fusion.3
  62.3 1.9 %collective-permute-start.2 = (bf16[20,32,768]{2,1,0:T(8,128)(2,1)S(1)}, bf16[20,32,768]{2,1,0:T(8,128)(2,1)S(1)}, u32[]{:S(2)}, u32[]{:S(2)}) collective-permute-start(bf16[20,32,768]{2,1,0:T(8,128)(2,1)S(1)} %get-tuple-element.12), channel_id=1, source_target_pairs={{0,64},{1,9},{2,66},{3,11},{4,68},{5,13},{6,70},{7,15},{8,72},{9,1... | collective-permute-start | bytes 2949128 | tf_op jit(solution)/shard_map/ppermute | solution.py:137
  64.2 4.6 %collective-permute-start.3 = (bf16[20,32,768]{2,1,0:T(8,128)(2,1)S(1)}, bf16[20,32,768]{2,1,0:T(8,128)(2,1)S(1)}, u32[]{:S(2)}, u32[]{:S(2)}) collective-permute-start(bf16[20,32,768]{2,1,0:T(8,128)(2,1)S(1)} %get-tuple-element.11), channel_id=1, source_target_pairs={{0,448},{1,57},{2,450},{3,59},{4,452},{5,61},{6,454},{7,63},{8,456... | collective-permute-start | bytes 2949128 | tf_op jit(solution)/shard_map/ppermute | solution.py:137
  68.8 9.5 %collective-permute-done.2.refs_3_ = bf16[20,32,768]{2,1,0:T(8,128)(2,1)S(1)} collective-permute-done((bf16[20,32,768]{2,1,0:T(8,128)(2,1)S(1)}, bf16[20,32,768]{2,1,0:T(8,128)(2,1)S(1)}, u32[]{:S(2)}, u32[]{:S(2)}) %collective-permute-start.2) | collective-permute-done | bytes 983072 | tf_op jit(solution)/shard_map/ppermute | solution.py:137
  78.3 1.5 %collective-permute-done.3.refs_4_ = bf16[20,32,768]{2,1,0:T(8,128)(2,1)S(1)} collective-permute-done((bf16[20,32,768]{2,1,0:T(8,128)(2,1)S(1)}, bf16[20,32,768]{2,1,0:T(8,128)(2,1)S(1)}, u32[]{:S(2)}, u32[]{:S(2)}) %collective-permute-start.3) | collective-permute-done | bytes 983072 | tf_op jit(solution)/shard_map/ppermute | solution.py:137
  79.8 0.9 copy-done
  80.7 0.0 all-to-all-done
  80.8 1.2 copy-done.1
  82.0 5.0 %shard_map.68 = bf16[640,384]{1,0:T(8,128)(2,1)} custom-call(bf16[640,1024]{1,0:T(8,128)(2,1)S(1)} %bitcast.35, bf16[8,32,768]{2,1,0:T(8,128)(2,1)S(1)} %all-to-all-done.1.refs_0_, bf16[8,32,768]{2,1,0:T(8,128)(2,1)S(1)} %collective-permute-done.refs_1_, bf16[8,32,768]{2,1,0:T(8,128)(2,1)S(1)} %collective-permute-done.1.refs_2_, ...), custom_call_target="tpu_custom_call" | custom-call | flops 2000000000 | bytes 10000000 | tf_op jit(solution)/shard_map/pallas_call | solution.py:158
  86.9 0.0 copy-start.3
  87.0 14.7 %all-to-all-start.2 = ((bf16[16,40,384]{2,1,0:T(8,128)(2,1)}), bf16[16,40,384]{2,1,0:T(8,128)(2,1)S(1)}, u32[]{:S(2)}, u32[]{:S(2)}) async-start(bf16[16,40,384]{2,1,0:T(8,128)(2,1)} %bitcast.9), calls=%async_computation.2 | async-start | bytes 983040 | tf_op jit(solution)/shard_map/all_to_all | solution.py:170
  101.7 16.6 %all-to-all-done.2 = bf16[16,40,384]{2,1,0:T(8,128)(2,1)S(1)} async-done(((bf16[16,40,384]{2,1,0:T(8,128)(2,1)}), bf16[16,40,384]{2,1,0:T(8,128)(2,1)S(1)}, u32[]{:S(2)}, u32[]{:S(2)}) %all-to-all-start.2) | async-done | bytes 491552 | tf_op jit(solution)/shard_map/all_to_all | solution.py:170
  118.3 0.3 fusion.22
  118.6 0.3 fusion.20
  118.9 0.8 fusion.25
  119.8 0.8 pad_maximum_fusion.4
  (15 shorter events, 0.1 us)
Async XLA Ops:
  0.6 10.7 %copy-start.4 = (s32[128,1]{0,1:T(1,128)S(1)}, s32[128,1]{0,1:T(1,128)}, u32[]{:S(2)}) copy-start(s32[128,1]{0,1:T(1,128)} %param.8) | copy-start | bytes 1540
  0.6 10.9 %copy-start.2 = (bf16[128,4096]{1,0:T(8,128)(2,1)S(1)}, bf16[128,4096]{1,0:T(8,128)(2,1)}, u32[]{:S(2)}) copy-start(bf16[128,4096]{1,0:T(8,128)(2,1)} %param.5) | copy-start | bytes 3145732
  2.3 18.8 %all-to-all-start.1 = ((bf16[8,32,768]{2,1,0:T(8,128)(2,1)}), bf16[8,32,768]{2,1,0:T(8,128)(2,1)S(1)}, u32[]{:S(2)}, u32[]{:S(2)}) async-start(bf16[8,32,768]{2,1,0:T(8,128)(2,1)} %broadcast_in_dim.5), calls=%async_computation.1 | async-start | bytes 786432 | tf_op jit(solution)/shard_map/all_to_all | solution.py:125
  21.2 59.6 %all-to-all-start = ((bf16[16,40,1024]{2,1,0:T(8,128)(2,1)}), bf16[16,40,1024]{2,1,0:T(8,128)(2,1)S(1)}, u32[]{:S(2)}, u32[]{:S(2)}) async-start(bf16[16,40,1024]{2,1,0:T(8,128)(2,1)} %bitcast.6), calls=%async_computation | async-start | bytes 2621440 | tf_op jit(solution)/shard_map/all_to_all | solution.py:156
  39.2 18.3 %collective-permute-start.1 = (bf16[8,32,768]{2,1,0:T(8,128)(2,1)S(1)}, bf16[8,32,768]{2,1,0:T(8,128)(2,1)S(1)}, u32[]{:S(2)}, u32[]{:S(2)}) collective-permute-start(bf16[8,32,768]{2,1,0:T(8,128)(2,1)S(1)} %all-to-all-done.1.refs_0_), channel_id=1, source_target_pairs={{0,192},{1,25},{2,194},{3,27},{4,196},{5,29},{6,198},{7,31},{8,200... | collective-permute-start | bytes 1179656 | tf_op jit(solution)/shard_map/ppermute | solution.py:134
  41.2 20.9 %collective-permute-start = (bf16[8,32,768]{2,1,0:T(8,128)(2,1)S(1)}, bf16[8,32,768]{2,1,0:T(8,128)(2,1)S(1)}, u32[]{:S(2)}, u32[]{:S(2)}) collective-permute-start(bf16[8,32,768]{2,1,0:T(8,128)(2,1)S(1)} %all-to-all-done.1.refs_0_), channel_id=1, source_target_pairs={{0,320},{1,41},{2,322},{3,43},{4,324},{5,45},{6,326},{7,47},{8,328... | collective-permute-start | bytes 1179656 | tf_op jit(solution)/shard_map/ppermute | solution.py:133
  62.3 16.1 %collective-permute-start.2 = (bf16[20,32,768]{2,1,0:T(8,128)(2,1)S(1)}, bf16[20,32,768]{2,1,0:T(8,128)(2,1)S(1)}, u32[]{:S(2)}, u32[]{:S(2)}) collective-permute-start(bf16[20,32,768]{2,1,0:T(8,128)(2,1)S(1)} %get-tuple-element.12), channel_id=1, source_target_pairs={{0,64},{1,9},{2,66},{3,11},{4,68},{5,13},{6,70},{7,15},{8,72},{9,1... | collective-permute-start | bytes 2949128 | tf_op jit(solution)/shard_map/ppermute | solution.py:137
  64.2 15.6 %collective-permute-start.3 = (bf16[20,32,768]{2,1,0:T(8,128)(2,1)S(1)}, bf16[20,32,768]{2,1,0:T(8,128)(2,1)S(1)}, u32[]{:S(2)}, u32[]{:S(2)}) collective-permute-start(bf16[20,32,768]{2,1,0:T(8,128)(2,1)S(1)} %get-tuple-element.11), channel_id=1, source_target_pairs={{0,448},{1,57},{2,450},{3,59},{4,452},{5,61},{6,454},{7,63},{8,456... | collective-permute-start | bytes 2949128 | tf_op jit(solution)/shard_map/ppermute | solution.py:137
  79.8 0.9 copy-start
  80.8 1.2 copy-start.1
  82.0 19.7 %copy-start.5 = (bf16[128,1]{0,1:T(2,128)(2,1)S(1)}, bf16[128,1]{0,1:T(2,128)(2,1)}, u32[]{:S(2)}) copy-start(bf16[128,1]{0,1:T(2,128)(2,1)} %param.7) | copy-start | bytes 772
  86.9 32.0 %copy-start.3 = (bf16[128,1,1536]{2,0,1:T(8,128)(2,1)S(1)}, bf16[128,1,1536]{2,0,1:T(8,128)(2,1)}, u32[]{:S(2)}) copy-start(bf16[128,1,1536]{2,0,1:T(8,128)(2,1)} %param.6) | copy-start | bytes 1179652
  87.0 31.3 %all-to-all-start.2 = ((bf16[16,40,384]{2,1,0:T(8,128)(2,1)}), bf16[16,40,384]{2,1,0:T(8,128)(2,1)S(1)}, u32[]{:S(2)}, u32[]{:S(2)}) async-start(bf16[16,40,384]{2,1,0:T(8,128)(2,1)} %bitcast.9), calls=%async_computation.2 | async-start | bytes 983040 | tf_op jit(solution)/shard_map/all_to_all | solution.py:170

commit v5 on v3

--- a/solution.py
+++ b/solution.py
@@ -18,6 +18,7 @@
 
 TORUS = ("y", "z", "xh", "core")
 RING = 8
+HALF_RING = RING // 2
 LINES = [(h, c) for h in range(4) for c in range(2)]
 COUNT = PEERS * 2 * CAP
 
@@ -28,9 +29,13 @@
 
 def first_groups():
     return [
-        [place_of(k, i, h, c) if c == 0 else place_of(i, k, h, c) for i in range(RING)]
+        [
+            place_of(k + far, i, h, c) if c == 0 else place_of(i, k + far, h, c)
+            for far in (0, HALF_RING)
+            for i in range(RING)
+        ]
         for h, c in LINES
-        for k in range(RING)
+        for k in range(HALF_RING)
     ]
 
 
@@ -43,37 +48,46 @@
     ]
 
 
-def product(got_ref, *refs):
-    parts, out_ref, weight_ref = refs[:RING], refs[RING], refs[RING + 1]
+PIECES = (
+    (0, 0, 0, 0),
+    (0, RING, 0, 1),
+    (1, 0, 1, 0),
+    (1, RING, 1, 1),
+    (2, 0, -1, 0),
+    (2, RING, -1, 1),
+    (3, 0, 2, 0),
+    (4, 0, 2, 1),
+)
+ARRAYS = 5
+
+
+def product(rows_ref, *refs):
+    parts, out_ref, weight_ref = refs[:ARRAYS], refs[ARRAYS], refs[ARRAYS + 1]
     y, z, core = lax.axis_index("y"), lax.axis_index("z"), lax.axis_index("core")
     mine = jnp.where(core == 0, y, z)
     outer = jnp.where(core == 0, RING, 1)
     inner = jnp.where(core == 0, 1, RING)
-    for step in range(RING):
-        source = lax.rem(mine + RING - step, RING)
+    for which, first, offset, far in PIECES:
+        source = lax.rem(mine + offset + RING, HALF_RING) + far * HALF_RING
         for i in range(RING):
-            weight_ref[source * outer + i * inner] = parts[step][i]
+            weight_ref[source * outer + i * inner] = parts[which][first + i]
 
-    def order(shape, axis):
-        i = lax.broadcasted_iota(jnp.int32, shape, axis)
-        piece = (i >= COUNT // 2).astype(jnp.int32)
-        j = i - piece * (COUNT // 2)
-        source = (j * 3277) >> 16
-        return source * (2 * CAP) + piece * CAP + j - source * CAP
-
-    square = (COUNT, COUNT)
-    take = (lax.broadcasted_iota(jnp.int32, square, 1) == order((COUNT, 1), 0)).astype(jnp.bfloat16)
-    give = (lax.broadcasted_iota(jnp.int32, square, 0) == order((1, COUNT), 1)).astype(jnp.bfloat16)
-    rows = jnp.dot(take, got_ref[...], preferred_element_type=jnp.float32).astype(jnp.bfloat16)
     half = RING * RING // 2
     width = weight_ref.shape[1] * half
     back = jnp.dot(
-        rows[: COUNT // 2], weight_ref[:half].reshape(width, FFW), preferred_element_type=jnp.float32
+        rows_ref[: COUNT // 2], weight_ref[:half].reshape(width, FFW), preferred_element_type=jnp.float32
     ) + jnp.dot(
-        rows[COUNT // 2 :], weight_ref[half:].reshape(width, FFW), preferred_element_type=jnp.float32
+        rows_ref[COUNT // 2 :], weight_ref[half:].reshape(width, FFW), preferred_element_type=jnp.float32
     )
     back = back.astype(jnp.bfloat16)
     back = jnp.concatenate([back[:, : FFW // 2], back[:, FFW // 2 :]], axis=0)
+
+    i = lax.broadcasted_iota(jnp.int32, (1, COUNT), 1)
+    piece = (i >= COUNT // 2).astype(jnp.int32)
+    j = i - piece * (COUNT // 2)
+    source = (j * 3277) >> 16
+    order = source * (2 * CAP) + piece * CAP + j - source * CAP
+    give = (lax.broadcasted_iota(jnp.int32, (COUNT, COUNT), 0) == order).astype(jnp.bfloat16)
     out_ref[...] = jnp.dot(give, back, preferred_element_type=jnp.float32).astype(jnp.bfloat16)
 
 
@@ -85,15 +99,21 @@
     tokens = cotangent.shape[0]
 
     own = down_weight[0]
-    line = lax.all_to_all(
-        jnp.broadcast_to(own[None], (RING,) + own.shape),
+    lines = lax.all_to_all(
+        jnp.broadcast_to(own[None], (2 * RING,) + own.shape),
         TORUS,
         split_axis=0,
         concat_axis=0,
         axis_index_groups=first_groups(),
         tiled=True,
     )
-    parts = [line] + [lax.ppermute(line, TORUS, second_shift(step)) for step in range(1, RING)]
+    parts = [
+        lines,
+        lax.ppermute(lines, TORUS, second_shift(-1)),
+        lax.ppermute(lines, TORUS, second_shift(1)),
+        lax.ppermute(lines[:RING], TORUS, second_shift(-2)),
+        lax.ppermute(lines[RING:], TORUS, second_shift(2)),
+    ]
 
     flat_routes = routes.reshape(tokens)
     member = (flat_routes[:, None] == jnp.arange(EXPERTS, dtype=jnp.int32)[None, :]).astype(jnp.int32)
@@ -114,15 +134,19 @@
     ).reshape(PEERS, 2 * CAP, QUART)
     got = lax.all_to_all(sent, SHARE, split_axis=0, concat_axis=0, tiled=True)
 
+    order = jnp.arange(COUNT, dtype=jnp.int32)
+    order = (order % (COUNT // 2)) // CAP * (2 * CAP) + order // (COUNT // 2) * CAP + order % CAP
+    take = (order[:, None] == jnp.arange(COUNT, dtype=jnp.int32)[None, :]).astype(jnp.bfloat16)
+    rows = jnp.dot(take, got.reshape(COUNT, QUART), preferred_element_type=jnp.float32).astype(jnp.bfloat16)
     back = pl.pallas_call(
         product,
         out_shape=jax.ShapeDtypeStruct((COUNT, FFW // 2), jnp.bfloat16),
-        in_specs=[pl.BlockSpec(memory_space=pltpu.VMEM)] * (RING + 1),
+        in_specs=[pl.BlockSpec(memory_space=pltpu.VMEM)] * (ARRAYS + 1),
         out_specs=pl.BlockSpec(memory_space=pltpu.VMEM),
         scratch_shapes=[pltpu.VMEM((RING * RING,) + own.shape, jnp.bfloat16)],
         compiler_params=pltpu.CompilerParams(vmem_limit_bytes=20 * 2**20),
         cost_estimate=pl.CostEstimate(flops=2 * 10**9, bytes_accessed=10**7, transcendentals=0),
-    )(got.reshape(COUNT, QUART), *parts)
+    )(rows, *parts)
     came = lax.all_to_all(
         back.reshape(PEERS, 2 * CAP, FFW // 2), SHARE, split_axis=0, concat_axis=0, tiled=True
     ).reshape(COUNT, FFW // 2)

time: 129 us -> 122 us (0.946)
  starting transfers between devices: 62.7 us -> 54 us
  waiting for transfers between devices: 47.4 us -> 53.5 us
  local copies, waits for them, and re-layouts: 7.03 us -> 2.76 us
  matrix products: 1.31 us -> 3.85 us
    ppermute x7 -> x4, waiting for transfers between devices: 23.2 us -> 0.01 us  [the longest x1 0.01 us: body(): lax.ppermute(lines[:RING], TORUS, second_shift(-2))]
    all_to_all x1, waiting for transfers between devices: 0.01 us -> 19.5 us  [body(): got = lax.all_to_all(sent, SHARE, split_axis=0, concat_axis=0, tiled=True)]
    ppermute x7 -> x4, starting transfers between devices: 25.4 us -> 11.4 us  [the longest x1 3.9 us: body(): lax.ppermute(lines[:RING], TORUS, second_shift(-2))]
    all_to_all x1, starting transfers between devices: 8.11 us -> 20.3 us  [body(): lax.all_to_all(jnp.broadcast_to(own[None], (2 * RING,) + own.shape), TORU...]
    all_to_all x1, waiting for transfers between devices: 7.6 us -> 17.4 us  [body(): lax.all_to_all(jnp.broadcast_to(own[None], (2 * RING,) + own.shape), TORU...]
    all_to_all x1, starting transfers between devices: 11.2 us -> 5.59 us  [body(): lax.all_to_all(back.reshape(PEERS, 2 * CAP, FFW // 2), SHARE, split_axis=...]
    unnamed x20 -> x8, local copies, waits for them, and re-layouts: 5.29 us -> 0.02 us
    dot_general x0 -> x1, matrix products: none -> 2.54 us  [body(): jnp.dot(take, got.reshape(COUNT, QUART), preferred_element_type=jnp.float32)]
  transfers between devices with their start and end apart: 10 -> 7, of which waited for: 6 -> 3; matrix products, arithmetic and copies ran while one was open for 2% -> 5% of each run, Pallas kernels for 0% -> 0%
where the time goes in v5:
time: 122 us
  starting transfers between devices  54 us (44%)
  waiting for transfers between devices  53.5 us (44%)
  matrix products  3.85 us (3%)
  Pallas kernels  3.35 us (3%)
  other arithmetic  3.3 us (3%)
  local copies, waits for them, and re-layouts  2.76 us (2%)
    all_to_all x1, starting transfers between devices, body(): lax.all_to_all(jnp.broadcast_to(own[None], (2 * RING,) + own.shape), TORU...  20.3 us
    all_to_all x1, waiting for transfers between devices, body(): got = lax.all_to_all(sent, SHARE, split_axis=0, concat_axis=0, tiled=True)  19.5 us
    all_to_all x1, waiting for transfers between devices, body(): lax.all_to_all(jnp.broadcast_to(own[None], (2 * RING,) + own.shape), TORU...  17.4 us
    all_to_all x1, starting transfers between devices, body(): got = lax.all_to_all(sent, SHARE, split_axis=0, concat_axis=0, tiled=True)  16.7 us
    all_to_all x1, waiting for transfers between devices, body(): lax.all_to_all(back.reshape(PEERS, 2 * CAP, FFW // 2), SHARE, split_axis=...  16.6 us
    all_to_all x1, starting transfers between devices, body(): lax.all_to_all(back.reshape(PEERS, 2 * CAP, FFW // 2), SHARE, split_axis=...  5.59 us
    ppermute x1, starting transfers between devices, body(): lax.ppermute(lines[:RING], TORUS, second_shift(-2))  3.9 us
    pallas_call x1, Pallas kernels, body(): pl.pallas_call(product, out_shape=jax.ShapeDtypeStruct((COUNT, FFW // 2),...  3.35 us
  transfers between devices with their start and end apart: 7, of which 3 were waited for; matrix products, arithmetic and copies ran while one was open for 5% of the time, Pallas kernels for 0%

profile of v5, /device:TPU:1, one launch (start us, length us, event | category | flops | bytes accessed | tf_op | source)
XLA Modules:
  0.0 121.6 jit_solution(16150114038358366809)
XLA Ops:
  0.6 0.0 copy-start.2
  0.6 0.0 copy-start
  0.6 1.9 %broadcast_in_dim.5 = bf16[16,32,768]{2,1,0:T(8,128)(2,1)} broadcast(bf16[32,768]{1,0:T(8,128)(2,1)} %bitcast.39), dimensions={1,2} | broadcast | bytes 835584 | tf_op jit(solution)/shard_map/broadcast_in_dim | solution.py:103
  2.5 20.3 %all-to-all-start.1 = ((bf16[16,32,768]{2,1,0:T(8,128)(2,1)}), bf16[16,32,768]{2,1,0:T(8,128)(2,1)S(1)}, u32[]{:S(2)}, u32[]{:S(2)}) async-start(bf16[16,32,768]{2,1,0:T(8,128)(2,1)} %broadcast_in_dim.5), calls=%async_computation.1 | async-start | bytes 1572864 | tf_op jit(solution)/shard_map/all_to_all | solution.py:102
  22.8 0.1 fusion.33
  22.9 0.2 reduce_window_sum.11
  23.1 0.2 select_reduce_fusion
  23.3 0.1 fusion.52
  23.4 0.3 fusion.2
  23.7 0.3 fusion.3
  24.1 1.2 pad_maximum_fusion
  25.3 17.4 %all-to-all-done.1.refs_0_ = bf16[16,32,768]{2,1,0:T(8,128)(2,1)S(1)} async-done(((bf16[16,32,768]{2,1,0:T(8,128)(2,1)}), bf16[16,32,768]{2,1,0:T(8,128)(2,1)S(1)}, u32[]{:S(2)}, u32[]{:S(2)}) %all-to-all-start.1) | async-done | bytes 786464 | tf_op jit(solution)/shard_map/all_to_all | solution.py:102
  42.7 16.7 %all-to-all-start = ((bf16[16,40,1024]{2,1,0:T(8,128)(2,1)}), bf16[16,40,1024]{2,1,0:T(8,128)(2,1)}, u32[]{:S(2)}, u32[]{:S(2)}) async-start(bf16[16,40,1024]{2,1,0:T(8,128)(2,1)} %bitcast.6), calls=%async_computation | async-start | bytes 2621440 | tf_op jit(solution)/shard_map/all_to_all | solution.py:135
  59.4 2.1 %collective-permute-start = (bf16[16,32,768]{2,1,0:T(8,128)(2,1)S(1)}, bf16[16,32,768]{2,1,0:T(8,128)(2,1)S(1)}, u32[]{:S(2)}, u32[]{:S(2)}) collective-permute-start(bf16[16,32,768]{2,1,0:T(8,128)(2,1)S(1)} %all-to-all-done.1.refs_0_), channel_id=1, source_target_pairs={{0,448},{1,57},{2,450},{3,59},{4,452},{5,61},{6,454},{7,63},{8,456... | collective-permute-start | bytes 2359304 | tf_op jit(solution)/shard_map/ppermute | solution.py:112
  61.5 3.2 %collective-permute-start.1 = (bf16[16,32,768]{2,1,0:T(8,128)(2,1)S(1)}, bf16[16,32,768]{2,1,0:T(8,128)(2,1)S(1)}, u32[]{:S(2)}, u32[]{:S(2)}) collective-permute-start(bf16[16,32,768]{2,1,0:T(8,128)(2,1)S(1)} %all-to-all-done.1.refs_0_), channel_id=1, source_target_pairs={{0,64},{1,9},{2,66},{3,11},{4,68},{5,13},{6,70},{7,15},{8,72},{9,1... | collective-permute-start | bytes 2359304 | tf_op jit(solution)/shard_map/ppermute | solution.py:113
  64.7 0.8 fusion.53
  65.5 3.9 %collective-permute-start.2 = (bf16[8,32,768]{2,1,0:T(8,128)(2,1)}, bf16[8,32,768]{2,1,0:T(8,128)(2,1)S(1)}, u32[]{:S(2)}, u32[]{:S(2)}) collective-permute-start(bf16[8,32,768]{2,1,0:T(8,128)(2,1)} %get-tuple-element.12), channel_id=1, source_target_pairs={{0,384},{1,49},{2,386},{3,51},{4,388},{5,53},{6,390},{7,55},{8,392... | collective-permute-start | bytes 1179656 | tf_op jit(solution)/shard_map/ppermute | solution.py:114
  69.4 2.3 %collective-permute-start.3 = (bf16[8,32,768]{2,1,0:T(8,128)(2,1)S(1)}, bf16[8,32,768]{2,1,0:T(8,128)(2,1)S(1)}, u32[]{:S(2)}, u32[]{:S(2)}) collective-permute-start(bf16[8,32,768]{2,1,0:T(8,128)(2,1)S(1)} %get-tuple-element.11), channel_id=1, source_target_pairs={{0,128},{1,17},{2,130},{3,19},{4,132},{5,21},{6,134},{7,23},{8,136... | collective-permute-start | bytes 1179656 | tf_op jit(solution)/shard_map/ppermute | solution.py:115
  71.7 19.5 %all-to-all-done = bf16[16,40,1024]{2,1,0:T(8,128)(2,1)} async-done(((bf16[16,40,1024]{2,1,0:T(8,128)(2,1)}), bf16[16,40,1024]{2,1,0:T(8,128)(2,1)}, u32[]{:S(2)}, u32[]{:S(2)}) %all-to-all-start) | async-done | bytes 1310752 | tf_op jit(solution)/shard_map/all_to_all | solution.py:135
  91.2 2.5 %fusion.1.rows_ref = bf16[640,1024]{1,0:T(8,128)(2,1)S(1)} fusion(bf16[640,1024]{1,0:T(8,128)(2,1)} %bitcast.7, s32[640]{0:T(1024)S(1)} %fusion.40), kind=kOutput, calls=%fused_computation.2 | convolution fusion | flops 839925760 | bytes 2624000 | tf_op jit(solution)/shard_map/dot_general | solution.py:140
  93.7 0.0 copy-start.3
  93.7 0.0 collective-permute-done.2.refs_3_
  93.7 0.0 collective-permute-done.3.refs_4_
  93.7 0.0 collective-permute-done.refs_1_
  93.8 0.0 collective-permute-done.1.refs_2_
  93.8 3.3 %shard_map.68 = bf16[640,384]{1,0:T(8,128)(2,1)} custom-call(bf16[640,1024]{1,0:T(8,128)(2,1)S(1)} %fusion.1.rows_ref, bf16[16,32,768]{2,1,0:T(8,128)(2,1)S(1)} %all-to-all-done.1.refs_0_, bf16[16,32,768]{2,1,0:T(8,128)(2,1)S(1)} %collective-permute-done.refs_1_, bf16[16,32,768]{2,1,0:T(8,128)(2,1)S(1)} %collective-permute-done.1.refs_2_, ...), custom_call_target="tpu_custom_call" | custom-call | flops 2000000000 | bytes 10000000 | tf_op jit(solution)/shard_map/pallas_call | solution.py:141
  97.1 5.6 %all-to-all-start.2 = ((bf16[16,40,384]{2,1,0:T(8,128)(2,1)}), bf16[16,40,384]{2,1,0:T(8,128)(2,1)S(1)}, u32[]{:S(2)}, u32[]{:S(2)}) async-start(bf16[16,40,384]{2,1,0:T(8,128)(2,1)} %bitcast.9), calls=%async_computation.2 | async-start | bytes 983040 | tf_op jit(solution)/shard_map/all_to_all | solution.py:150
  102.7 16.6 %all-to-all-done.2 = bf16[16,40,384]{2,1,0:T(8,128)(2,1)S(1)} async-done(((bf16[16,40,384]{2,1,0:T(8,128)(2,1)}), bf16[16,40,384]{2,1,0:T(8,128)(2,1)S(1)}, u32[]{:S(2)}, u32[]{:S(2)}) %all-to-all-start.2) | async-done | bytes 491552 | tf_op jit(solution)/shard_map/all_to_all | solution.py:150
  119.3 0.3 fusion.23
  119.7 0.3 fusion.21
  120.0 0.8 fusion.26
  120.8 0.8 pad_maximum_fusion.2
  (11 shorter events, 0.1 us)
Async XLA Ops:
  0.6 22.2 %copy-start.2 = (s32[128,1]{0,1:T(1,128)S(1)}, s32[128,1]{0,1:T(1,128)}, u32[]{:S(2)}) copy-start(s32[128,1]{0,1:T(1,128)} %param.8) | copy-start | bytes 1540
  0.6 22.6 %copy-start = (bf16[128,4096]{1,0:T(8,128)(2,1)S(1)}, bf16[128,4096]{1,0:T(8,128)(2,1)}, u32[]{:S(2)}) copy-start(bf16[128,4096]{1,0:T(8,128)(2,1)} %param.5) | copy-start | bytes 3145732
  2.5 40.2 %all-to-all-start.1 = ((bf16[16,32,768]{2,1,0:T(8,128)(2,1)}), bf16[16,32,768]{2,1,0:T(8,128)(2,1)S(1)}, u32[]{:S(2)}, u32[]{:S(2)}) async-start(bf16[16,32,768]{2,1,0:T(8,128)(2,1)} %broadcast_in_dim.5), calls=%async_computation.1 | async-start | bytes 1572864 | tf_op jit(solution)/shard_map/all_to_all | solution.py:102
  42.7 48.5 %all-to-all-start = ((bf16[16,40,1024]{2,1,0:T(8,128)(2,1)}), bf16[16,40,1024]{2,1,0:T(8,128)(2,1)}, u32[]{:S(2)}, u32[]{:S(2)}) async-start(bf16[16,40,1024]{2,1,0:T(8,128)(2,1)} %bitcast.6), calls=%async_computation | async-start | bytes 2621440 | tf_op jit(solution)/shard_map/all_to_all | solution.py:135
  59.4 34.4 %collective-permute-start = (bf16[16,32,768]{2,1,0:T(8,128)(2,1)S(1)}, bf16[16,32,768]{2,1,0:T(8,128)(2,1)S(1)}, u32[]{:S(2)}, u32[]{:S(2)}) collective-permute-start(bf16[16,32,768]{2,1,0:T(8,128)(2,1)S(1)} %all-to-all-done.1.refs_0_), channel_id=1, source_target_pairs={{0,448},{1,57},{2,450},{3,59},{4,452},{5,61},{6,454},{7,63},{8,456... | collective-permute-start | bytes 2359304 | tf_op jit(solution)/shard_map/ppermute | solution.py:112
  61.5 32.3 %collective-permute-start.1 = (bf16[16,32,768]{2,1,0:T(8,128)(2,1)S(1)}, bf16[16,32,768]{2,1,0:T(8,128)(2,1)S(1)}, u32[]{:S(2)}, u32[]{:S(2)}) collective-permute-start(bf16[16,32,768]{2,1,0:T(8,128)(2,1)S(1)} %all-to-all-done.1.refs_0_), channel_id=1, source_target_pairs={{0,64},{1,9},{2,66},{3,11},{4,68},{5,13},{6,70},{7,15},{8,72},{9,1... | collective-permute-start | bytes 2359304 | tf_op jit(solution)/shard_map/ppermute | solution.py:113
  65.5 28.2 %collective-permute-start.2 = (bf16[8,32,768]{2,1,0:T(8,128)(2,1)}, bf16[8,32,768]{2,1,0:T(8,128)(2,1)S(1)}, u32[]{:S(2)}, u32[]{:S(2)}) collective-permute-start(bf16[8,32,768]{2,1,0:T(8,128)(2,1)} %get-tuple-element.12), channel_id=1, source_target_pairs={{0,384},{1,49},{2,386},{3,51},{4,388},{5,53},{6,390},{7,55},{8,392... | collective-permute-start | bytes 1179656 | tf_op jit(solution)/shard_map/ppermute | solution.py:114
  69.4 24.3 %collective-permute-start.3 = (bf16[8,32,768]{2,1,0:T(8,128)(2,1)S(1)}, bf16[8,32,768]{2,1,0:T(8,128)(2,1)S(1)}, u32[]{:S(2)}, u32[]{:S(2)}) collective-permute-start(bf16[8,32,768]{2,1,0:T(8,128)(2,1)S(1)} %get-tuple-element.11), channel_id=1, source_target_pairs={{0,128},{1,17},{2,130},{3,19},{4,132},{5,21},{6,134},{7,23},{8,136... | collective-permute-start | bytes 1179656 | tf_op jit(solution)/shard_map/ppermute | solution.py:115
  93.7 9.0 %copy-start.3 = (bf16[128,1]{0,1:T(2,128)(2,1)S(1)}, bf16[128,1]{0,1:T(2,128)(2,1)}, u32[]{:S(2)}) copy-start(bf16[128,1]{0,1:T(2,128)(2,1)} %param.7) | copy-start | bytes 772
  97.1 22.9 %copy-start.1 = (bf16[128,1,1536]{2,0,1:T(8,128)(2,1)S(1)}, bf16[128,1,1536]{2,0,1:T(8,128)(2,1)}, u32[]{:S(2)}) copy-start(bf16[128,1,1536]{2,0,1:T(8,128)(2,1)} %param.6) | copy-start | bytes 1179652
  97.1 22.2 %all-to-all-start.2 = ((bf16[16,40,384]{2,1,0:T(8,128)(2,1)}), bf16[16,40,384]{2,1,0:T(8,128)(2,1)S(1)}, u32[]{:S(2)}, u32[]{:S(2)}) async-start(bf16[16,40,384]{2,1,0:T(8,128)(2,1)} %bitcast.9), calls=%async_computation.2 | async-start | bytes 983040 | tf_op jit(solution)/shard_map/all_to_all | solution.py:150

commit v6 on v5

--- a/solution.py
+++ b/solution.py
@@ -29,13 +29,9 @@
 
 def first_groups():
     return [
-        [
-            place_of(k + far, i, h, c) if c == 0 else place_of(i, k + far, h, c)
-            for far in (0, HALF_RING)
-            for i in range(RING)
-        ]
+        [place_of(k, i, h, c) if c == 0 else place_of(i, k, h, c) for i in range(RING)]
         for h, c in LINES
-        for k in range(HALF_RING)
+        for k in range(RING)
     ]
 
 
@@ -49,14 +45,15 @@
 
 
 PIECES = (
-    (0, 0, 0, 0),
-    (0, RING, 0, 1),
-    (1, 0, 1, 0),
-    (1, RING, 1, 1),
-    (2, 0, -1, 0),
-    (2, RING, -1, 1),
-    (3, 0, 2, 0),
-    (4, 0, 2, 1),
+    (0, 0, RING, 0, 0),
+    (1, 0, RING, 3, 0),
+    (2, 0, RING, -3, 0),
+    (3, 0, RING, -1, 0),
+    (3, RING, RING, 2, 0),
+    (3, 2 * RING, HALF_RING, 4, 0),
+    (4, 0, RING, 1, 0),
+    (4, RING, RING, -2, 0),
+    (4, 2 * RING, HALF_RING, 4, HALF_RING),
 )
 ARRAYS = 5
 
@@ -67,10 +64,10 @@
     mine = jnp.where(core == 0, y, z)
     outer = jnp.where(core == 0, RING, 1)
     inner = jnp.where(core == 0, 1, RING)
-    for which, first, offset, far in PIECES:
-        source = lax.rem(mine + offset + RING, HALF_RING) + far * HALF_RING
-        for i in range(RING):
-            weight_ref[source * outer + i * inner] = parts[which][first + i]
+    for which, first, blocks, offset, at in PIECES:
+        source = lax.rem(mine + offset + RING, RING)
+        for i in range(blocks):
+            weight_ref[source * outer + (at + i) * inner] = parts[which][first + i]
 
     half = RING * RING // 2
     width = weight_ref.shape[1] * half
@@ -99,21 +96,19 @@
     tokens = cotangent.shape[0]
 
     own = down_weight[0]
-    lines = lax.all_to_all(
-        jnp.broadcast_to(own[None], (2 * RING,) + own.shape),
+    line = lax.all_to_all(
+        jnp.broadcast_to(own[None], (RING,) + own.shape),
         TORUS,
         split_axis=0,
         concat_axis=0,
         axis_index_groups=first_groups(),
         tiled=True,
     )
-    parts = [
-        lines,
-        lax.ppermute(lines, TORUS, second_shift(-1)),
-        lax.ppermute(lines, TORUS, second_shift(1)),
-        lax.ppermute(lines[:RING], TORUS, second_shift(-2)),
-        lax.ppermute(lines[RING:], TORUS, second_shift(2)),
-    ]
+    ahead = lax.ppermute(line, TORUS, second_shift(-3))
+    behind = lax.ppermute(line, TORUS, second_shift(3))
+    up = jnp.concatenate([line, ahead, behind[:HALF_RING]], axis=0)
+    down = jnp.concatenate([line, behind, ahead[HALF_RING:]], axis=0)
+    parts = [line, ahead, behind, lax.ppermute(up, TORUS, second_shift(1)), lax.ppermute(down, TORUS, second_shift(-1))]
 
     flat_routes = routes.reshape(tokens)
     member = (flat_routes[:, None] == jnp.arange(EXPERTS, dtype=jnp.int32)[None, :]).astype(jnp.int32)

time: 122 us -> 117 us (0.959)
  waiting for transfers between devices: 53.5 us -> 47.7 us
  other arithmetic: 3.3 us -> 5.41 us
    ppermute x4, waiting for transfers between devices: 0.01 us -> 22.6 us  [the longest x1 9.97 us: body(): behind = lax.ppermute(line, TORUS, second_shift(3))]
    all_to_all x1, waiting for transfers between devices: 19.5 us -> 0.84 us  [body(): got = lax.all_to_all(sent, SHARE, split_axis=0, concat_axis=0, tiled=True)]
    all_to_all x1, starting transfers between devices: 20.3 us -> 8.11 us  [body(): lax.all_to_all(jnp.broadcast_to(own[None], (RING,) + own.shape), TORUS, s...]
    all_to_all x1, waiting for transfers between devices: 17.4 us -> 7.62 us  [body(): lax.all_to_all(jnp.broadcast_to(own[None], (RING,) + own.shape), TORUS, s...]
    all_to_all x1, starting transfers between devices: 5.59 us -> 13 us  [body(): lax.all_to_all(back.reshape(PEERS, 2 * CAP, FFW // 2), SHARE, split_axis=...]
    ppermute x4, starting transfers between devices: 11.4 us -> 14.8 us  [the longest x1 6.25 us: body(): ahead = lax.ppermute(line, TORUS, second_shift(-3))]
    concatenate x0 -> x1, other arithmetic: none -> 1.48 us  [body(): down = jnp.concatenate([line, behind, ahead[HALF_RING:]], axis=0)]
    all_to_all x1, starting transfers between devices: 16.7 us -> 18 us  [body(): got = lax.all_to_all(sent, SHARE, split_axis=0, concat_axis=0, tiled=True)]
  transfers between devices with their start and end apart: 7 -> 7, of which waited for: 3 -> 7; matrix products, arithmetic and copies ran while one was open for 5% -> 6% of each run, Pallas kernels for 0% -> 0%
where the time goes in v6:
time: 117 us
  starting transfers between devices  53.9 us (46%)
  waiting for transfers between devices  47.7 us (41%)
  other arithmetic  5.41 us (5%)
  matrix products  3.85 us (3%)
  Pallas kernels  3.34 us (3%)
  local copies, waits for them, and re-layouts  1.8 us (2%)
    all_to_all x1, starting transfers between devices, body(): got = lax.all_to_all(sent, SHARE, split_axis=0, concat_axis=0, tiled=True)  18 us
    all_to_all x1, waiting for transfers between devices, body(): lax.all_to_all(back.reshape(PEERS, 2 * CAP, FFW // 2), SHARE, split_axis=...  16.6 us
    all_to_all x1, starting transfers between devices, body(): lax.all_to_all(back.reshape(PEERS, 2 * CAP, FFW // 2), SHARE, split_axis=...  13 us
    ppermute x1, waiting for transfers between devices, body(): behind = lax.ppermute(line, TORUS, second_shift(3))  9.97 us
    all_to_all x1, starting transfers between devices, body(): lax.all_to_all(jnp.broadcast_to(own[None], (RING,) + own.shape), TORUS, s...  8.11 us
    all_to_all x1, waiting for transfers between devices, body(): lax.all_to_all(jnp.broadcast_to(own[None], (RING,) + own.shape), TORUS, s...  7.62 us
    ppermute x1, waiting for transfers between devices, body(): lax.ppermute(up, TORUS, second_shift(1))  6.33 us
    ppermute x1, starting transfers between devices, body(): ahead = lax.ppermute(line, TORUS, second_shift(-3))  6.25 us
  transfers between devices with their start and end apart: 7, of which 7 were waited for; matrix products, arithmetic and copies ran while one was open for 6% of the time, Pallas kernels for 0%

profile of v6, /device:TPU:1, one launch (start us, length us, event | category | flops | bytes accessed | tf_op | source)
XLA Modules:
  0.0 116.8 jit_solution(712044020598129323)
XLA Ops:
  0.6 0.0 copy-start.2
  0.7 1.7 %broadcast_in_dim.5 = bf16[8,32,768]{2,1,0:T(8,128)(2,1)} broadcast(bf16[32,768]{1,0:T(8,128)(2,1)} %bitcast.39), dimensions={1,2} | broadcast | bytes 442368 | tf_op jit(solution)/shard_map/broadcast_in_dim | solution.py:100
  2.3 8.1 %all-to-all-start.1 = ((bf16[8,32,768]{2,1,0:T(8,128)(2,1)}), bf16[8,32,768]{2,1,0:T(8,128)(2,1)S(1)}, u32[]{:S(2)}, u32[]{:S(2)}) async-start(bf16[8,32,768]{2,1,0:T(8,128)(2,1)} %broadcast_in_dim.5), calls=%async_computation.1 | async-start | bytes 786432 | tf_op jit(solution)/shard_map/all_to_all | solution.py:99
  10.4 0.7 fusion.35
  11.2 0.2 reduce_window_sum.11
  11.3 0.2 select_reduce_fusion
  11.5 0.0 copy-done
  11.6 0.1 fusion.54
  11.6 0.3 fusion.2
  12.0 0.3 fusion.3
  12.3 1.2 %pad_maximum_fusion = bf16[2,320,1024]{2,1,0:T(8,128)(2,1)} fusion(bf16[1,320,1024]{2,1,0:T(8,128)(2,1)S(1)} %fusion.3, bf16[1,320,1024]{2,1,0:T(8,128)(2,1)S(1)} %fusion.2), kind=kLoop, calls=%fused_computation.5 | loop fusion | flops 655360 | bytes 2621440 | tf_op jit(solution)/shard_map/stack | solution.py:120
  13.5 7.6 %all-to-all-done.1.refs_0_ = bf16[8,32,768]{2,1,0:T(8,128)(2,1)S(1)} async-done(((bf16[8,32,768]{2,1,0:T(8,128)(2,1)}), bf16[8,32,768]{2,1,0:T(8,128)(2,1)S(1)}, u32[]{:S(2)}, u32[]{:S(2)}) %all-to-all-start.1) | async-done | bytes 393248 | tf_op jit(solution)/shard_map/all_to_all | solution.py:99
  21.2 18.0 %all-to-all-start = ((bf16[16,40,1024]{2,1,0:T(8,128)(2,1)}), bf16[16,40,1024]{2,1,0:T(8,128)(2,1)}, u32[]{:S(2)}, u32[]{:S(2)}) async-start(bf16[16,40,1024]{2,1,0:T(8,128)(2,1)} %bitcast.6), calls=%async_computation | async-start | bytes 2621440 | tf_op jit(solution)/shard_map/all_to_all | solution.py:130
  39.2 2.0 %collective-permute-start.1 = (bf16[8,32,768]{2,1,0:T(8,128)(2,1)S(1)}, bf16[8,32,768]{2,1,0:T(8,128)(2,1)S(1)}, u32[]{:S(2)}, u32[]{:S(2)}) collective-permute-start(bf16[8,32,768]{2,1,0:T(8,128)(2,1)S(1)} %all-to-all-done.1.refs_0_), channel_id=1, source_target_pairs={{0,192},{1,25},{2,194},{3,27},{4,196},{5,29},{6,198},{7,31},{8,200... | collective-permute-start | bytes 1179656 | tf_op jit(solution)/shard_map/ppermute | solution.py:108
  41.2 6.2 %collective-permute-start = (bf16[8,32,768]{2,1,0:T(8,128)(2,1)S(1)}, bf16[8,32,768]{2,1,0:T(8,128)(2,1)S(1)}, u32[]{:S(2)}, u32[]{:S(2)}) collective-permute-start(bf16[8,32,768]{2,1,0:T(8,128)(2,1)S(1)} %all-to-all-done.1.refs_0_), channel_id=1, source_target_pairs={{0,320},{1,41},{2,322},{3,43},{4,324},{5,45},{6,326},{7,47},{8,328... | collective-permute-start | bytes 1179656 | tf_op jit(solution)/shard_map/ppermute | solution.py:107
  47.5 10.0 %collective-permute-done.1.refs_2_ = bf16[8,32,768]{2,1,0:T(8,128)(2,1)S(1)} collective-permute-done((bf16[8,32,768]{2,1,0:T(8,128)(2,1)S(1)}, bf16[8,32,768]{2,1,0:T(8,128)(2,1)S(1)}, u32[]{:S(2)}, u32[]{:S(2)}) %collective-permute-start.1) | collective-permute-done | bytes 393248 | tf_op jit(solution)/shard_map/ppermute | solution.py:108
  57.4 4.7 %collective-permute-done.refs_1_ = bf16[8,32,768]{2,1,0:T(8,128)(2,1)S(1)} collective-permute-done((bf16[8,32,768]{2,1,0:T(8,128)(2,1)S(1)}, bf16[8,32,768]{2,1,0:T(8,128)(2,1)S(1)}, u32[]{:S(2)}, u32[]{:S(2)}) %collective-permute-start) | collective-permute-done | bytes 393248 | tf_op jit(solution)/shard_map/ppermute | solution.py:107
  62.2 1.5 %fusion.5 = (bf16[20,32,768]{2,1,0:T(8,128)(2,1)}, bf16[20,32,768]{2,1,0:T(8,128)(2,1)}) fusion(bf16[8,32,768]{2,1,0:T(8,128)(2,1)S(1)} %all-to-all-done.1.refs_0_, bf16[4,32,768]{2,1,0:T(8,128)(2,1)S(1)} %slice.33, bf16[8,32,768]{2,1,0:T(8,128)(2,1)S(1)} %collective-permute-done.1.refs_2_, bf16[4,32,768]{2,1,0:T(8,128)(2,1)S(1)} %slice.32, ...), kind=kLoop, calls=%fused_computation.11 | loop fusion | flops 1966080 | bytes 3538944 | tf_op jit(solution)/shard_map/concatenate | solution.py:110
  63.7 1.9 %collective-permute-start.2 = (bf16[20,32,768]{2,1,0:T(8,128)(2,1)}, bf16[20,32,768]{2,1,0:T(8,128)(2,1)S(1)}, u32[]{:S(2)}, u32[]{:S(2)}) collective-permute-start(bf16[20,32,768]{2,1,0:T(8,128)(2,1)} %get-tuple-element.12), channel_id=1, source_target_pairs={{0,64},{1,9},{2,66},{3,11},{4,68},{5,13},{6,70},{7,15},{8,72},{9,1... | collective-permute-start | bytes 2949128 | tf_op jit(solution)/shard_map/ppermute | solution.py:111
  65.6 4.6 %collective-permute-start.3 = (bf16[20,32,768]{2,1,0:T(8,128)(2,1)}, bf16[20,32,768]{2,1,0:T(8,128)(2,1)S(1)}, u32[]{:S(2)}, u32[]{:S(2)}) collective-permute-start(bf16[20,32,768]{2,1,0:T(8,128)(2,1)} %get-tuple-element.11), channel_id=1, source_target_pairs={{0,448},{1,57},{2,450},{3,59},{4,452},{5,61},{6,454},{7,63},{8,456... | collective-permute-start | bytes 2949128 | tf_op jit(solution)/shard_map/ppermute | solution.py:111
  70.2 0.8 all-to-all-done
  71.0 2.5 %fusion.1.rows_ref = bf16[640,1024]{1,0:T(8,128)(2,1)S(1)} fusion(bf16[640,1024]{1,0:T(8,128)(2,1)} %bitcast.7, s32[640]{0:T(1024)S(1)} %fusion.42), kind=kOutput, calls=%fused_computation.2 | convolution fusion | flops 839925760 | bytes 2624000 | tf_op jit(solution)/shard_map/dot_general | solution.py:135
  73.6 0.0 copy-start.3
  73.6 6.3 %collective-permute-done.2.refs_3_ = bf16[20,32,768]{2,1,0:T(8,128)(2,1)S(1)} collective-permute-done((bf16[20,32,768]{2,1,0:T(8,128)(2,1)}, bf16[20,32,768]{2,1,0:T(8,128)(2,1)S(1)}, u32[]{:S(2)}, u32[]{:S(2)}) %collective-permute-start.2) | collective-permute-done | bytes 983072 | tf_op jit(solution)/shard_map/ppermute | solution.py:111
  79.9 1.6 %collective-permute-done.3.refs_4_ = bf16[20,32,768]{2,1,0:T(8,128)(2,1)S(1)} collective-permute-done((bf16[20,32,768]{2,1,0:T(8,128)(2,1)}, bf16[20,32,768]{2,1,0:T(8,128)(2,1)S(1)}, u32[]{:S(2)}, u32[]{:S(2)}) %collective-permute-start.3) | collective-permute-done | bytes 983072 | tf_op jit(solution)/shard_map/ppermute | solution.py:111
  81.5 3.3 %shard_map.68 = bf16[640,384]{1,0:T(8,128)(2,1)} custom-call(bf16[640,1024]{1,0:T(8,128)(2,1)S(1)} %fusion.1.rows_ref, bf16[8,32,768]{2,1,0:T(8,128)(2,1)S(1)} %all-to-all-done.1.refs_0_, bf16[8,32,768]{2,1,0:T(8,128)(2,1)S(1)} %collective-permute-done.refs_1_, bf16[8,32,768]{2,1,0:T(8,128)(2,1)S(1)} %collective-permute-done.1.refs_2_, ...), custom_call_target="tpu_custom_call" | custom-call | flops 2000000000 | bytes 10000000 | tf_op jit(solution)/shard_map/pallas_call | solution.py:136
  84.8 13.0 %all-to-all-start.2 = ((bf16[16,40,384]{2,1,0:T(8,128)(2,1)}), bf16[16,40,384]{2,1,0:T(8,128)(2,1)S(1)}, u32[]{:S(2)}, u32[]{:S(2)}) async-start(bf16[16,40,384]{2,1,0:T(8,128)(2,1)} %bitcast.9), calls=%async_computation.2 | async-start | bytes 983040 | tf_op jit(solution)/shard_map/all_to_all | solution.py:145
  97.9 16.6 %all-to-all-done.2 = bf16[16,40,384]{2,1,0:T(8,128)(2,1)S(1)} async-done(((bf16[16,40,384]{2,1,0:T(8,128)(2,1)}), bf16[16,40,384]{2,1,0:T(8,128)(2,1)S(1)}, u32[]{:S(2)}, u32[]{:S(2)}) %all-to-all-start.2) | async-done | bytes 491552 | tf_op jit(solution)/shard_map/all_to_all | solution.py:145
  114.5 0.3 fusion.25
  114.8 0.3 fusion.23
  115.2 0.8 fusion.28
  116.0 0.8 pad_maximum_fusion.4
  (13 shorter events, 0.1 us)
Async XLA Ops:
  0.6 10.7 %copy-start.2 = (s32[128,1]{0,1:T(1,128)S(1)}, s32[128,1]{0,1:T(1,128)}, u32[]{:S(2)}) copy-start(s32[128,1]{0,1:T(1,128)} %param.8) | copy-start | bytes 1540
  0.6 10.9 %copy-start = (bf16[128,4096]{1,0:T(8,128)(2,1)S(1)}, bf16[128,4096]{1,0:T(8,128)(2,1)}, u32[]{:S(2)}) copy-start(bf16[128,4096]{1,0:T(8,128)(2,1)} %param.5) | copy-start | bytes 3145732
  2.3 18.8 %all-to-all-start.1 = ((bf16[8,32,768]{2,1,0:T(8,128)(2,1)}), bf16[8,32,768]{2,1,0:T(8,128)(2,1)S(1)}, u32[]{:S(2)}, u32[]{:S(2)}) async-start(bf16[8,32,768]{2,1,0:T(8,128)(2,1)} %broadcast_in_dim.5), calls=%async_computation.1 | async-start | bytes 786432 | tf_op jit(solution)/shard_map/all_to_all | solution.py:99
  21.2 49.9 %all-to-all-start = ((bf16[16,40,1024]{2,1,0:T(8,128)(2,1)}), bf16[16,40,1024]{2,1,0:T(8,128)(2,1)}, u32[]{:S(2)}, u32[]{:S(2)}) async-start(bf16[16,40,1024]{2,1,0:T(8,128)(2,1)} %bitcast.6), calls=%async_computation | async-start | bytes 2621440 | tf_op jit(solution)/shard_map/all_to_all | solution.py:130
  39.2 18.3 %collective-permute-start.1 = (bf16[8,32,768]{2,1,0:T(8,128)(2,1)S(1)}, bf16[8,32,768]{2,1,0:T(8,128)(2,1)S(1)}, u32[]{:S(2)}, u32[]{:S(2)}) collective-permute-start(bf16[8,32,768]{2,1,0:T(8,128)(2,1)S(1)} %all-to-all-done.1.refs_0_), channel_id=1, source_target_pairs={{0,192},{1,25},{2,194},{3,27},{4,196},{5,29},{6,198},{7,31},{8,200... | collective-permute-start | bytes 1179656 | tf_op jit(solution)/shard_map/ppermute | solution.py:108
  41.2 21.0 %collective-permute-start = (bf16[8,32,768]{2,1,0:T(8,128)(2,1)S(1)}, bf16[8,32,768]{2,1,0:T(8,128)(2,1)S(1)}, u32[]{:S(2)}, u32[]{:S(2)}) collective-permute-start(bf16[8,32,768]{2,1,0:T(8,128)(2,1)S(1)} %all-to-all-done.1.refs_0_), channel_id=1, source_target_pairs={{0,320},{1,41},{2,322},{3,43},{4,324},{5,45},{6,326},{7,47},{8,328... | collective-permute-start | bytes 1179656 | tf_op jit(solution)/shard_map/ppermute | solution.py:107
  63.7 16.2 %collective-permute-start.2 = (bf16[20,32,768]{2,1,0:T(8,128)(2,1)}, bf16[20,32,768]{2,1,0:T(8,128)(2,1)S(1)}, u32[]{:S(2)}, u32[]{:S(2)}) collective-permute-start(bf16[20,32,768]{2,1,0:T(8,128)(2,1)} %get-tuple-element.12), channel_id=1, source_target_pairs={{0,64},{1,9},{2,66},{3,11},{4,68},{5,13},{6,70},{7,15},{8,72},{9,1... | collective-permute-start | bytes 2949128 | tf_op jit(solution)/shard_map/ppermute | solution.py:111
  65.6 15.9 %collective-permute-start.3 = (bf16[20,32,768]{2,1,0:T(8,128)(2,1)}, bf16[20,32,768]{2,1,0:T(8,128)(2,1)S(1)}, u32[]{:S(2)}, u32[]{:S(2)}) collective-permute-start(bf16[20,32,768]{2,1,0:T(8,128)(2,1)} %get-tuple-element.11), channel_id=1, source_target_pairs={{0,448},{1,57},{2,450},{3,59},{4,452},{5,61},{6,454},{7,63},{8,456... | collective-permute-start | bytes 2949128 | tf_op jit(solution)/shard_map/ppermute | solution.py:111
  73.6 24.3 %copy-start.3 = (bf16[128,1]{0,1:T(2,128)(2,1)S(1)}, bf16[128,1]{0,1:T(2,128)(2,1)}, u32[]{:S(2)}) copy-start(bf16[128,1]{0,1:T(2,128)(2,1)} %param.7) | copy-start | bytes 772
  84.8 30.3 %copy-start.1 = (bf16[128,1,1536]{2,0,1:T(8,128)(2,1)S(1)}, bf16[128,1,1536]{2,0,1:T(8,128)(2,1)}, u32[]{:S(2)}) copy-start(bf16[128,1,1536]{2,0,1:T(8,128)(2,1)} %param.6) | copy-start | bytes 1179652
  84.8 29.7 %all-to-all-start.2 = ((bf16[16,40,384]{2,1,0:T(8,128)(2,1)}), bf16[16,40,384]{2,1,0:T(8,128)(2,1)S(1)}, u32[]{:S(2)}, u32[]{:S(2)}) async-start(bf16[16,40,384]{2,1,0:T(8,128)(2,1)} %bitcast.9), calls=%async_computation.2 | async-start | bytes 983040 | tf_op jit(solution)/shard_map/all_to_all | solution.py:145

commit v7 on v6

--- a/solution.py
+++ b/solution.py
@@ -8,7 +8,6 @@
 D = 4096
 FFW = 768
 HALF = D // 2
-QUART = D // 4
 EXPERTS = 8
 CAP = 20
 PEERS = 16
@@ -72,24 +71,48 @@
     half = RING * RING // 2
     width = weight_ref.shape[1] * half
     back = jnp.dot(
-        rows_ref[: COUNT // 2], weight_ref[:half].reshape(width, FFW), preferred_element_type=jnp.float32
+        rows_ref[:, :width], weight_ref[:half].reshape(width, FFW), preferred_element_type=jnp.float32
     ) + jnp.dot(
-        rows_ref[COUNT // 2 :], weight_ref[half:].reshape(width, FFW), preferred_element_type=jnp.float32
+        rows_ref[:, width:], weight_ref[half:].reshape(width, FFW), preferred_element_type=jnp.float32
     )
     back = back.astype(jnp.bfloat16)
     back = jnp.concatenate([back[:, : FFW // 2], back[:, FFW // 2 :]], axis=0)
 
     i = lax.broadcasted_iota(jnp.int32, (1, COUNT), 1)
-    piece = (i >= COUNT // 2).astype(jnp.int32)
-    j = i - piece * (COUNT // 2)
-    source = (j * 3277) >> 16
-    order = source * (2 * CAP) + piece * CAP + j - source * CAP
+    columns = (i >= COUNT // 2).astype(jnp.int32)
+    j = i - columns * (COUNT // 2)
+    source = (j * 1639) >> 16
+    j = j - source * (2 * CAP)
+    other = (j >= CAP).astype(jnp.int32)
+    xl = jnp.where(lax.axis_index("xl") == 0, other, 1 - other)
+    order = xl * (COUNT // 2) + source * (2 * CAP) + columns * CAP + j - other * CAP
     give = (lax.broadcasted_iota(jnp.int32, (COUNT, COUNT), 0) == order).astype(jnp.bfloat16)
     out_ref[...] = jnp.dot(give, back, preferred_element_type=jnp.float32).astype(jnp.bfloat16)
 
 
-def onehot(index, rows):
-    return (jnp.arange(rows, dtype=jnp.int32)[:, None] == index[None, :]).astype(jnp.bfloat16)
+def gather_rows(cotangent_ref, came_ref, routes_ref, sent_ref):
+    tokens = cotangent_ref.shape[0]
+    half = pl.multiple_of(lax.axis_index("xl") * HALF, HALF)
+    square = (tokens, tokens)
+    before = (
+        lax.broadcasted_iota(jnp.int32, square, 0) < lax.broadcasted_iota(jnp.int32, square, 1)
+    ).astype(jnp.bfloat16)
+    expert = lax.broadcasted_iota(jnp.int32, (2 * EXPERTS, tokens), 0)
+    row = lax.broadcasted_iota(jnp.int32, (PEERS * CAP, tokens), 0)
+
+    def placing(routes, other):
+        member = expert == routes
+        earlier = jnp.dot(member.astype(jnp.bfloat16), before, preferred_element_type=jnp.float32)
+        rank = jnp.sum(jnp.where(member, earlier, 0.0), axis=0, keepdims=True).astype(jnp.int32)
+        return (row == routes * (2 * CAP) + other * CAP + rank).astype(jnp.bfloat16)
+
+    theirs = came_ref[tokens : tokens + 16, :tokens][:1].astype(jnp.float32).astype(jnp.int32)
+    sent_ref[...] = (
+        jnp.dot(
+            placing(routes_ref[...], 0), cotangent_ref[:, pl.ds(half, HALF)], preferred_element_type=jnp.float32
+        )
+        + jnp.dot(placing(theirs, 1), came_ref[:tokens], preferred_element_type=jnp.float32)
+    ).astype(jnp.bfloat16)
 
 
 def body(cotangent, gate_up, route_probs, routes, down_weight):
@@ -114,25 +137,23 @@
     member = (flat_routes[:, None] == jnp.arange(EXPERTS, dtype=jnp.int32)[None, :]).astype(jnp.int32)
     rank = jnp.sum(jnp.cumsum(member, axis=0) * member, axis=1) - 1
     first = flat_routes * (2 * CAP) + rank
-    both = jnp.concatenate([first, first + CAP])
-    placing = onehot(both, EXPERTS * 2 * CAP)
-    quarters = [cotangent[:, i * QUART : (i + 1) * QUART] for i in range(4)]
-    sent = jnp.stack(
-        [
-            jnp.dot(
-                placing,
-                jnp.concatenate([quarters[2 * h], quarters[2 * h + 1]], axis=0),
-                preferred_element_type=jnp.float32,
-            ).astype(jnp.bfloat16)
-            for h in range(2)
-        ]
-    ).reshape(PEERS, 2 * CAP, QUART)
-    got = lax.all_to_all(sent, SHARE, split_axis=0, concat_axis=0, tiled=True)
-
-    order = jnp.arange(COUNT, dtype=jnp.int32)
-    order = (order % (COUNT // 2)) // CAP * (2 * CAP) + order // (COUNT // 2) * CAP + order % CAP
-    take = (order[:, None] == jnp.arange(COUNT, dtype=jnp.int32)[None, :]).astype(jnp.bfloat16)
-    rows = jnp.dot(take, got.reshape(COUNT, QUART), preferred_element_type=jnp.float32).astype(jnp.bfloat16)
+
+    theirs = lax.dynamic_slice_in_dim(cotangent, (1 - lax.axis_index("xl")) * HALF, HALF, axis=1)
+    told = jnp.pad(routes.reshape(1, tokens).astype(jnp.bfloat16), ((0, 15), (0, HALF - tokens)))
+    came = lax.ppermute(jnp.concatenate([theirs, told], axis=0), "xl", [(0, 1), (1, 0)])
+    sent = pl.pallas_call(
+        gather_rows,
+        out_shape=jax.ShapeDtypeStruct((PEERS * CAP, HALF), jnp.bfloat16),
+        in_specs=[pl.BlockSpec(memory_space=pltpu.VMEM)] * 3,
+        out_specs=pl.BlockSpec(memory_space=pltpu.VMEM),
+        compiler_params=pltpu.CompilerParams(vmem_limit_bytes=20 * 2**20),
+        cost_estimate=pl.CostEstimate(flops=4 * 10**8, bytes_accessed=3 * 10**6, transcendentals=0),
+    )(cotangent, came, routes.reshape(1, tokens))
+    got = lax.all_to_all(
+        sent.reshape(EXPERTS, 2 * CAP, HALF), ("xh", "core"), split_axis=0, concat_axis=0, tiled=True
+    )
+
+    rows = jnp.where(lax.axis_index("xl") < 2, got.reshape(PEERS * CAP, HALF), 0)
     back = pl.pallas_call(
         product,
         out_shape=jax.ShapeDtypeStruct((COUNT, FFW // 2), jnp.bfloat16),

time: 117 us -> 122 us (1.043)
  waiting for transfers between devices: 47.7 us -> 52.1 us
  matrix products: 3.85 us -> 0.61 us
  Pallas kernels: 3.34 us -> 5.34 us
  starting transfers between devices: 53.9 us -> 55.3 us
    all_to_all x1, waiting for transfers between devices: 7.62 us -> 0.01 us  [body(): lax.all_to_all(jnp.broadcast_to(own[None], (RING,) + own.shape), TORUS, s...]
    ppermute x0 -> x1, waiting for transfers between devices: none -> 7.5 us  [body(): lax.ppermute(jnp.concatenate([theirs, told], axis=0), 'xl', [(0, 1), (1,...]
    ppermute x1, waiting for transfers between devices: 4.72 us -> 11.2 us  [body(): ahead = lax.ppermute(line, TORUS, second_shift(-3))]
    all_to_all x1, starting transfers between devices: 13 us -> 6.71 us  [body(): lax.all_to_all(back.reshape(PEERS, 2 * CAP, FFW // 2), SHARE, split_axis=...]
    ppermute x1, starting transfers between devices: 6.25 us -> 11 us  [body(): ahead = lax.ppermute(line, TORUS, second_shift(-3))]
    ppermute x1, waiting for transfers between devices: 9.97 us -> 5.35 us  [body(): behind = lax.ppermute(line, TORUS, second_shift(3))]
    dot_general x3 -> x0, matrix products: 3.23 us -> none  [the longest x1 2.54 us: body(): jnp.dot(take, got.reshape(COUNT, QUART), preferred_element_type=jnp.float32)]
    ppermute x0 -> x1, starting transfers between devices: none -> 3.12 us  [body(): lax.ppermute(jnp.concatenate([theirs, told], axis=0), 'xl', [(0, 1), (1,...]
  transfers between devices with their start and end apart: 7 -> 8, of which waited for: 7 -> 6; matrix products, arithmetic and copies ran while one was open for 6% -> 3% of each run, Pallas kernels for 0% -> 2%
where the time goes in v7:
time: 122 us
  starting transfers between devices  55.3 us (45%)
  waiting for transfers between devices  52.1 us (43%)
  other arithmetic  5.66 us (5%)
  Pallas kernels  5.34 us (4%)
  local copies, waits for them, and re-layouts  1.75 us (1%)
    all_to_all x1, starting transfers between devices, body(): lax.all_to_all(sent.reshape(EXPERTS, 2 * CAP, HALF), ('xh', 'core'), spli...  18 us
    all_to_all x1, waiting for transfers between devices, body(): lax.all_to_all(back.reshape(PEERS, 2 * CAP, FFW // 2), SHARE, split_axis=...  16.6 us
    ppermute x1, waiting for transfers between devices, body(): ahead = lax.ppermute(line, TORUS, second_shift(-3))  11.2 us
    ppermute x1, starting transfers between devices, body(): ahead = lax.ppermute(line, TORUS, second_shift(-3))  11 us
    ppermute x1, waiting for transfers between devices, body(): lax.ppermute(up, TORUS, second_shift(1))  8.33 us
    all_to_all x1, starting transfers between devices, body(): lax.all_to_all(jnp.broadcast_to(own[None], (RING,) + own.shape), TORUS, s...  8.11 us
    ppermute x1, waiting for transfers between devices, body(): lax.ppermute(jnp.concatenate([theirs, told], axis=0), 'xl', [(0, 1), (1,...  7.5 us
    all_to_all x1, starting transfers between devices, body(): lax.all_to_all(back.reshape(PEERS, 2 * CAP, FFW // 2), SHARE, split_axis=...  6.71 us
  transfers between devices with their start and end apart: 8, of which 6 were waited for; matrix products, arithmetic and copies ran while one was open for 3% of the time, Pallas kernels for 2%

profile of v7, /device:TPU:1, one launch (start us, length us, event | category | flops | bytes accessed | tf_op | source)
XLA Modules:
  0.0 121.6 jit_solution(1304881900551476717)
XLA Ops:
  0.6 0.0 copy-start.1
  0.6 0.0 copy-start
  0.7 1.7 %broadcast_in_dim.10 = bf16[8,32,768]{2,1,0:T(8,128)(2,1)} broadcast(bf16[32,768]{1,0:T(8,128)(2,1)} %bitcast.38), dimensions={1,2} | broadcast | bytes 442368 | tf_op jit(solution)/shard_map/broadcast_in_dim | solution.py:123
  2.3 8.1 %all-to-all-start.1 = ((bf16[8,32,768]{2,1,0:T(8,128)(2,1)}), bf16[8,32,768]{2,1,0:T(8,128)(2,1)S(1)}, u32[]{:S(2)}, u32[]{:S(2)}) async-start(bf16[8,32,768]{2,1,0:T(8,128)(2,1)} %broadcast_in_dim.10), calls=%async_computation.1 | async-start | bytes 786432 | tf_op jit(solution)/shard_map/all_to_all | solution.py:122
  10.4 0.7 fusion.24
  11.2 0.2 reduce_window_sum.11
  11.3 0.0 copy-done.1
  11.3 0.2 select_reduce_fusion
  11.6 0.1 fusion.3
  11.7 3.1 %collective-permute-start = (bf16[144,2048]{1,0:T(8,128)(2,1)S(1)}, bf16[144,2048]{1,0:T(8,128)(2,1)S(1)}, u32[]{:S(2)}, u32[]{:S(2)}) collective-permute-start(bf16[144,2048]{1,0:T(8,128)(2,1)S(1)} %fusion.3), channel_id=1, source_target_pairs={{0,512},{512,0},{1,513},{513,1},{2,514},{514,2},{3,515},{515,3},{4... | collective-permute-start | bytes 1769480 | tf_op jit(solution)/shard_map/ppermute | solution.py:143
  14.8 7.5 %collective-permute-done.came_ref = bf16[144,2048]{1,0:T(8,128)(2,1)S(1)} collective-permute-done((bf16[144,2048]{1,0:T(8,128)(2,1)S(1)}, bf16[144,2048]{1,0:T(8,128)(2,1)S(1)}, u32[]{:S(2)}, u32[]{:S(2)}) %collective-permute-start) | collective-permute-done | bytes 589856 | tf_op jit(solution)/shard_map/ppermute | solution.py:143
  22.3 2.0 %shard_map.68 = bf16[320,2048]{1,0:T(8,128)(2,1)} custom-call(bf16[128,4096]{1,0:T(8,128)(2,1)S(1)} %copy-done, bf16[144,2048]{1,0:T(8,128)(2,1)S(1)} %collective-permute-done.came_ref, s32[1,128]{1,0:T(1,128)S(1)} %bitcast.34), custom_call_target="tpu_custom_call" | custom-call | flops 400000000 | bytes 3000000 | tf_op jit(solution)/shard_map/pallas_call | solution.py:144
  24.3 0.0 all-to-all-done.1.refs_0_
  24.3 18.0 %all-to-all-start = ((bf16[8,40,2048]{2,1,0:T(8,128)(2,1)}), bf16[8,40,2048]{2,1,0:T(8,128)(2,1)}, u32[]{:S(2)}, u32[]{:S(2)}) async-start(bf16[8,40,2048]{2,1,0:T(8,128)(2,1)} %bitcast.5), calls=%async_computation | async-start | bytes 2621440 | tf_op jit(solution)/shard_map/all_to_all | solution.py:152
  42.3 11.0 %collective-permute-start.1 = (bf16[8,32,768]{2,1,0:T(8,128)(2,1)S(1)}, bf16[8,32,768]{2,1,0:T(8,128)(2,1)S(1)}, u32[]{:S(2)}, u32[]{:S(2)}) collective-permute-start(bf16[8,32,768]{2,1,0:T(8,128)(2,1)S(1)} %all-to-all-done.1.refs_0_), channel_id=1, source_target_pairs={{0,320},{1,41},{2,322},{3,43},{4,324},{5,45},{6,326},{7,47},{8,328... | collective-permute-start | bytes 1179656 | tf_op jit(solution)/shard_map/ppermute | solution.py:130
  53.2 1.9 %collective-permute-start.2 = (bf16[8,32,768]{2,1,0:T(8,128)(2,1)S(1)}, bf16[8,32,768]{2,1,0:T(8,128)(2,1)S(1)}, u32[]{:S(2)}, u32[]{:S(2)}) collective-permute-start(bf16[8,32,768]{2,1,0:T(8,128)(2,1)S(1)} %all-to-all-done.1.refs_0_), channel_id=1, source_target_pairs={{0,192},{1,25},{2,194},{3,27},{4,196},{5,29},{6,198},{7,31},{8,200... | collective-permute-start | bytes 1179656 | tf_op jit(solution)/shard_map/ppermute | solution.py:131
  55.2 11.2 %collective-permute-done.1.refs_1_ = bf16[8,32,768]{2,1,0:T(8,128)(2,1)S(1)} collective-permute-done((bf16[8,32,768]{2,1,0:T(8,128)(2,1)S(1)}, bf16[8,32,768]{2,1,0:T(8,128)(2,1)S(1)}, u32[]{:S(2)}, u32[]{:S(2)}) %collective-permute-start.1) | collective-permute-done | bytes 393248 | tf_op jit(solution)/shard_map/ppermute | solution.py:130
  66.4 5.4 %collective-permute-done.2.refs_2_ = bf16[8,32,768]{2,1,0:T(8,128)(2,1)S(1)} collective-permute-done((bf16[8,32,768]{2,1,0:T(8,128)(2,1)S(1)}, bf16[8,32,768]{2,1,0:T(8,128)(2,1)S(1)}, u32[]{:S(2)}, u32[]{:S(2)}) %collective-permute-start.2) | collective-permute-done | bytes 393248 | tf_op jit(solution)/shard_map/ppermute | solution.py:131
  71.8 1.5 %fusion.2 = (bf16[20,32,768]{2,1,0:T(8,128)(2,1)}, bf16[20,32,768]{2,1,0:T(8,128)(2,1)}) fusion(bf16[8,32,768]{2,1,0:T(8,128)(2,1)S(1)} %all-to-all-done.1.refs_0_, bf16[4,32,768]{2,1,0:T(8,128)(2,1)S(1)} %slice.17, bf16[8,32,768]{2,1,0:T(8,128)(2,1)S(1)} %collective-permute-done.2.refs_2_, bf16[4,32,768]{2,1,0:T(8,128)(2,1)S(1)} %slice.16, ...), kind=kLoop, calls=%fused_computation.6 | loop fusion | flops 1966080 | bytes 3538944 | tf_op jit(solution)/shard_map/concatenate | solution.py:133
  73.3 3.2 %collective-permute-start.3 = (bf16[20,32,768]{2,1,0:T(8,128)(2,1)}, bf16[20,32,768]{2,1,0:T(8,128)(2,1)S(1)}, u32[]{:S(2)}, u32[]{:S(2)}) collective-permute-start(bf16[20,32,768]{2,1,0:T(8,128)(2,1)} %get-tuple-element.6), channel_id=1, source_target_pairs={{0,64},{1,9},{2,66},{3,11},{4,68},{5,13},{6,70},{7,15},{8,72},{9,1... | collective-permute-start | bytes 2949128 | tf_op jit(solution)/shard_map/ppermute | solution.py:134
  76.5 3.3 %collective-permute-start.4 = (bf16[20,32,768]{2,1,0:T(8,128)(2,1)}, bf16[20,32,768]{2,1,0:T(8,128)(2,1)S(1)}, u32[]{:S(2)}, u32[]{:S(2)}) collective-permute-start(bf16[20,32,768]{2,1,0:T(8,128)(2,1)} %get-tuple-element.5), channel_id=1, source_target_pairs={{0,448},{1,57},{2,450},{3,59},{4,452},{5,61},{6,454},{7,63},{8,456... | collective-permute-start | bytes 2949128 | tf_op jit(solution)/shard_map/ppermute | solution.py:134
  79.8 0.0 all-to-all-done
  79.8 1.4 %broadcast_select_fusion = bf16[8,40,2048]{2,1,0:T(8,128)(2,1)S(1)} fusion(bf16[8,40,2048]{2,1,0:T(8,128)(2,1)} %all-to-all-done, pred[]{:T(512)S(6)} %lt.15), kind=kLoop, calls=%fused_computation | loop fusion | flops 655360 | bytes 2621441 | tf_op jit(solution)/shard_map/jit(_where)/select_n | solution.py:156
  81.2 8.3 %collective-permute-done.3.refs_3_ = bf16[20,32,768]{2,1,0:T(8,128)(2,1)S(1)} collective-permute-done((bf16[20,32,768]{2,1,0:T(8,128)(2,1)}, bf16[20,32,768]{2,1,0:T(8,128)(2,1)S(1)}, u32[]{:S(2)}, u32[]{:S(2)}) %collective-permute-start.3) | collective-permute-done | bytes 983072 | tf_op jit(solution)/shard_map/ppermute | solution.py:134
  89.5 3.1 %collective-permute-done.4.refs_4_ = bf16[20,32,768]{2,1,0:T(8,128)(2,1)S(1)} collective-permute-done((bf16[20,32,768]{2,1,0:T(8,128)(2,1)}, bf16[20,32,768]{2,1,0:T(8,128)(2,1)S(1)}, u32[]{:S(2)}, u32[]{:S(2)}) %collective-permute-start.4) | collective-permute-done | bytes 983072 | tf_op jit(solution)/shard_map/ppermute | solution.py:134
  92.6 3.3 %shard_map.69 = bf16[640,384]{1,0:T(8,128)(2,1)} custom-call(bf16[320,2048]{1,0:T(8,128)(2,1)S(1)} %bitcast.31, bf16[8,32,768]{2,1,0:T(8,128)(2,1)S(1)} %all-to-all-done.1.refs_0_, bf16[8,32,768]{2,1,0:T(8,128)(2,1)S(1)} %collective-permute-done.1.refs_1_, bf16[8,32,768]{2,1,0:T(8,128)(2,1)S(1)} %collective-permute-done.2.refs_2_, ...), custom_call_target="tpu_custom_call" | custom-call | flops 2000000000 | bytes 10000000 | tf_op jit(solution)/shard_map/pallas_call | solution.py:157
  95.9 6.7 %all-to-all-start.2 = ((bf16[16,40,384]{2,1,0:T(8,128)(2,1)}), bf16[16,40,384]{2,1,0:T(8,128)(2,1)S(1)}, u32[]{:S(2)}, u32[]{:S(2)}) async-start(bf16[16,40,384]{2,1,0:T(8,128)(2,1)} %bitcast.8), calls=%async_computation.2 | async-start | bytes 983040 | tf_op jit(solution)/shard_map/all_to_all | solution.py:166
  102.7 16.6 %all-to-all-done.2 = bf16[16,40,384]{2,1,0:T(8,128)(2,1)S(1)} async-done(((bf16[16,40,384]{2,1,0:T(8,128)(2,1)}), bf16[16,40,384]{2,1,0:T(8,128)(2,1)S(1)}, u32[]{:S(2)}, u32[]{:S(2)}) %all-to-all-start.2) | async-done | bytes 491552 | tf_op jit(solution)/shard_map/all_to_all | solution.py:166
  119.3 0.3 fusion.14
  119.6 0.3 fusion.16
  119.9 0.8 fusion.19
  120.8 0.8 pad_maximum_fusion.3
  (11 shorter events, 0.1 us)
Async XLA Ops:
  0.6 10.7 %copy-start.1 = (s32[128,1]{0,1:T(1,128)S(1)}, s32[128,1]{0,1:T(1,128)}, u32[]{:S(2)}) copy-start(s32[128,1]{0,1:T(1,128)} %param.8) | copy-start | bytes 1540
  0.6 10.9 %copy-start = (bf16[128,4096]{1,0:T(8,128)(2,1)S(1)}, bf16[128,4096]{1,0:T(8,128)(2,1)}, u32[]{:S(2)}) copy-start(bf16[128,4096]{1,0:T(8,128)(2,1)} %cotangent_ref.1) | copy-start | bytes 3145732
  2.3 22.0 %all-to-all-start.1 = ((bf16[8,32,768]{2,1,0:T(8,128)(2,1)}), bf16[8,32,768]{2,1,0:T(8,128)(2,1)S(1)}, u32[]{:S(2)}, u32[]{:S(2)}) async-start(bf16[8,32,768]{2,1,0:T(8,128)(2,1)} %broadcast_in_dim.10), calls=%async_computation.1 | async-start | bytes 786432 | tf_op jit(solution)/shard_map/all_to_all | solution.py:122
  11.7 10.6 %collective-permute-start = (bf16[144,2048]{1,0:T(8,128)(2,1)S(1)}, bf16[144,2048]{1,0:T(8,128)(2,1)S(1)}, u32[]{:S(2)}, u32[]{:S(2)}) collective-permute-start(bf16[144,2048]{1,0:T(8,128)(2,1)S(1)} %fusion.3), channel_id=1, source_target_pairs={{0,512},{512,0},{1,513},{513,1},{2,514},{514,2},{3,515},{515,3},{4... | collective-permute-start | bytes 1769480 | tf_op jit(solution)/shard_map/ppermute | solution.py:143
  24.3 55.5 %all-to-all-start = ((bf16[8,40,2048]{2,1,0:T(8,128)(2,1)}), bf16[8,40,2048]{2,1,0:T(8,128)(2,1)}, u32[]{:S(2)}, u32[]{:S(2)}) async-start(bf16[8,40,2048]{2,1,0:T(8,128)(2,1)} %bitcast.5), calls=%async_computation | async-start | bytes 2621440 | tf_op jit(solution)/shard_map/all_to_all | solution.py:152
  42.3 24.1 %collective-permute-start.1 = (bf16[8,32,768]{2,1,0:T(8,128)(2,1)S(1)}, bf16[8,32,768]{2,1,0:T(8,128)(2,1)S(1)}, u32[]{:S(2)}, u32[]{:S(2)}) collective-permute-start(bf16[8,32,768]{2,1,0:T(8,128)(2,1)S(1)} %all-to-all-done.1.refs_0_), channel_id=1, source_target_pairs={{0,320},{1,41},{2,322},{3,43},{4,324},{5,45},{6,326},{7,47},{8,328... | collective-permute-start | bytes 1179656 | tf_op jit(solution)/shard_map/ppermute | solution.py:130
  53.2 18.5 %collective-permute-start.2 = (bf16[8,32,768]{2,1,0:T(8,128)(2,1)S(1)}, bf16[8,32,768]{2,1,0:T(8,128)(2,1)S(1)}, u32[]{:S(2)}, u32[]{:S(2)}) collective-permute-start(bf16[8,32,768]{2,1,0:T(8,128)(2,1)S(1)} %all-to-all-done.1.refs_0_), channel_id=1, source_target_pairs={{0,192},{1,25},{2,194},{3,27},{4,196},{5,29},{6,198},{7,31},{8,200... | collective-permute-start | bytes 1179656 | tf_op jit(solution)/shard_map/ppermute | solution.py:131
  73.3 16.2 %collective-permute-start.3 = (bf16[20,32,768]{2,1,0:T(8,128)(2,1)}, bf16[20,32,768]{2,1,0:T(8,128)(2,1)S(1)}, u32[]{:S(2)}, u32[]{:S(2)}) collective-permute-start(bf16[20,32,768]{2,1,0:T(8,128)(2,1)} %get-tuple-element.6), channel_id=1, source_target_pairs={{0,64},{1,9},{2,66},{3,11},{4,68},{5,13},{6,70},{7,15},{8,72},{9,1... | collective-permute-start | bytes 2949128 | tf_op jit(solution)/shard_map/ppermute | solution.py:134
  76.5 16.1 %collective-permute-start.4 = (bf16[20,32,768]{2,1,0:T(8,128)(2,1)}, bf16[20,32,768]{2,1,0:T(8,128)(2,1)S(1)}, u32[]{:S(2)}, u32[]{:S(2)}) collective-permute-start(bf16[20,32,768]{2,1,0:T(8,128)(2,1)} %get-tuple-element.5), channel_id=1, source_target_pairs={{0,448},{1,57},{2,450},{3,59},{4,452},{5,61},{6,454},{7,63},{8,456... | collective-permute-start | bytes 2949128 | tf_op jit(solution)/shard_map/ppermute | solution.py:134
  92.6 10.1 %copy-start.3 = (bf16[128,1]{0,1:T(2,128)(2,1)S(1)}, bf16[128,1]{0,1:T(2,128)(2,1)}, u32[]{:S(2)}) copy-start(bf16[128,1]{0,1:T(2,128)(2,1)} %param.7) | copy-start | bytes 772
  95.9 24.0 %copy-start.2 = (bf16[128,1,1536]{2,0,1:T(8,128)(2,1)S(1)}, bf16[128,1,1536]{2,0,1:T(8,128)(2,1)}, u32[]{:S(2)}) copy-start(bf16[128,1,1536]{2,0,1:T(8,128)(2,1)} %param.6) | copy-start | bytes 1179652
  95.9 23.4 %all-to-all-start.2 = ((bf16[16,40,384]{2,1,0:T(8,128)(2,1)}), bf16[16,40,384]{2,1,0:T(8,128)(2,1)S(1)}, u32[]{:S(2)}, u32[]{:S(2)}) async-start(bf16[16,40,384]{2,1,0:T(8,128)(2,1)} %bitcast.8), calls=%async_computation.2 | async-start | bytes 983040 | tf_op jit(solution)/shard_map/all_to_all | solution.py:166

commit v8 on v6

--- a/solution.py
+++ b/solution.py
@@ -86,6 +86,34 @@
     order = source * (2 * CAP) + piece * CAP + j - source * CAP
     give = (lax.broadcasted_iota(jnp.int32, (COUNT, COUNT), 0) == order).astype(jnp.bfloat16)
     out_ref[...] = jnp.dot(give, back, preferred_element_type=jnp.float32).astype(jnp.bfloat16)
+
+
+def finish(came_ref, pre_ref, probs_ref, first_ref, grads_ref, grad_probs_ref):
+    tokens = pre_ref.shape[0]
+    square = (tokens, tokens)
+    line = lax.broadcasted_iota(jnp.int32, square, 0)
+    told = jnp.where(line == 0, first_ref[...].astype(jnp.float32), probs_ref[...].astype(jnp.float32)).T
+    first, prob = told[:, :1].astype(jnp.int32), told[:, 1:2]
+    place = lax.broadcasted_iota(jnp.int32, (tokens, COUNT), 1)
+    place = jnp.where(place >= COUNT // 2, place - COUNT // 2, place)
+    total = jnp.zeros((tokens, 1), jnp.float32)
+    part = FFW // 2
+    for c in range(2):
+        back = jnp.dot(
+            (place == first + c * CAP).astype(jnp.bfloat16), came_ref[...], preferred_element_type=jnp.float32
+        )
+        gate = pre_ref[:, c * part : (c + 1) * part].astype(jnp.float32)
+        up = pre_ref[:, FFW + c * part : FFW + (c + 1) * part].astype(jnp.float32)
+        squash = 1.0 / (1.0 + jnp.exp(-gate))
+        silu = gate * squash
+        hidden = (silu * up).astype(jnp.bfloat16).astype(jnp.float32)
+        total += jnp.sum(hidden * back, axis=1, keepdims=True)
+        scaled = prob * back
+        grads_ref[:, c * part : (c + 1) * part] = (
+            scaled * up * squash * (1.0 + gate * (1.0 - squash))
+        ).astype(jnp.bfloat16)
+        grads_ref[:, FFW + c * part : FFW + (c + 1) * part] = (scaled * silu).astype(jnp.bfloat16)
+    grad_probs_ref[...] = jnp.broadcast_to(total, square).T[:1].astype(jnp.bfloat16)
 
 
 def onehot(index, rows):
@@ -146,30 +174,18 @@
         back.reshape(PEERS, 2 * CAP, FFW // 2), SHARE, split_axis=0, concat_axis=0, tiled=True
     ).reshape(COUNT, FFW // 2)
 
-    place = jnp.arange(COUNT, dtype=jnp.int32) % (COUNT // 2)
-    back_hidden = jnp.concatenate(
-        [
-            jnp.dot(
-                (place[None, :] == (first + c * CAP)[:, None]).astype(jnp.bfloat16),
-                came,
-                preferred_element_type=jnp.float32,
-            )
-            for c in range(2)
-        ],
-        axis=1,
-    )
-
-    flat_pre = gate_up.reshape(tokens, 2 * FFW)
-    gate = flat_pre[:, :FFW].astype(jnp.float32)
-    up = flat_pre[:, FFW:].astype(jnp.float32)
-    squash = jax.nn.sigmoid(gate)
-    hidden = (gate * squash * up).astype(jnp.bfloat16).astype(jnp.float32)
-    grad_probs = jnp.sum(hidden * back_hidden, axis=1, keepdims=True).astype(jnp.bfloat16)
-    scaled = route_probs.astype(jnp.float32) * back_hidden
-    grad_gate = scaled * up * squash * (1.0 + gate * (1.0 - squash))
-    grad_up = scaled * gate * squash
-    grads = jnp.concatenate([grad_gate, grad_up], axis=-1).astype(jnp.bfloat16)
-    return grads.reshape(tokens, 1, 2 * FFW), grad_probs
+    grads, grad_probs = pl.pallas_call(
+        finish,
+        out_shape=(
+            jax.ShapeDtypeStruct((tokens, 2 * FFW), jnp.bfloat16),
+            jax.ShapeDtypeStruct((1, tokens), jnp.bfloat16),
+        ),
+        in_specs=[pl.BlockSpec(memory_space=pltpu.VMEM)] * 4,
+        out_specs=(pl.BlockSpec(memory_space=pltpu.VMEM),) * 2,
+        compiler_params=pltpu.CompilerParams(vmem_limit_bytes=20 * 2**20),
+        cost_estimate=pl.CostEstimate(flops=2 * 10**8, bytes_accessed=2 * 10**6, transcendentals=10**5),
+    )(came, gate_up.reshape(tokens, 2 * FFW), route_probs.reshape(1, tokens), first.reshape(1, tokens))
+    return grads.reshape(tokens, 1, 2 * FFW), grad_probs.reshape(tokens, 1)
 
 
 def solution(mesh):

time: 117 us -> 115 us (0.983)
  starting transfers between devices: 53.9 us -> 49 us
  waiting for transfers between devices: 47.7 us -> 51 us
  other arithmetic: 5.41 us -> 3.77 us
  Pallas kernels: 3.34 us -> 4.76 us
    all_to_all x1, starting transfers between devices: 13 us -> 8.49 us  [body(): lax.all_to_all(back.reshape(PEERS, 2 * CAP, FFW // 2), SHARE, split_axis=...]
    ppermute x1, waiting for transfers between devices: 1.58 us -> 5.73 us  [body(): lax.ppermute(down, TORUS, second_shift(-1))]
    concatenate x2 -> x0, other arithmetic: 1.61 us -> none  [body(): grads = jnp.concatenate([grad_gate, grad_up], axis=-1).astype(jnp.bfloat16)]
    pallas_call x0 -> x1, Pallas kernels: none -> 1.43 us  [body(): pl.pallas_call(finish, out_shape=(jax.ShapeDtypeStruct((tokens, 2 * FFW),...]
where the time goes in v8:
time: 115 us; the launch traced here: 114 us
  waiting for transfers between devices  51 us (44%)
  starting transfers between devices  49 us (43%)
  Pallas kernels  4.76 us (4%)
  other arithmetic  3.77 us (3%)
  matrix products  3.23 us (3%)
  local copies, waits for them, and re-layouts  1.8 us (2%)
    all_to_all x1, starting transfers between devices, body(): got = lax.all_to_all(sent, SHARE, split_axis=0, concat_axis=0, tiled=True)  18 us
    all_to_all x1, waiting for transfers between devices, body(): lax.all_to_all(back.reshape(PEERS, 2 * CAP, FFW // 2), SHARE, split_axis=...  16.6 us
    ppermute x1, waiting for transfers between devices, body(): behind = lax.ppermute(line, TORUS, second_shift(3))  9.97 us
    all_to_all x1, starting transfers between devices, body(): lax.all_to_all(back.reshape(PEERS, 2 * CAP, FFW // 2), SHARE, split_axis=...  8.49 us
    all_to_all x1, starting transfers between devices, body(): lax.all_to_all(jnp.broadcast_to(own[None], (RING,) + own.shape), TORUS, s...  8.11 us
    all_to_all x1, waiting for transfers between devices, body(): lax.all_to_all(jnp.broadcast_to(own[None], (RING,) + own.shape), TORUS, s...  7.63 us
    ppermute x1, starting transfers between devices, body(): ahead = lax.ppermute(line, TORUS, second_shift(-3))  6.25 us
    ppermute x1, waiting for transfers between devices, body(): lax.ppermute(down, TORUS, second_shift(-1))  5.73 us
  transfers between devices with their start and end apart: 7, of which 7 were waited for; matrix products, arithmetic and copies ran while one was open for 6% of the time, Pallas kernels for 0%

profile of v8, /device:TPU:1, one launch (start us, length us, event | category | flops | bytes accessed | tf_op | source)
XLA Modules:
  0.0 114.4 jit_solution(4915488191242259848)
XLA Ops:
  0.6 0.0 copy-start.3
  0.6 0.0 copy-start.2
  0.7 1.7 %broadcast_in_dim.5 = bf16[8,32,768]{2,1,0:T(8,128)(2,1)} broadcast(bf16[32,768]{1,0:T(8,128)(2,1)} %bitcast.24), dimensions={1,2} | broadcast | bytes 442368 | tf_op jit(solution)/shard_map/broadcast_in_dim | solution.py:128
  2.3 8.1 %all-to-all-start.1 = ((bf16[8,32,768]{2,1,0:T(8,128)(2,1)}), bf16[8,32,768]{2,1,0:T(8,128)(2,1)S(1)}, u32[]{:S(2)}, u32[]{:S(2)}) async-start(bf16[8,32,768]{2,1,0:T(8,128)(2,1)} %broadcast_in_dim.5), calls=%async_computation.1 | async-start | bytes 786432 | tf_op jit(solution)/shard_map/all_to_all | solution.py:127
  10.4 0.7 fusion.15
  11.2 0.2 reduce_window_sum.11
  11.3 0.0 copy-done.3
  11.3 0.2 select_reduce_fusion
  11.6 0.1 fusion.40
  11.6 0.3 fusion.2
  12.0 0.3 fusion.3
  12.3 1.2 %pad_maximum_fusion = bf16[2,320,1024]{2,1,0:T(8,128)(2,1)} fusion(bf16[1,320,1024]{2,1,0:T(8,128)(2,1)S(1)} %fusion.3, bf16[1,320,1024]{2,1,0:T(8,128)(2,1)S(1)} %fusion.2), kind=kLoop, calls=%fused_computation.5 | loop fusion | flops 655360 | bytes 2621440 | tf_op jit(solution)/shard_map/stack | solution.py:148
  13.5 7.6 %all-to-all-done.1.refs_0_ = bf16[8,32,768]{2,1,0:T(8,128)(2,1)S(1)} async-done(((bf16[8,32,768]{2,1,0:T(8,128)(2,1)}), bf16[8,32,768]{2,1,0:T(8,128)(2,1)S(1)}, u32[]{:S(2)}, u32[]{:S(2)}) %all-to-all-start.1) | async-done | bytes 393248 | tf_op jit(solution)/shard_map/all_to_all | solution.py:127
  21.2 18.0 %all-to-all-start = ((bf16[16,40,1024]{2,1,0:T(8,128)(2,1)}), bf16[16,40,1024]{2,1,0:T(8,128)(2,1)}, u32[]{:S(2)}, u32[]{:S(2)}) async-start(bf16[16,40,1024]{2,1,0:T(8,128)(2,1)} %bitcast.3), calls=%async_computation | async-start | bytes 2621440 | tf_op jit(solution)/shard_map/all_to_all | solution.py:158
  39.2 2.0 %collective-permute-start.1 = (bf16[8,32,768]{2,1,0:T(8,128)(2,1)S(1)}, bf16[8,32,768]{2,1,0:T(8,128)(2,1)S(1)}, u32[]{:S(2)}, u32[]{:S(2)}) collective-permute-start(bf16[8,32,768]{2,1,0:T(8,128)(2,1)S(1)} %all-to-all-done.1.refs_0_), channel_id=1, source_target_pairs={{0,192},{1,25},{2,194},{3,27},{4,196},{5,29},{6,198},{7,31},{8,200... | collective-permute-start | bytes 1179656 | tf_op jit(solution)/shard_map/ppermute | solution.py:136
  41.2 6.2 %collective-permute-start = (bf16[8,32,768]{2,1,0:T(8,128)(2,1)S(1)}, bf16[8,32,768]{2,1,0:T(8,128)(2,1)S(1)}, u32[]{:S(2)}, u32[]{:S(2)}) collective-permute-start(bf16[8,32,768]{2,1,0:T(8,128)(2,1)S(1)} %all-to-all-done.1.refs_0_), channel_id=1, source_target_pairs={{0,320},{1,41},{2,322},{3,43},{4,324},{5,45},{6,326},{7,47},{8,328... | collective-permute-start | bytes 1179656 | tf_op jit(solution)/shard_map/ppermute | solution.py:135
  47.5 10.0 %collective-permute-done.1.refs_2_ = bf16[8,32,768]{2,1,0:T(8,128)(2,1)S(1)} collective-permute-done((bf16[8,32,768]{2,1,0:T(8,128)(2,1)S(1)}, bf16[8,32,768]{2,1,0:T(8,128)(2,1)S(1)}, u32[]{:S(2)}, u32[]{:S(2)}) %collective-permute-start.1) | collective-permute-done | bytes 393248 | tf_op jit(solution)/shard_map/ppermute | solution.py:136
  57.4 4.7 %collective-permute-done.refs_1_ = bf16[8,32,768]{2,1,0:T(8,128)(2,1)S(1)} collective-permute-done((bf16[8,32,768]{2,1,0:T(8,128)(2,1)S(1)}, bf16[8,32,768]{2,1,0:T(8,128)(2,1)S(1)}, u32[]{:S(2)}, u32[]{:S(2)}) %collective-permute-start) | collective-permute-done | bytes 393248 | tf_op jit(solution)/shard_map/ppermute | solution.py:135
  62.2 1.5 %fusion.5 = (bf16[20,32,768]{2,1,0:T(8,128)(2,1)}, bf16[20,32,768]{2,1,0:T(8,128)(2,1)}) fusion(bf16[8,32,768]{2,1,0:T(8,128)(2,1)S(1)} %all-to-all-done.1.refs_0_, bf16[4,32,768]{2,1,0:T(8,128)(2,1)S(1)} %slice.25, bf16[8,32,768]{2,1,0:T(8,128)(2,1)S(1)} %collective-permute-done.1.refs_2_, bf16[4,32,768]{2,1,0:T(8,128)(2,1)S(1)} %slice.24, ...), kind=kLoop, calls=%fused_computation.11 | loop fusion | flops 1966080 | bytes 3538944 | tf_op jit(solution)/shard_map/concatenate | solution.py:138
  63.7 4.2 %collective-permute-start.3 = (bf16[20,32,768]{2,1,0:T(8,128)(2,1)}, bf16[20,32,768]{2,1,0:T(8,128)(2,1)S(1)}, u32[]{:S(2)}, u32[]{:S(2)}) collective-permute-start(bf16[20,32,768]{2,1,0:T(8,128)(2,1)} %get-tuple-element.12), channel_id=1, source_target_pairs={{0,448},{1,57},{2,450},{3,59},{4,452},{5,61},{6,454},{7,63},{8,456... | collective-permute-start | bytes 2949128 | tf_op jit(solution)/shard_map/ppermute | solution.py:139
  67.9 1.9 %collective-permute-start.2 = (bf16[20,32,768]{2,1,0:T(8,128)(2,1)}, bf16[20,32,768]{2,1,0:T(8,128)(2,1)S(1)}, u32[]{:S(2)}, u32[]{:S(2)}) collective-permute-start(bf16[20,32,768]{2,1,0:T(8,128)(2,1)} %get-tuple-element.13), channel_id=1, source_target_pairs={{0,64},{1,9},{2,66},{3,11},{4,68},{5,13},{6,70},{7,15},{8,72},{9,1... | collective-permute-start | bytes 2949128 | tf_op jit(solution)/shard_map/ppermute | solution.py:139
  69.8 1.1 all-to-all-done
  70.9 2.5 %fusion.1.rows_ref = bf16[640,1024]{1,0:T(8,128)(2,1)S(1)} fusion(bf16[640,1024]{1,0:T(8,128)(2,1)} %bitcast.4, s32[640]{0:T(1024)S(1)} %fusion.28), kind=kOutput, calls=%fused_computation.2 | convolution fusion | flops 839925760 | bytes 2624000 | tf_op jit(solution)/shard_map/dot_general | solution.py:163
  73.5 0.0 copy-start
  73.5 0.0 copy-start.1
  73.5 5.7 %collective-permute-done.3.refs_4_ = bf16[20,32,768]{2,1,0:T(8,128)(2,1)S(1)} collective-permute-done((bf16[20,32,768]{2,1,0:T(8,128)(2,1)}, bf16[20,32,768]{2,1,0:T(8,128)(2,1)S(1)}, u32[]{:S(2)}, u32[]{:S(2)}) %collective-permute-start.3) | collective-permute-done | bytes 983072 | tf_op jit(solution)/shard_map/ppermute | solution.py:139
  79.2 5.2 %collective-permute-done.2.refs_3_ = bf16[20,32,768]{2,1,0:T(8,128)(2,1)S(1)} collective-permute-done((bf16[20,32,768]{2,1,0:T(8,128)(2,1)}, bf16[20,32,768]{2,1,0:T(8,128)(2,1)S(1)}, u32[]{:S(2)}, u32[]{:S(2)}) %collective-permute-start.2) | collective-permute-done | bytes 983072 | tf_op jit(solution)/shard_map/ppermute | solution.py:139
  84.5 3.3 %shard_map.68 = bf16[640,384]{1,0:T(8,128)(2,1)} custom-call(bf16[640,1024]{1,0:T(8,128)(2,1)S(1)} %fusion.1.rows_ref, bf16[8,32,768]{2,1,0:T(8,128)(2,1)S(1)} %all-to-all-done.1.refs_0_, bf16[8,32,768]{2,1,0:T(8,128)(2,1)S(1)} %collective-permute-done.refs_1_, bf16[8,32,768]{2,1,0:T(8,128)(2,1)S(1)} %collective-permute-done.1.refs_2_, ...), custom_call_target="tpu_custom_call" | custom-call | flops 2000000000 | bytes 10000000 | tf_op jit(solution)/shard_map/pallas_call | solution.py:164
  87.8 8.5 %all-to-all-start.2 = ((bf16[16,40,384]{2,1,0:T(8,128)(2,1)}), bf16[16,40,384]{2,1,0:T(8,128)(2,1)S(1)}, u32[]{:S(2)}, u32[]{:S(2)}) async-start(bf16[16,40,384]{2,1,0:T(8,128)(2,1)} %bitcast.6), calls=%async_computation.2 | async-start | bytes 983040 | tf_op jit(solution)/shard_map/all_to_all | solution.py:173
  96.3 16.6 %all-to-all-done.2 = bf16[16,40,384]{2,1,0:T(8,128)(2,1)S(1)} async-done(((bf16[16,40,384]{2,1,0:T(8,128)(2,1)}), bf16[16,40,384]{2,1,0:T(8,128)(2,1)S(1)}, u32[]{:S(2)}, u32[]{:S(2)}) %all-to-all-start.2) | async-done | bytes 491552 | tf_op jit(solution)/shard_map/all_to_all | solution.py:173
  112.9 0.0 copy-done.1
  112.9 1.4 %shard_map.69 = (bf16[128,1536]{1,0:T(8,128)(2,1)}, bf16[1,128]{1,0:T(2,128)(2,1)}) custom-call(bf16[640,384]{1,0:T(8,128)(2,1)S(1)} %bitcast.21, bf16[128,1536]{1,0:T(8,128)(2,1)S(1)} %bitcast.22, bf16[1,128]{1,0:T(2,128)(2,1)S(1)} %bitcast.23, s32[1,128]{1,0:T(1,128)S(1)} %bitcast_add_fusion.first_ref), custom_call_target="tpu_custom_call" | custom-call | flops 200000000 | bytes 2000000 | tf_op jit(solution)/shard_map/pallas_call | solution.py:177
  (8 shorter events, 0.1 us)
Async XLA Ops:
  0.6 10.7 %copy-start.3 = (s32[128,1]{0,1:T(1,128)S(1)}, s32[128,1]{0,1:T(1,128)}, u32[]{:S(2)}) copy-start(s32[128,1]{0,1:T(1,128)} %param.8) | copy-start | bytes 1540
  0.6 10.9 %copy-start.2 = (bf16[128,4096]{1,0:T(8,128)(2,1)S(1)}, bf16[128,4096]{1,0:T(8,128)(2,1)}, u32[]{:S(2)}) copy-start(bf16[128,4096]{1,0:T(8,128)(2,1)} %param.5) | copy-start | bytes 3145732
  2.3 18.8 %all-to-all-start.1 = ((bf16[8,32,768]{2,1,0:T(8,128)(2,1)}), bf16[8,32,768]{2,1,0:T(8,128)(2,1)S(1)}, u32[]{:S(2)}, u32[]{:S(2)}) async-start(bf16[8,32,768]{2,1,0:T(8,128)(2,1)} %broadcast_in_dim.5), calls=%async_computation.1 | async-start | bytes 786432 | tf_op jit(solution)/shard_map/all_to_all | solution.py:127
  21.2 49.8 %all-to-all-start = ((bf16[16,40,1024]{2,1,0:T(8,128)(2,1)}), bf16[16,40,1024]{2,1,0:T(8,128)(2,1)}, u32[]{:S(2)}, u32[]{:S(2)}) async-start(bf16[16,40,1024]{2,1,0:T(8,128)(2,1)} %bitcast.3), calls=%async_computation | async-start | bytes 2621440 | tf_op jit(solution)/shard_map/all_to_all | solution.py:158
  39.2 18.3 %collective-permute-start.1 = (bf16[8,32,768]{2,1,0:T(8,128)(2,1)S(1)}, bf16[8,32,768]{2,1,0:T(8,128)(2,1)S(1)}, u32[]{:S(2)}, u32[]{:S(2)}) collective-permute-start(bf16[8,32,768]{2,1,0:T(8,128)(2,1)S(1)} %all-to-all-done.1.refs_0_), channel_id=1, source_target_pairs={{0,192},{1,25},{2,194},{3,27},{4,196},{5,29},{6,198},{7,31},{8,200... | collective-permute-start | bytes 1179656 | tf_op jit(solution)/shard_map/ppermute | solution.py:136
  41.2 21.0 %collective-permute-start = (bf16[8,32,768]{2,1,0:T(8,128)(2,1)S(1)}, bf16[8,32,768]{2,1,0:T(8,128)(2,1)S(1)}, u32[]{:S(2)}, u32[]{:S(2)}) collective-permute-start(bf16[8,32,768]{2,1,0:T(8,128)(2,1)S(1)} %all-to-all-done.1.refs_0_), channel_id=1, source_target_pairs={{0,320},{1,41},{2,322},{3,43},{4,324},{5,45},{6,326},{7,47},{8,328... | collective-permute-start | bytes 1179656 | tf_op jit(solution)/shard_map/ppermute | solution.py:135
  63.7 15.6 %collective-permute-start.3 = (bf16[20,32,768]{2,1,0:T(8,128)(2,1)}, bf16[20,32,768]{2,1,0:T(8,128)(2,1)S(1)}, u32[]{:S(2)}, u32[]{:S(2)}) collective-permute-start(bf16[20,32,768]{2,1,0:T(8,128)(2,1)} %get-tuple-element.12), channel_id=1, source_target_pairs={{0,448},{1,57},{2,450},{3,59},{4,452},{5,61},{6,454},{7,63},{8,456... | collective-permute-start | bytes 2949128 | tf_op jit(solution)/shard_map/ppermute | solution.py:139
  67.9 16.6 %collective-permute-start.2 = (bf16[20,32,768]{2,1,0:T(8,128)(2,1)}, bf16[20,32,768]{2,1,0:T(8,128)(2,1)S(1)}, u32[]{:S(2)}, u32[]{:S(2)}) collective-permute-start(bf16[20,32,768]{2,1,0:T(8,128)(2,1)} %get-tuple-element.13), channel_id=1, source_target_pairs={{0,64},{1,9},{2,66},{3,11},{4,68},{5,13},{6,70},{7,15},{8,72},{9,1... | collective-permute-start | bytes 2949128 | tf_op jit(solution)/shard_map/ppermute | solution.py:139
  73.5 39.5 %copy-start = (bf16[128,1,1536]{2,0,1:T(8,128)(2,1)S(1)}, bf16[128,1,1536]{2,0,1:T(8,128)(2,1)}, u32[]{:S(2)}) copy-start(bf16[128,1,1536]{2,0,1:T(8,128)(2,1)} %param.6) | copy-start | bytes 1179652
  73.5 39.4 %copy-start.1 = (bf16[128,1]{0,1:T(2,128)(2,1)S(1)}, bf16[128,1]{0,1:T(2,128)(2,1)}, u32[]{:S(2)}) copy-start(bf16[128,1]{0,1:T(2,128)(2,1)} %param.7) | copy-start | bytes 772
  87.8 25.1 %all-to-all-start.2 = ((bf16[16,40,384]{2,1,0:T(8,128)(2,1)}), bf16[16,40,384]{2,1,0:T(8,128)(2,1)S(1)}, u32[]{:S(2)}, u32[]{:S(2)}) async-start(bf16[16,40,384]{2,1,0:T(8,128)(2,1)} %bitcast.6), calls=%async_computation.2 | async-start | bytes 983040 | tf_op jit(solution)/shard_map/all_to_all | solution.py:173

commit v9 on v8

--- a/solution.py
+++ b/solution.py
@@ -86,6 +86,15 @@
     order = source * (2 * CAP) + piece * CAP + j - source * CAP
     give = (lax.broadcasted_iota(jnp.int32, (COUNT, COUNT), 0) == order).astype(jnp.bfloat16)
     out_ref[...] = jnp.dot(give, back, preferred_element_type=jnp.float32).astype(jnp.bfloat16)
+
+
+def join(line_ref, ahead_ref, behind_ref, up_ref, down_ref):
+    up_ref[:RING] = line_ref[...]
+    up_ref[RING : 2 * RING] = ahead_ref[...]
+    up_ref[2 * RING :] = behind_ref[:HALF_RING]
+    down_ref[:RING] = line_ref[...]
+    down_ref[RING : 2 * RING] = behind_ref[...]
+    down_ref[2 * RING :] = ahead_ref[HALF_RING:]
 
 
 def finish(came_ref, pre_ref, probs_ref, first_ref, grads_ref, grad_probs_ref):
@@ -134,8 +143,15 @@
     )
     ahead = lax.ppermute(line, TORUS, second_shift(-3))
     behind = lax.ppermute(line, TORUS, second_shift(3))
-    up = jnp.concatenate([line, ahead, behind[:HALF_RING]], axis=0)
-    down = jnp.concatenate([line, behind, ahead[HALF_RING:]], axis=0)
+    passed = jax.ShapeDtypeStruct((2 * RING + HALF_RING,) + own.shape, jnp.bfloat16)
+    up, down = pl.pallas_call(
+        join,
+        out_shape=(passed, passed),
+        in_specs=[pl.BlockSpec(memory_space=pltpu.VMEM)] * 3,
+        out_specs=(pl.BlockSpec(memory_space=pltpu.VMEM),) * 2,
+        compiler_params=pltpu.CompilerParams(vmem_limit_bytes=16 * 2**20),
+        cost_estimate=pl.CostEstimate(flops=2 * 10**11, bytes_accessed=4 * 10**6, transcendentals=0),
+    )(line, ahead, behind)
     parts = [line, ahead, behind, lax.ppermute(up, TORUS, second_shift(1)), lax.ppermute(down, TORUS, second_shift(-1))]
 
     flat_routes = routes.reshape(tokens)

time: 115 us -> 114 us (level)
  Pallas kernels: 4.76 us -> 7.15 us
  other arithmetic: 3.77 us -> 2.31 us
  starting transfers between devices: 49 us -> 47.6 us
  waiting for transfers between devices: 51 us -> 49.7 us
    all_to_all x1, waiting for transfers between devices: 1.08 us -> 19.9 us  [body(): got = lax.all_to_all(sent, SHARE, split_axis=0, concat_axis=0, tiled=True)]
    ppermute x1, waiting for transfers between devices: 9.97 us -> 0.01 us  [body(): behind = lax.ppermute(line, TORUS, second_shift(3))]
    ppermute x1, starting transfers between devices: 2.03 us -> 10.3 us  [body(): behind = lax.ppermute(line, TORUS, second_shift(3))]
    all_to_all x1, starting transfers between devices: 18 us -> 10.4 us  [body(): got = lax.all_to_all(sent, SHARE, split_axis=0, concat_axis=0, tiled=True)]
    ppermute x1, waiting for transfers between devices: 5.73 us -> 0.01 us  [body(): lax.ppermute(down, TORUS, second_shift(-1))]
    ppermute x1, waiting for transfers between devices: 5.22 us -> 0.01 us  [body(): lax.ppermute(up, TORUS, second_shift(1))]
    all_to_all x1, starting transfers between devices: 8.49 us -> 5.46 us  [body(): lax.all_to_all(back.reshape(PEERS, 2 * CAP, FFW // 2), SHARE, split_axis=...]
    concatenate x1 -> x0, other arithmetic: 1.47 us -> none  [body(): down = jnp.concatenate([line, behind, ahead[HALF_RING:]], axis=0)]
  transfers between devices with their start and end apart: 7 -> 7, of which waited for: 7 -> 4; matrix products, arithmetic and copies ran while one was open for 6% -> 5% of each run, Pallas kernels for 0% -> 1%
where the time goes in v9:
time: 114 us; the launch traced here: 113 us
  waiting for transfers between devices  49.7 us (44%)
  starting transfers between devices  47.6 us (42%)
  Pallas kernels  7.15 us (6%)
  matrix products  3.27 us (3%)
  other arithmetic  2.31 us (2%)
  local copies, waits for them, and re-layouts  2.29 us (2%)
    all_to_all x1, waiting for transfers between devices, body(): got = lax.all_to_all(sent, SHARE, split_axis=0, concat_axis=0, tiled=True)  19.9 us
    all_to_all x1, waiting for transfers between devices, body(): lax.all_to_all(back.reshape(PEERS, 2 * CAP, FFW // 2), SHARE, split_axis=...  16.6 us
    all_to_all x1, starting transfers between devices, body(): got = lax.all_to_all(sent, SHARE, split_axis=0, concat_axis=0, tiled=True)  10.4 us
    ppermute x1, starting transfers between devices, body(): behind = lax.ppermute(line, TORUS, second_shift(3))  10.3 us
    all_to_all x1, waiting for transfers between devices, body(): lax.all_to_all(jnp.broadcast_to(own[None], (RING,) + own.shape), TORUS, s...  9.02 us
    all_to_all x1, starting transfers between devices, body(): lax.all_to_all(jnp.broadcast_to(own[None], (RING,) + own.shape), TORUS, s...  8.11 us
    ppermute x1, starting transfers between devices, body(): ahead = lax.ppermute(line, TORUS, second_shift(-3))  6.77 us
    all_to_all x1, starting transfers between devices, body(): lax.all_to_all(back.reshape(PEERS, 2 * CAP, FFW // 2), SHARE, split_axis=...  5.46 us
  transfers between devices with their start and end apart: 7, of which 4 were waited for; matrix products, arithmetic and copies ran while one was open for 5% of the time, Pallas kernels for 1%

profile of v9, /device:TPU:1, one launch (start us, length us, event | category | flops | bytes accessed | tf_op | source)
XLA Modules:
  0.0 113.2 jit_solution(6791442314780505330)
XLA Ops:
  0.6 0.0 copy-start.5
  0.7 1.7 %broadcast_in_dim.5 = bf16[8,32,768]{2,1,0:T(8,128)(2,1)} broadcast(bf16[32,768]{1,0:T(8,128)(2,1)} %bitcast.24), dimensions={1,2} | broadcast | bytes 442368 | tf_op jit(solution)/shard_map/broadcast_in_dim | solution.py:137
  2.3 8.1 %all-to-all-start.1 = ((bf16[8,32,768]{2,1,0:T(8,128)(2,1)}), bf16[8,32,768]{2,1,0:T(8,128)(2,1)S(1)}, u32[]{:S(2)}, u32[]{:S(2)}) async-start(bf16[8,32,768]{2,1,0:T(8,128)(2,1)} %broadcast_in_dim.5), calls=%async_computation.1 | async-start | bytes 786432 | tf_op jit(solution)/shard_map/all_to_all | solution.py:136
  10.4 0.7 fusion.13
  11.2 0.2 reduce_window_sum.11
  11.3 0.2 select_reduce_fusion
  11.5 0.0 copy-start.7
  11.5 0.5 copy-done.7
  12.0 0.1 fusion.38
  12.1 9.0 %all-to-all-done.1.line_ref.refs_0_ = bf16[8,32,768]{2,1,0:T(8,128)(2,1)S(1)} async-done(((bf16[8,32,768]{2,1,0:T(8,128)(2,1)}), bf16[8,32,768]{2,1,0:T(8,128)(2,1)S(1)}, u32[]{:S(2)}, u32[]{:S(2)}) %all-to-all-start.1) | async-done | bytes 393248 | tf_op jit(solution)/shard_map/all_to_all | solution.py:136
  21.2 10.3 %collective-permute-start.1 = (bf16[8,32,768]{2,1,0:T(8,128)(2,1)S(1)}, bf16[8,32,768]{2,1,0:T(8,128)(2,1)S(1)}, u32[]{:S(2)}, u32[]{:S(2)}) collective-permute-start(bf16[8,32,768]{2,1,0:T(8,128)(2,1)S(1)} %all-to-all-done.1.line_ref.refs_0_), channel_id=1, source_target_pairs={{0,192},{1,25},{2,194},{3,27},{4,196},{5,29},{6,198},{7,31},{8,200... | collective-permute-start | bytes 1179656 | tf_op jit(solution)/shard_map/ppermute | solution.py:145
  31.5 6.8 %collective-permute-start = (bf16[8,32,768]{2,1,0:T(8,128)(2,1)S(1)}, bf16[8,32,768]{2,1,0:T(8,128)(2,1)S(1)}, u32[]{:S(2)}, u32[]{:S(2)}) collective-permute-start(bf16[8,32,768]{2,1,0:T(8,128)(2,1)S(1)} %all-to-all-done.1.line_ref.refs_0_), channel_id=1, source_target_pairs={{0,320},{1,41},{2,322},{3,43},{4,324},{5,45},{6,326},{7,47},{8,328... | collective-permute-start | bytes 1179656 | tf_op jit(solution)/shard_map/ppermute | solution.py:144
  38.3 0.3 fusion.2
  38.6 0.3 fusion.3
  39.0 1.2 %pad_maximum_fusion = bf16[2,320,1024]{2,1,0:T(8,128)(2,1)} fusion(bf16[1,320,1024]{2,1,0:T(8,128)(2,1)S(1)} %fusion.3, bf16[1,320,1024]{2,1,0:T(8,128)(2,1)S(1)} %fusion.2), kind=kLoop, calls=%fused_computation.5 | loop fusion | flops 655360 | bytes 2621440 | tf_op jit(solution)/shard_map/stack | solution.py:164
  40.2 10.4 %all-to-all-start = ((bf16[16,40,1024]{2,1,0:T(8,128)(2,1)}), bf16[16,40,1024]{2,1,0:T(8,128)(2,1)}, u32[]{:S(2)}, u32[]{:S(2)}) async-start(bf16[16,40,1024]{2,1,0:T(8,128)(2,1)} %bitcast.3), calls=%async_computation | async-start | bytes 2621440 | tf_op jit(solution)/shard_map/all_to_all | solution.py:174
  50.6 0.0 collective-permute-done.1.behind_ref.refs_2_
  50.6 4.2 %collective-permute-done.ahead_ref.refs_1_ = bf16[8,32,768]{2,1,0:T(8,128)(2,1)S(1)} collective-permute-done((bf16[8,32,768]{2,1,0:T(8,128)(2,1)S(1)}, bf16[8,32,768]{2,1,0:T(8,128)(2,1)S(1)}, u32[]{:S(2)}, u32[]{:S(2)}) %collective-permute-start) | collective-permute-done | bytes 393248 | tf_op jit(solution)/shard_map/ppermute | solution.py:144
  54.8 1.2 %shard_map.68 = (bf16[20,32,768]{2,1,0:T(8,128)(2,1)}, bf16[20,32,768]{2,1,0:T(8,128)(2,1)S(1)}) custom-call(bf16[8,32,768]{2,1,0:T(8,128)(2,1)S(1)} %all-to-all-done.1.line_ref.refs_0_, bf16[8,32,768]{2,1,0:T(8,128)(2,1)S(1)} %collective-permute-done.ahead_ref.refs_1_, bf16[8,32,768]{2,1,0:T(8,128)(2,1)S(1)} %collective-permute-done.1.behind_ref.refs_2_), custom_call_target="tpu_custom_call" | custom-call | flops 199999995904 | bytes 4000000 | tf_op jit(solution)/shard_map/pallas_call | solution.py:147
  56.0 1.9 %collective-permute-start.2 = (bf16[20,32,768]{2,1,0:T(8,128)(2,1)}, bf16[20,32,768]{2,1,0:T(8,128)(2,1)S(1)}, u32[]{:S(2)}, u32[]{:S(2)}) collective-permute-start(bf16[20,32,768]{2,1,0:T(8,128)(2,1)} %get-tuple-element.6), channel_id=1, source_target_pairs={{0,64},{1,9},{2,66},{3,11},{4,68},{5,13},{6,70},{7,15},{8,72},{9,1... | collective-permute-start | bytes 2949128 | tf_op jit(solution)/shard_map/ppermute | solution.py:155
  57.9 4.6 %collective-permute-start.3 = (bf16[20,32,768]{2,1,0:T(8,128)(2,1)S(1)}, bf16[20,32,768]{2,1,0:T(8,128)(2,1)}, u32[]{:S(2)}, u32[]{:S(2)}) collective-permute-start(bf16[20,32,768]{2,1,0:T(8,128)(2,1)S(1)} %get-tuple-element.7), channel_id=1, source_target_pairs={{0,448},{1,57},{2,450},{3,59},{4,452},{5,61},{6,454},{7,63},{8,456... | collective-permute-start | bytes 2949128 | tf_op jit(solution)/shard_map/ppermute | solution.py:155
  62.5 19.9 %all-to-all-done = bf16[16,40,1024]{2,1,0:T(8,128)(2,1)} async-done(((bf16[16,40,1024]{2,1,0:T(8,128)(2,1)}), bf16[16,40,1024]{2,1,0:T(8,128)(2,1)}, u32[]{:S(2)}, u32[]{:S(2)}) %all-to-all-start) | async-done | bytes 1310752 | tf_op jit(solution)/shard_map/all_to_all | solution.py:174
  82.4 2.6 %fusion.1.rows_ref = bf16[640,1024]{1,0:T(8,128)(2,1)S(1)} fusion(bf16[640,1024]{1,0:T(8,128)(2,1)} %bitcast.4, s32[640]{0:T(1024)S(1)} %fusion.26), kind=kOutput, calls=%fused_computation.2 | convolution fusion | flops 839925760 | bytes 2624000 | tf_op jit(solution)/shard_map/dot_general | solution.py:179
  85.0 0.0 copy-start.6
  85.0 0.0 copy-start.8
  85.0 0.0 copy-start
  85.0 0.0 copy-start.1
  85.0 0.0 collective-permute-done.2.refs_3_
  85.0 4.6 %shard_map.69 = bf16[640,384]{1,0:T(8,128)(2,1)} custom-call(bf16[640,1024]{1,0:T(8,128)(2,1)S(1)} %fusion.1.rows_ref, bf16[8,32,768]{2,1,0:T(8,128)(2,1)S(1)} %all-to-all-done.1.line_ref.refs_0_, bf16[8,32,768]{2,1,0:T(8,128)(2,1)S(1)} %copy-done.3, bf16[8,32,768]{2,1,0:T(8,128)(2,1)S(1)} %collective-permute-done.1.behind_ref.refs_2_, ...), custom_call_target="tpu_custom_call" | custom-call | flops 2000000000 | bytes 10000000 | tf_op jit(solution)/shard_map/pallas_call | solution.py:180
  89.6 5.5 %all-to-all-start.2 = ((bf16[16,40,384]{2,1,0:T(8,128)(2,1)}), bf16[16,40,384]{2,1,0:T(8,128)(2,1)S(1)}, u32[]{:S(2)}, u32[]{:S(2)}) async-start(bf16[16,40,384]{2,1,0:T(8,128)(2,1)} %bitcast.6), calls=%async_computation.2 | async-start | bytes 983040 | tf_op jit(solution)/shard_map/all_to_all | solution.py:189
  95.1 16.6 %all-to-all-done.2 = bf16[16,40,384]{2,1,0:T(8,128)(2,1)S(1)} async-done(((bf16[16,40,384]{2,1,0:T(8,128)(2,1)}), bf16[16,40,384]{2,1,0:T(8,128)(2,1)S(1)}, u32[]{:S(2)}, u32[]{:S(2)}) %all-to-all-start.2) | async-done | bytes 491552 | tf_op jit(solution)/shard_map/all_to_all | solution.py:189
  111.7 1.4 %shard_map.70 = (bf16[128,1536]{1,0:T(8,128)(2,1)}, bf16[1,128]{1,0:T(2,128)(2,1)}) custom-call(bf16[640,384]{1,0:T(8,128)(2,1)S(1)} %bitcast.21, bf16[128,1536]{1,0:T(8,128)(2,1)S(1)} %bitcast.22, bf16[1,128]{1,0:T(2,128)(2,1)S(1)} %bitcast.23, s32[1,128]{1,0:T(1,128)S(1)} %bitcast_add_fusion.first_ref), custom_call_target="tpu_custom_call" | custom-call | flops 200000000 | bytes 2000000 | tf_op jit(solution)/shard_map/pallas_call | solution.py:193
  (16 shorter events, 0.1 us)
Async XLA Ops:
  0.6 10.7 %copy-start.5 = (s32[128,1]{0,1:T(1,128)S(1)}, s32[128,1]{0,1:T(1,128)}, u32[]{:S(2)}) copy-start(s32[128,1]{0,1:T(1,128)} %param.8) | copy-start | bytes 1540
  0.6 11.4 %copy-start.4 = (bf16[128,4096]{1,0:T(8,128)(2,1)S(1)}, bf16[128,4096]{1,0:T(8,128)(2,1)}, u32[]{:S(2)}) copy-start(bf16[128,4096]{1,0:T(8,128)(2,1)} %param.5) | copy-start | bytes 3145732
  2.3 18.8 %all-to-all-start.1 = ((bf16[8,32,768]{2,1,0:T(8,128)(2,1)}), bf16[8,32,768]{2,1,0:T(8,128)(2,1)S(1)}, u32[]{:S(2)}, u32[]{:S(2)}) async-start(bf16[8,32,768]{2,1,0:T(8,128)(2,1)} %broadcast_in_dim.5), calls=%async_computation.1 | async-start | bytes 786432 | tf_op jit(solution)/shard_map/all_to_all | solution.py:136
  11.5 0.5 copy-start.7
  21.2 29.4 %collective-permute-start.1 = (bf16[8,32,768]{2,1,0:T(8,128)(2,1)S(1)}, bf16[8,32,768]{2,1,0:T(8,128)(2,1)S(1)}, u32[]{:S(2)}, u32[]{:S(2)}) collective-permute-start(bf16[8,32,768]{2,1,0:T(8,128)(2,1)S(1)} %all-to-all-done.1.line_ref.refs_0_), channel_id=1, source_target_pairs={{0,192},{1,25},{2,194},{3,27},{4,196},{5,29},{6,198},{7,31},{8,200... | collective-permute-start | bytes 1179656 | tf_op jit(solution)/shard_map/ppermute | solution.py:145
  31.5 23.3 %collective-permute-start = (bf16[8,32,768]{2,1,0:T(8,128)(2,1)S(1)}, bf16[8,32,768]{2,1,0:T(8,128)(2,1)S(1)}, u32[]{:S(2)}, u32[]{:S(2)}) collective-permute-start(bf16[8,32,768]{2,1,0:T(8,128)(2,1)S(1)} %all-to-all-done.1.line_ref.refs_0_), channel_id=1, source_target_pairs={{0,320},{1,41},{2,322},{3,43},{4,324},{5,45},{6,326},{7,47},{8,328... | collective-permute-start | bytes 1179656 | tf_op jit(solution)/shard_map/ppermute | solution.py:144
  40.2 42.2 %all-to-all-start = ((bf16[16,40,1024]{2,1,0:T(8,128)(2,1)}), bf16[16,40,1024]{2,1,0:T(8,128)(2,1)}, u32[]{:S(2)}, u32[]{:S(2)}) async-start(bf16[16,40,1024]{2,1,0:T(8,128)(2,1)} %bitcast.3), calls=%async_computation | async-start | bytes 2621440 | tf_op jit(solution)/shard_map/all_to_all | solution.py:174
  54.8 1.2 %copy-start.2 = (bf16[8,32,768]{2,1,0:T(8,128)(2,1)}, bf16[8,32,768]{2,1,0:T(8,128)(2,1)S(1)}, u32[]{:S(2)}) copy-start(bf16[8,32,768]{2,1,0:T(8,128)(2,1)S(1)} %collective-permute-done.ahead_ref.refs_1_) | copy-start | bytes 1179652
  56.0 29.0 %collective-permute-start.2 = (bf16[20,32,768]{2,1,0:T(8,128)(2,1)}, bf16[20,32,768]{2,1,0:T(8,128)(2,1)S(1)}, u32[]{:S(2)}, u32[]{:S(2)}) collective-permute-start(bf16[20,32,768]{2,1,0:T(8,128)(2,1)} %get-tuple-element.6), channel_id=1, source_target_pairs={{0,64},{1,9},{2,66},{3,11},{4,68},{5,13},{6,70},{7,15},{8,72},{9,1... | collective-permute-start | bytes 2949128 | tf_op jit(solution)/shard_map/ppermute | solution.py:155
  57.9 27.1 %collective-permute-start.3 = (bf16[20,32,768]{2,1,0:T(8,128)(2,1)S(1)}, bf16[20,32,768]{2,1,0:T(8,128)(2,1)}, u32[]{:S(2)}, u32[]{:S(2)}) collective-permute-start(bf16[20,32,768]{2,1,0:T(8,128)(2,1)S(1)} %get-tuple-element.7), channel_id=1, source_target_pairs={{0,448},{1,57},{2,450},{3,59},{4,452},{5,61},{6,454},{7,63},{8,456... | collective-permute-start | bytes 2949128 | tf_op jit(solution)/shard_map/ppermute | solution.py:155
  82.4 2.7 %copy-start.3 = (bf16[8,32,768]{2,1,0:T(8,128)(2,1)S(1)}, bf16[8,32,768]{2,1,0:T(8,128)(2,1)}, u32[]{:S(2)}) copy-start(bf16[8,32,768]{2,1,0:T(8,128)(2,1)} %copy-done.2) | copy-start | bytes 1179652
  85.0 10.1 %copy-start.6 = (s32[128,1]{0,1:T(1,128)S(1)}, s32[128,1]{0,1:T(1,128)}, u32[]{:S(2)}) copy-start(s32[128,1]{0,1:T(1,128)} %param.8) | copy-start | bytes 1540
  85.0 10.1 %copy-start.8 = (s32[128]{0:T(128)S(1)}, s32[128]{0:T(128)}, u32[]{:S(2)}) copy-start(s32[128]{0:T(128)} %copy-done.7) | copy-start | bytes 1540
  85.0 26.7 %copy-start = (bf16[128,1,1536]{2,0,1:T(8,128)(2,1)S(1)}, bf16[128,1,1536]{2,0,1:T(8,128)(2,1)}, u32[]{:S(2)}) copy-start(bf16[128,1,1536]{2,0,1:T(8,128)(2,1)} %param.6) | copy-start | bytes 1179652
  85.0 26.7 %copy-start.1 = (bf16[128,1]{0,1:T(2,128)(2,1)S(1)}, bf16[128,1]{0,1:T(2,128)(2,1)}, u32[]{:S(2)}) copy-start(bf16[128,1]{0,1:T(2,128)(2,1)} %param.7) | copy-start | bytes 772
  89.6 22.1 %all-to-all-start.2 = ((bf16[16,40,384]{2,1,0:T(8,128)(2,1)}), bf16[16,40,384]{2,1,0:T(8,128)(2,1)S(1)}, u32[]{:S(2)}, u32[]{:S(2)}) async-start(bf16[16,40,384]{2,1,0:T(8,128)(2,1)} %bitcast.6), calls=%async_computation.2 | async-start | bytes 983040 | tf_op jit(solution)/shard_map/all_to_all | solution.py:189

commit v10 on v9

--- a/solution.py
+++ b/solution.py
@@ -58,7 +58,7 @@
 ARRAYS = 5
 
 
-def product(rows_ref, *refs):
+def product(got_ref, *refs):
     parts, out_ref, weight_ref = refs[:ARRAYS], refs[ARRAYS], refs[ARRAYS + 1]
     y, z, core = lax.axis_index("y"), lax.axis_index("z"), lax.axis_index("core")
     mine = jnp.where(core == 0, y, z)
@@ -69,22 +69,26 @@
         for i in range(blocks):
             weight_ref[source * outer + (at + i) * inner] = parts[which][first + i]
 
+    def order(shape, axis):
+        i = lax.broadcasted_iota(jnp.int32, shape, axis)
+        piece = (i >= COUNT // 2).astype(jnp.int32)
+        j = i - piece * (COUNT // 2)
+        source = (j * 3277) >> 16
+        return source * (2 * CAP) + piece * CAP + j - source * CAP
+
+    take = (lax.broadcasted_iota(jnp.int32, (COUNT, COUNT), 1) == order((COUNT, 1), 0)).astype(jnp.bfloat16)
+    rows = jnp.dot(take, got_ref[...], preferred_element_type=jnp.float32).astype(jnp.bfloat16)
     half = RING * RING // 2
     width = weight_ref.shape[1] * half
     back = jnp.dot(
-        rows_ref[: COUNT // 2], weight_ref[:half].reshape(width, FFW), preferred_element_type=jnp.float32
+        rows[: COUNT // 2], weight_ref[:half].reshape(width, FFW), preferred_element_type=jnp.float32
     ) + jnp.dot(
-        rows_ref[COUNT // 2 :], weight_ref[half:].reshape(width, FFW), preferred_element_type=jnp.float32
+        rows[COUNT // 2 :], weight_ref[half:].reshape(width, FFW), preferred_element_type=jnp.float32
     )
     back = back.astype(jnp.bfloat16)
     back = jnp.concatenate([back[:, : FFW // 2], back[:, FFW // 2 :]], axis=0)
 
-    i = lax.broadcasted_iota(jnp.int32, (1, COUNT), 1)
-    piece = (i >= COUNT // 2).astype(jnp.int32)
-    j = i - piece * (COUNT // 2)
-    source = (j * 3277) >> 16
-    order = source * (2 * CAP) + piece * CAP + j - source * CAP
-    give = (lax.broadcasted_iota(jnp.int32, (COUNT, COUNT), 0) == order).astype(jnp.bfloat16)
+    give = (lax.broadcasted_iota(jnp.int32, (COUNT, COUNT), 0) == order((1, COUNT), 1)).astype(jnp.bfloat16)
     out_ref[...] = jnp.dot(give, back, preferred_element_type=jnp.float32).astype(jnp.bfloat16)
 
 
@@ -141,18 +145,6 @@
         axis_index_groups=first_groups(),
         tiled=True,
     )
-    ahead = lax.ppermute(line, TORUS, second_shift(-3))
-    behind = lax.ppermute(line, TORUS, second_shift(3))
-    passed = jax.ShapeDtypeStruct((2 * RING + HALF_RING,) + own.shape, jnp.bfloat16)
-    up, down = pl.pallas_call(
-        join,
-        out_shape=(passed, passed),
-        in_specs=[pl.BlockSpec(memory_space=pltpu.VMEM)] * 3,
-        out_specs=(pl.BlockSpec(memory_space=pltpu.VMEM),) * 2,
-        compiler_params=pltpu.CompilerParams(vmem_limit_bytes=16 * 2**20),
-        cost_estimate=pl.CostEstimate(flops=2 * 10**11, bytes_accessed=4 * 10**6, transcendentals=0),
-    )(line, ahead, behind)
-    parts = [line, ahead, behind, lax.ppermute(up, TORUS, second_shift(1)), lax.ppermute(down, TORUS, second_shift(-1))]
 
     flat_routes = routes.reshape(tokens)
     member = (flat_routes[:, None] == jnp.arange(EXPERTS, dtype=jnp.int32)[None, :]).astype(jnp.int32)
@@ -171,12 +163,21 @@
             for h in range(2)
         ]
     ).reshape(PEERS, 2 * CAP, QUART)
+    line, sent = lax.optimization_barrier((line, sent))
+    ahead = lax.ppermute(line, TORUS, second_shift(-3))
+    behind = lax.ppermute(line, TORUS, second_shift(3))
+    passed = jax.ShapeDtypeStruct((2 * RING + HALF_RING,) + own.shape, jnp.bfloat16)
+    up, down = pl.pallas_call(
+        join,
+        out_shape=(passed, passed),
+        in_specs=[pl.BlockSpec(memory_space=pltpu.VMEM)] * 3,
+        out_specs=(pl.BlockSpec(memory_space=pltpu.VMEM),) * 2,
+        compiler_params=pltpu.CompilerParams(vmem_limit_bytes=16 * 2**20),
+        cost_estimate=pl.CostEstimate(flops=2 * 10**11, bytes_accessed=4 * 10**6, transcendentals=0),
+    )(line, ahead, behind)
+    parts = [line, ahead, behind, lax.ppermute(up, TORUS, second_shift(1)), lax.ppermute(down, TORUS, second_shift(-1))]
     got = lax.all_to_all(sent, SHARE, split_axis=0, concat_axis=0, tiled=True)
 
-    order = jnp.arange(COUNT, dtype=jnp.int32)
-    order = (order % (COUNT // 2)) // CAP * (2 * CAP) + order // (COUNT // 2) * CAP + order % CAP
-    take = (order[:, None] == jnp.arange(COUNT, dtype=jnp.int32)[None, :]).astype(jnp.bfloat16)
-    rows = jnp.dot(take, got.reshape(COUNT, QUART), preferred_element_type=jnp.float32).astype(jnp.bfloat16)
     back = pl.pallas_call(
         product,
         out_shape=jax.ShapeDtypeStruct((COUNT, FFW // 2), jnp.bfloat16),
@@ -185,7 +186,7 @@
         scratch_shapes=[pltpu.VMEM((RING * RING,) + own.shape, jnp.bfloat16)],
         compiler_params=pltpu.CompilerParams(vmem_limit_bytes=20 * 2**20),
         cost_estimate=pl.CostEstimate(flops=2 * 10**9, bytes_accessed=10**7, transcendentals=0),
-    )(rows, *parts)
+    )(got.reshape(COUNT, QUART), *parts)
     came = lax.all_to_all(
         back.reshape(PEERS, 2 * CAP, FFW // 2), SHARE, split_axis=0, concat_axis=0, tiled=True
     ).reshape(COUNT, FFW // 2)

time: 114 us -> 112 us (0.982)
  matrix products: 3.27 us -> 0.69 us
    all_to_all x1, waiting for transfers between devices: 19.9 us -> 6.22 us  [body(): got = lax.all_to_all(sent, SHARE, split_axis=0, concat_axis=0, tiled=True)]
    ppermute x1, waiting for transfers between devices: 0.01 us -> 9.94 us  [body(): lax.ppermute(up, TORUS, second_shift(1))]
    dot_general x1 -> x0, matrix products: 2.59 us -> none  [body(): jnp.dot(take, got.reshape(COUNT, QUART), preferred_element_type=jnp.float32)]
    ppermute x1, waiting for transfers between devices: 4.22 us -> 6.5 us  [body(): ahead = lax.ppermute(line, TORUS, second_shift(-3))]
    ppermute x1, waiting for transfers between devices: 0.01 us -> 1.85 us  [body(): lax.ppermute(down, TORUS, second_shift(-1))]
    all_to_all x1, waiting for transfers between devices: 9.02 us -> 7.59 us  [body(): lax.all_to_all(jnp.broadcast_to(own[None], (RING,) + own.shape), TORUS, s...]
  transfers between devices with their start and end apart: 7 -> 7, of which waited for: 4 -> 6; matrix products, arithmetic and copies ran while one was open for 5% -> 3% of each run, Pallas kernels for 1% -> 0%
where the time goes in v10:
time: 112 us; the launch traced here: 111 us
  waiting for transfers between devices  48.7 us (43%)
  starting transfers between devices  47.9 us (43%)
  Pallas kernels  7.18 us (6%)
  local copies, waits for them, and re-layouts  3.41 us (3%)
  other arithmetic  2.29 us (2%)
    all_to_all x1, waiting for transfers between devices, body(): lax.all_to_all(back.reshape(PEERS, 2 * CAP, FFW // 2), SHARE, split_axis=...  16.6 us
    all_to_all x1, starting transfers between devices, body(): got = lax.all_to_all(sent, SHARE, split_axis=0, concat_axis=0, tiled=True)  10.4 us
    ppermute x1, starting transfers between devices, body(): behind = lax.ppermute(line, TORUS, second_shift(3))  10.3 us
    ppermute x1, waiting for transfers between devices, body(): lax.ppermute(up, TORUS, second_shift(1))  9.94 us
    all_to_all x1, starting transfers between devices, body(): lax.all_to_all(jnp.broadcast_to(own[None], (RING,) + own.shape), TORUS, s...  8.11 us
    all_to_all x1, waiting for transfers between devices, body(): lax.all_to_all(jnp.broadcast_to(own[None], (RING,) + own.shape), TORUS, s...  7.59 us
    ppermute x1, starting transfers between devices, body(): ahead = lax.ppermute(line, TORUS, second_shift(-3))  6.77 us
    ppermute x1, waiting for transfers between devices, body(): ahead = lax.ppermute(line, TORUS, second_shift(-3))  6.5 us
  transfers between devices with their start and end apart: 7, of which 6 were waited for; matrix products, arithmetic and copies ran while one was open for 3% of the time, Pallas kernels for 0%

profile of v10, /device:TPU:1, one launch (start us, length us, event | category | flops | bytes accessed | tf_op | source)
XLA Modules:
  0.0 110.9 jit_solution(18107507112132584230)
XLA Ops:
  0.6 0.0 copy-start.5
  0.6 0.0 copy-start.4
  0.7 1.7 %broadcast_in_dim.5 = bf16[8,32,768]{2,1,0:T(8,128)(2,1)} broadcast(bf16[32,768]{1,0:T(8,128)(2,1)} %bitcast.23), dimensions={1,2} | broadcast | bytes 442368 | tf_op jit(solution)/shard_map/broadcast_in_dim | solution.py:141
  2.3 8.1 %all-to-all-start = ((bf16[8,32,768]{2,1,0:T(8,128)(2,1)}), bf16[8,32,768]{2,1,0:T(8,128)(2,1)S(1)}, u32[]{:S(2)}, u32[]{:S(2)}) async-start(bf16[8,32,768]{2,1,0:T(8,128)(2,1)} %broadcast_in_dim.5), calls=%async_computation | async-start | bytes 786432 | tf_op jit(solution)/shard_map/all_to_all | solution.py:140
  10.4 0.7 fusion.10
  11.2 0.2 reduce_window_sum.11
  11.3 0.0 copy-done.5
  11.3 0.2 select_reduce_fusion
  11.5 0.0 copy-start.7
  11.6 0.1 fusion.13
  11.7 0.3 fusion
  12.0 0.0 copy-done.7
  12.0 0.3 fusion.1
  12.4 1.2 %pad_maximum_fusion = bf16[2,320,1024]{2,1,0:T(8,128)(2,1)} fusion(bf16[1,320,1024]{2,1,0:T(8,128)(2,1)S(1)} %fusion.1, bf16[1,320,1024]{2,1,0:T(8,128)(2,1)S(1)} %fusion), kind=kLoop, calls=%fused_computation.2 | loop fusion | flops 655360 | bytes 2621440 | tf_op jit(solution)/shard_map/stack | solution.py:156
  13.6 7.6 %all-to-all-done.line_ref.refs_0_ = bf16[8,32,768]{2,1,0:T(8,128)(2,1)S(1)} async-done(((bf16[8,32,768]{2,1,0:T(8,128)(2,1)}), bf16[8,32,768]{2,1,0:T(8,128)(2,1)S(1)}, u32[]{:S(2)}, u32[]{:S(2)}) %all-to-all-start) | async-done | bytes 393248 | tf_op jit(solution)/shard_map/all_to_all | solution.py:140
  21.2 10.3 %collective-permute-start.1 = (bf16[8,32,768]{2,1,0:T(8,128)(2,1)S(1)}, bf16[8,32,768]{2,1,0:T(8,128)(2,1)S(1)}, u32[]{:S(2)}, u32[]{:S(2)}) collective-permute-start(bf16[8,32,768]{2,1,0:T(8,128)(2,1)S(1)} %all-to-all-done.line_ref.refs_0_), channel_id=1, source_target_pairs={{0,192},{1,25},{2,194},{3,27},{4,196},{5,29},{6,198},{7,31},{8,200... | collective-permute-start | bytes 1179656 | tf_op jit(solution)/shard_map/ppermute | solution.py:168
  31.5 6.8 %collective-permute-start = (bf16[8,32,768]{2,1,0:T(8,128)(2,1)S(1)}, bf16[8,32,768]{2,1,0:T(8,128)(2,1)S(1)}, u32[]{:S(2)}, u32[]{:S(2)}) collective-permute-start(bf16[8,32,768]{2,1,0:T(8,128)(2,1)S(1)} %all-to-all-done.line_ref.refs_0_), channel_id=1, source_target_pairs={{0,320},{1,41},{2,322},{3,43},{4,324},{5,45},{6,326},{7,47},{8,328... | collective-permute-start | bytes 1179656 | tf_op jit(solution)/shard_map/ppermute | solution.py:167
  38.3 10.4 %all-to-all-start.1 = ((bf16[16,40,1024]{2,1,0:T(8,128)(2,1)}), bf16[16,40,1024]{2,1,0:T(8,128)(2,1)}, u32[]{:S(2)}, u32[]{:S(2)}) async-start(bf16[16,40,1024]{2,1,0:T(8,128)(2,1)} %bitcast.4), calls=%async_computation.1 | async-start | bytes 2621440 | tf_op jit(solution)/shard_map/all_to_all | solution.py:179
  48.7 0.0 collective-permute-done.1.behind_ref.refs_2_
  48.7 6.5 %collective-permute-done.ahead_ref.refs_1_ = bf16[8,32,768]{2,1,0:T(8,128)(2,1)S(1)} collective-permute-done((bf16[8,32,768]{2,1,0:T(8,128)(2,1)S(1)}, bf16[8,32,768]{2,1,0:T(8,128)(2,1)S(1)}, u32[]{:S(2)}, u32[]{:S(2)}) %collective-permute-start) | collective-permute-done | bytes 393248 | tf_op jit(solution)/shard_map/ppermute | solution.py:167
  55.2 0.1 shard_map.68
  55.4 0.6 copy-done.2
  56.0 1.9 %collective-permute-start.2 = (bf16[20,32,768]{2,1,0:T(8,128)(2,1)S(1)}, bf16[20,32,768]{2,1,0:T(8,128)(2,1)S(1)}, u32[]{:S(2)}, u32[]{:S(2)}) collective-permute-start(bf16[20,32,768]{2,1,0:T(8,128)(2,1)S(1)} %get-tuple-element.10), channel_id=1, source_target_pairs={{0,64},{1,9},{2,66},{3,11},{4,68},{5,13},{6,70},{7,15},{8,72},{9,1... | collective-permute-start | bytes 2949128 | tf_op jit(solution)/shard_map/ppermute | solution.py:178
  57.9 4.6 %collective-permute-start.3 = (bf16[20,32,768]{2,1,0:T(8,128)(2,1)S(1)}, bf16[20,32,768]{2,1,0:T(8,128)(2,1)S(1)}, u32[]{:S(2)}, u32[]{:S(2)}) collective-permute-start(bf16[20,32,768]{2,1,0:T(8,128)(2,1)S(1)} %get-tuple-element.11), channel_id=1, source_target_pairs={{0,448},{1,57},{2,450},{3,59},{4,452},{5,61},{6,454},{7,63},{8,456... | collective-permute-start | bytes 2949128 | tf_op jit(solution)/shard_map/ppermute | solution.py:178
  62.5 9.9 %collective-permute-done.2.refs_3_ = bf16[20,32,768]{2,1,0:T(8,128)(2,1)S(1)} collective-permute-done((bf16[20,32,768]{2,1,0:T(8,128)(2,1)S(1)}, bf16[20,32,768]{2,1,0:T(8,128)(2,1)S(1)}, u32[]{:S(2)}, u32[]{:S(2)}) %collective-permute-start.2) | collective-permute-done | bytes 983072 | tf_op jit(solution)/shard_map/ppermute | solution.py:178
  72.4 1.9 %collective-permute-done.3.refs_4_ = bf16[20,32,768]{2,1,0:T(8,128)(2,1)S(1)} collective-permute-done((bf16[20,32,768]{2,1,0:T(8,128)(2,1)S(1)}, bf16[20,32,768]{2,1,0:T(8,128)(2,1)S(1)}, u32[]{:S(2)}, u32[]{:S(2)}) %collective-permute-start.3) | collective-permute-done | bytes 983072 | tf_op jit(solution)/shard_map/ppermute | solution.py:178
  74.3 6.2 %all-to-all-done.1 = bf16[16,40,1024]{2,1,0:T(8,128)(2,1)} async-done(((bf16[16,40,1024]{2,1,0:T(8,128)(2,1)}), bf16[16,40,1024]{2,1,0:T(8,128)(2,1)}, u32[]{:S(2)}, u32[]{:S(2)}) %all-to-all-start.1) | async-done | bytes 1310752 | tf_op jit(solution)/shard_map/all_to_all | solution.py:179
  80.5 1.0 copy-done.3
  81.5 5.6 %shard_map.69 = bf16[640,384]{1,0:T(8,128)(2,1)} custom-call(bf16[640,1024]{1,0:T(8,128)(2,1)} %bitcast.5.got_ref, bf16[8,32,768]{2,1,0:T(8,128)(2,1)S(1)} %all-to-all-done.line_ref.refs_0_, bf16[8,32,768]{2,1,0:T(8,128)(2,1)S(1)} %copy-done.3, bf16[8,32,768]{2,1,0:T(8,128)(2,1)S(1)} %collective-permute-done.1.behind_ref.refs_2_, ...), custom_call_target="tpu_custom_call" | custom-call | flops 2000000000 | bytes 10000000 | tf_op jit(solution)/shard_map/pallas_call | solution.py:181
  87.1 5.7 %all-to-all-start.2 = ((bf16[16,40,384]{2,1,0:T(8,128)(2,1)}), bf16[16,40,384]{2,1,0:T(8,128)(2,1)S(1)}, u32[]{:S(2)}, u32[]{:S(2)}) async-start(bf16[16,40,384]{2,1,0:T(8,128)(2,1)} %bitcast.6), calls=%async_computation.2 | async-start | bytes 983040 | tf_op jit(solution)/shard_map/all_to_all | solution.py:190
  92.9 16.6 %all-to-all-done.2 = bf16[16,40,384]{2,1,0:T(8,128)(2,1)S(1)} async-done(((bf16[16,40,384]{2,1,0:T(8,128)(2,1)}), bf16[16,40,384]{2,1,0:T(8,128)(2,1)S(1)}, u32[]{:S(2)}, u32[]{:S(2)}) %all-to-all-start.2) | async-done | bytes 491552 | tf_op jit(solution)/shard_map/all_to_all | solution.py:190
  109.5 1.4 %shard_map.70 = (bf16[128,1536]{1,0:T(8,128)(2,1)}, bf16[1,128]{1,0:T(2,128)(2,1)}) custom-call(bf16[640,384]{1,0:T(8,128)(2,1)S(1)} %bitcast.20, bf16[128,1536]{1,0:T(8,128)(2,1)S(1)} %bitcast.21, bf16[1,128]{1,0:T(2,128)(2,1)S(1)} %bitcast.22, s32[1,128]{1,0:T(1,128)S(1)} %bitcast_add_fusion.first_ref), custom_call_target="tpu_custom_call" | custom-call | flops 200000000 | bytes 2000000 | tf_op jit(solution)/shard_map/pallas_call | solution.py:194
  (14 shorter events, 0.0 us)
Async XLA Ops:
  0.6 10.7 %copy-start.5 = (s32[128,1]{0,1:T(1,128)S(1)}, s32[128,1]{0,1:T(1,128)}, u32[]{:S(2)}) copy-start(s32[128,1]{0,1:T(1,128)} %param.8) | copy-start | bytes 1540
  0.6 10.9 %copy-start.4 = (bf16[128,4096]{1,0:T(8,128)(2,1)S(1)}, bf16[128,4096]{1,0:T(8,128)(2,1)}, u32[]{:S(2)}) copy-start(bf16[128,4096]{1,0:T(8,128)(2,1)} %param.5) | copy-start | bytes 3145732
  2.3 18.8 %all-to-all-start = ((bf16[8,32,768]{2,1,0:T(8,128)(2,1)}), bf16[8,32,768]{2,1,0:T(8,128)(2,1)S(1)}, u32[]{:S(2)}, u32[]{:S(2)}) async-start(bf16[8,32,768]{2,1,0:T(8,128)(2,1)} %broadcast_in_dim.5), calls=%async_computation | async-start | bytes 786432 | tf_op jit(solution)/shard_map/all_to_all | solution.py:140
  11.5 0.5 copy-start.7
  21.2 27.6 %collective-permute-start.1 = (bf16[8,32,768]{2,1,0:T(8,128)(2,1)S(1)}, bf16[8,32,768]{2,1,0:T(8,128)(2,1)S(1)}, u32[]{:S(2)}, u32[]{:S(2)}) collective-permute-start(bf16[8,32,768]{2,1,0:T(8,128)(2,1)S(1)} %all-to-all-done.line_ref.refs_0_), channel_id=1, source_target_pairs={{0,192},{1,25},{2,194},{3,27},{4,196},{5,29},{6,198},{7,31},{8,200... | collective-permute-start | bytes 1179656 | tf_op jit(solution)/shard_map/ppermute | solution.py:168
  31.5 23.7 %collective-permute-start = (bf16[8,32,768]{2,1,0:T(8,128)(2,1)S(1)}, bf16[8,32,768]{2,1,0:T(8,128)(2,1)S(1)}, u32[]{:S(2)}, u32[]{:S(2)}) collective-permute-start(bf16[8,32,768]{2,1,0:T(8,128)(2,1)S(1)} %all-to-all-done.line_ref.refs_0_), channel_id=1, source_target_pairs={{0,320},{1,41},{2,322},{3,43},{4,324},{5,45},{6,326},{7,47},{8,328... | collective-permute-start | bytes 1179656 | tf_op jit(solution)/shard_map/ppermute | solution.py:167
  38.3 42.2 %all-to-all-start.1 = ((bf16[16,40,1024]{2,1,0:T(8,128)(2,1)}), bf16[16,40,1024]{2,1,0:T(8,128)(2,1)}, u32[]{:S(2)}, u32[]{:S(2)}) async-start(bf16[16,40,1024]{2,1,0:T(8,128)(2,1)} %bitcast.4), calls=%async_computation.1 | async-start | bytes 2621440 | tf_op jit(solution)/shard_map/all_to_all | solution.py:179
  55.2 0.7 copy-start.2
  56.0 16.4 %collective-permute-start.2 = (bf16[20,32,768]{2,1,0:T(8,128)(2,1)S(1)}, bf16[20,32,768]{2,1,0:T(8,128)(2,1)S(1)}, u32[]{:S(2)}, u32[]{:S(2)}) collective-permute-start(bf16[20,32,768]{2,1,0:T(8,128)(2,1)S(1)} %get-tuple-element.10), channel_id=1, source_target_pairs={{0,64},{1,9},{2,66},{3,11},{4,68},{5,13},{6,70},{7,15},{8,72},{9,1... | collective-permute-start | bytes 2949128 | tf_op jit(solution)/shard_map/ppermute | solution.py:178
  57.9 16.4 %collective-permute-start.3 = (bf16[20,32,768]{2,1,0:T(8,128)(2,1)S(1)}, bf16[20,32,768]{2,1,0:T(8,128)(2,1)S(1)}, u32[]{:S(2)}, u32[]{:S(2)}) collective-permute-start(bf16[20,32,768]{2,1,0:T(8,128)(2,1)S(1)} %get-tuple-element.11), channel_id=1, source_target_pairs={{0,448},{1,57},{2,450},{3,59},{4,452},{5,61},{6,454},{7,63},{8,456... | collective-permute-start | bytes 2949128 | tf_op jit(solution)/shard_map/ppermute | solution.py:178
  80.5 1.0 copy-start.3
  81.5 11.4 %copy-start.6 = (s32[128,1]{0,1:T(1,128)S(1)}, s32[128,1]{0,1:T(1,128)}, u32[]{:S(2)}) copy-start(s32[128,1]{0,1:T(1,128)} %param.8) | copy-start | bytes 1540
  81.5 11.4 %copy-start.8 = (s32[128]{0:T(128)S(1)}, s32[128]{0:T(128)}, u32[]{:S(2)}) copy-start(s32[128]{0:T(128)} %copy-done.7) | copy-start | bytes 1540
  81.5 28.0 %copy-start = (bf16[128,1,1536]{2,0,1:T(8,128)(2,1)S(1)}, bf16[128,1,1536]{2,0,1:T(8,128)(2,1)}, u32[]{:S(2)}) copy-start(bf16[128,1,1536]{2,0,1:T(8,128)(2,1)} %param.6) | copy-start | bytes 1179652
  81.5 28.0 %copy-start.1 = (bf16[128,1]{0,1:T(2,128)(2,1)S(1)}, bf16[128,1]{0,1:T(2,128)(2,1)}, u32[]{:S(2)}) copy-start(bf16[128,1]{0,1:T(2,128)(2,1)} %param.7) | copy-start | bytes 772
  87.1 22.4 %all-to-all-start.2 = ((bf16[16,40,384]{2,1,0:T(8,128)(2,1)}), bf16[16,40,384]{2,1,0:T(8,128)(2,1)S(1)}, u32[]{:S(2)}, u32[]{:S(2)}) async-start(bf16[16,40,384]{2,1,0:T(8,128)(2,1)} %bitcast.6), calls=%async_computation.2 | async-start | bytes 983040 | tf_op jit(solution)/shard_map/all_to_all | solution.py:190

commit v11 on v10

--- a/solution.py
+++ b/solution.py
@@ -59,7 +59,9 @@
 
 
 def product(got_ref, *refs):
-    parts, out_ref, weight_ref = refs[:ARRAYS], refs[ARRAYS], refs[ARRAYS + 1]
+    parts, out_ref, weight_ref, held_ref, rows_ref, sem = refs[:ARRAYS], refs[ARRAYS], *refs[ARRAYS + 1 :]
+    fetch = pltpu.make_async_copy(got_ref, held_ref, sem)
+    fetch.start()
     y, z, core = lax.axis_index("y"), lax.axis_index("z"), lax.axis_index("core")
     mine = jnp.where(core == 0, y, z)
     outer = jnp.where(core == 0, RING, 1)
@@ -77,13 +79,18 @@
         return source * (2 * CAP) + piece * CAP + j - source * CAP
 
     take = (lax.broadcasted_iota(jnp.int32, (COUNT, COUNT), 1) == order((COUNT, 1), 0)).astype(jnp.bfloat16)
-    rows = jnp.dot(take, got_ref[...], preferred_element_type=jnp.float32).astype(jnp.bfloat16)
+    fetch.wait()
+    tile = QUART // 4
+    for k in range(4):
+        rows_ref[:, k * tile : (k + 1) * tile] = jnp.dot(
+            take, held_ref[:, k * tile : (k + 1) * tile], preferred_element_type=jnp.float32
+        ).astype(jnp.bfloat16)
     half = RING * RING // 2
     width = weight_ref.shape[1] * half
     back = jnp.dot(
-        rows[: COUNT // 2], weight_ref[:half].reshape(width, FFW), preferred_element_type=jnp.float32
+        rows_ref[: COUNT // 2], weight_ref[:half].reshape(width, FFW), preferred_element_type=jnp.float32
     ) + jnp.dot(
-        rows[COUNT // 2 :], weight_ref[half:].reshape(width, FFW), preferred_element_type=jnp.float32
+        rows_ref[COUNT // 2 :], weight_ref[half:].reshape(width, FFW), preferred_element_type=jnp.float32
     )
     back = back.astype(jnp.bfloat16)
     back = jnp.concatenate([back[:, : FFW // 2], back[:, FFW // 2 :]], axis=0)
@@ -181,9 +188,14 @@
     back = pl.pallas_call(
         product,
         out_shape=jax.ShapeDtypeStruct((COUNT, FFW // 2), jnp.bfloat16),
-        in_specs=[pl.BlockSpec(memory_space=pltpu.VMEM)] * (ARRAYS + 1),
+        in_specs=[pl.BlockSpec(memory_space=pl.ANY)] + [pl.BlockSpec(memory_space=pltpu.VMEM)] * ARRAYS,
         out_specs=pl.BlockSpec(memory_space=pltpu.VMEM),
-        scratch_shapes=[pltpu.VMEM((RING * RING,) + own.shape, jnp.bfloat16)],
+        scratch_shapes=[
+            pltpu.VMEM((RING * RING,) + own.shape, jnp.bfloat16),
+            pltpu.VMEM((COUNT, QUART), jnp.bfloat16),
+            pltpu.VMEM((COUNT, QUART), jnp.bfloat16),
+            pltpu.SemaphoreType.DMA,
+        ],
         compiler_params=pltpu.CompilerParams(vmem_limit_bytes=20 * 2**20),
         cost_estimate=pl.CostEstimate(flops=2 * 10**9, bytes_accessed=10**7, transcendentals=0),
     )(got.reshape(COUNT, QUART), *parts)

time: 112 us -> 112 us (level)
  no operation moved by 1% of the time
where the time goes in v11:
time: 112 us; the launch traced here: 111 us
  waiting for transfers between devices  48.7 us (43%)
  starting transfers between devices  47.9 us (43%)
  Pallas kernels  7.14 us (6%)
  local copies, waits for them, and re-layouts  3.41 us (3%)
  other arithmetic  2.29 us (2%)
    all_to_all x1, waiting for transfers between devices, body(): lax.all_to_all(back.reshape(PEERS, 2 * CAP, FFW // 2), SHARE, split_axis=...  16.6 us
    all_to_all x1, starting transfers between devices, body(): got = lax.all_to_all(sent, SHARE, split_axis=0, concat_axis=0, tiled=True)  10.4 us
    ppermute x1, starting transfers between devices, body(): behind = lax.ppermute(line, TORUS, second_shift(3))  10.3 us
    ppermute x1, waiting for transfers between devices, body(): lax.ppermute(up, TORUS, second_shift(1))  9.94 us
    all_to_all x1, starting transfers between devices, body(): lax.all_to_all(jnp.broadcast_to(own[None], (RING,) + own.shape), TORUS, s...  8.11 us
    all_to_all x1, waiting for transfers between devices, body(): lax.all_to_all(jnp.broadcast_to(own[None], (RING,) + own.shape), TORUS, s...  7.59 us
    ppermute x1, starting transfers between devices, body(): ahead = lax.ppermute(line, TORUS, second_shift(-3))  6.77 us
    ppermute x1, waiting for transfers between devices, body(): ahead = lax.ppermute(line, TORUS, second_shift(-3))  6.5 us
  transfers between devices with their start and end apart: 7, of which 6 were waited for; matrix products, arithmetic and copies ran while one was open for 3% of the time, Pallas kernels for 0%

profile of v11, /device:TPU:1, one launch (start us, length us, event | category | flops | bytes accessed | tf_op | source)
XLA Modules:
  0.0 110.9 jit_solution(2781778906848697455)
XLA Ops:
  0.6 0.0 copy-start.5
  0.6 0.0 copy-start.4
  0.7 1.7 %broadcast_in_dim.5 = bf16[8,32,768]{2,1,0:T(8,128)(2,1)} broadcast(bf16[32,768]{1,0:T(8,128)(2,1)} %bitcast.23), dimensions={1,2} | broadcast | bytes 442368 | tf_op jit(solution)/shard_map/broadcast_in_dim | solution.py:148
  2.3 8.1 %all-to-all-start = ((bf16[8,32,768]{2,1,0:T(8,128)(2,1)}), bf16[8,32,768]{2,1,0:T(8,128)(2,1)S(1)}, u32[]{:S(2)}, u32[]{:S(2)}) async-start(bf16[8,32,768]{2,1,0:T(8,128)(2,1)} %broadcast_in_dim.5), calls=%async_computation | async-start | bytes 786432 | tf_op jit(solution)/shard_map/all_to_all | solution.py:147
  10.4 0.7 fusion.10
  11.2 0.2 reduce_window_sum.11
  11.3 0.2 select_reduce_fusion
  11.5 0.0 copy-start.7
  11.6 0.0 copy-done.4
  11.6 0.1 fusion.13
  11.7 0.3 fusion
  12.0 0.0 copy-done.7
  12.0 0.3 fusion.1
  12.4 1.2 %pad_maximum_fusion = bf16[2,320,1024]{2,1,0:T(8,128)(2,1)} fusion(bf16[1,320,1024]{2,1,0:T(8,128)(2,1)S(1)} %fusion.1, bf16[1,320,1024]{2,1,0:T(8,128)(2,1)S(1)} %fusion), kind=kLoop, calls=%fused_computation.2 | loop fusion | flops 655360 | bytes 2621440 | tf_op jit(solution)/shard_map/stack | solution.py:163
  13.6 7.6 %all-to-all-done.line_ref.refs_0_ = bf16[8,32,768]{2,1,0:T(8,128)(2,1)S(1)} async-done(((bf16[8,32,768]{2,1,0:T(8,128)(2,1)}), bf16[8,32,768]{2,1,0:T(8,128)(2,1)S(1)}, u32[]{:S(2)}, u32[]{:S(2)}) %all-to-all-start) | async-done | bytes 393248 | tf_op jit(solution)/shard_map/all_to_all | solution.py:147
  21.2 10.3 %collective-permute-start.1 = (bf16[8,32,768]{2,1,0:T(8,128)(2,1)S(1)}, bf16[8,32,768]{2,1,0:T(8,128)(2,1)S(1)}, u32[]{:S(2)}, u32[]{:S(2)}) collective-permute-start(bf16[8,32,768]{2,1,0:T(8,128)(2,1)S(1)} %all-to-all-done.line_ref.refs_0_), channel_id=1, source_target_pairs={{0,192},{1,25},{2,194},{3,27},{4,196},{5,29},{6,198},{7,31},{8,200... | collective-permute-start | bytes 1179656 | tf_op jit(solution)/shard_map/ppermute | solution.py:175
  31.5 6.8 %collective-permute-start = (bf16[8,32,768]{2,1,0:T(8,128)(2,1)S(1)}, bf16[8,32,768]{2,1,0:T(8,128)(2,1)S(1)}, u32[]{:S(2)}, u32[]{:S(2)}) collective-permute-start(bf16[8,32,768]{2,1,0:T(8,128)(2,1)S(1)} %all-to-all-done.line_ref.refs_0_), channel_id=1, source_target_pairs={{0,320},{1,41},{2,322},{3,43},{4,324},{5,45},{6,326},{7,47},{8,328... | collective-permute-start | bytes 1179656 | tf_op jit(solution)/shard_map/ppermute | solution.py:174
  38.3 10.4 %all-to-all-start.1 = ((bf16[16,40,1024]{2,1,0:T(8,128)(2,1)}), bf16[16,40,1024]{2,1,0:T(8,128)(2,1)}, u32[]{:S(2)}, u32[]{:S(2)}) async-start(bf16[16,40,1024]{2,1,0:T(8,128)(2,1)} %bitcast.4), calls=%async_computation.1 | async-start | bytes 2621440 | tf_op jit(solution)/shard_map/all_to_all | solution.py:186
  48.7 0.0 collective-permute-done.1.behind_ref.refs_2_
  48.7 6.5 %collective-permute-done.ahead_ref.refs_1_ = bf16[8,32,768]{2,1,0:T(8,128)(2,1)S(1)} collective-permute-done((bf16[8,32,768]{2,1,0:T(8,128)(2,1)S(1)}, bf16[8,32,768]{2,1,0:T(8,128)(2,1)S(1)}, u32[]{:S(2)}, u32[]{:S(2)}) %collective-permute-start) | collective-permute-done | bytes 393248 | tf_op jit(solution)/shard_map/ppermute | solution.py:174
  55.2 0.1 shard_map.68
  55.4 0.6 copy-done.2
  56.0 1.9 %collective-permute-start.2 = (bf16[20,32,768]{2,1,0:T(8,128)(2,1)S(1)}, bf16[20,32,768]{2,1,0:T(8,128)(2,1)S(1)}, u32[]{:S(2)}, u32[]{:S(2)}) collective-permute-start(bf16[20,32,768]{2,1,0:T(8,128)(2,1)S(1)} %get-tuple-element.10), channel_id=1, source_target_pairs={{0,64},{1,9},{2,66},{3,11},{4,68},{5,13},{6,70},{7,15},{8,72},{9,1... | collective-permute-start | bytes 2949128 | tf_op jit(solution)/shard_map/ppermute | solution.py:185
  57.9 4.6 %collective-permute-start.3 = (bf16[20,32,768]{2,1,0:T(8,128)(2,1)S(1)}, bf16[20,32,768]{2,1,0:T(8,128)(2,1)S(1)}, u32[]{:S(2)}, u32[]{:S(2)}) collective-permute-start(bf16[20,32,768]{2,1,0:T(8,128)(2,1)S(1)} %get-tuple-element.11), channel_id=1, source_target_pairs={{0,448},{1,57},{2,450},{3,59},{4,452},{5,61},{6,454},{7,63},{8,456... | collective-permute-start | bytes 2949128 | tf_op jit(solution)/shard_map/ppermute | solution.py:185
  62.5 9.9 %collective-permute-done.2.refs_3_ = bf16[20,32,768]{2,1,0:T(8,128)(2,1)S(1)} collective-permute-done((bf16[20,32,768]{2,1,0:T(8,128)(2,1)S(1)}, bf16[20,32,768]{2,1,0:T(8,128)(2,1)S(1)}, u32[]{:S(2)}, u32[]{:S(2)}) %collective-permute-start.2) | collective-permute-done | bytes 983072 | tf_op jit(solution)/shard_map/ppermute | solution.py:185
  72.4 1.9 %collective-permute-done.3.refs_4_ = bf16[20,32,768]{2,1,0:T(8,128)(2,1)S(1)} collective-permute-done((bf16[20,32,768]{2,1,0:T(8,128)(2,1)S(1)}, bf16[20,32,768]{2,1,0:T(8,128)(2,1)S(1)}, u32[]{:S(2)}, u32[]{:S(2)}) %collective-permute-start.3) | collective-permute-done | bytes 983072 | tf_op jit(solution)/shard_map/ppermute | solution.py:185
  74.3 6.2 %all-to-all-done.1 = bf16[16,40,1024]{2,1,0:T(8,128)(2,1)} async-done(((bf16[16,40,1024]{2,1,0:T(8,128)(2,1)}), bf16[16,40,1024]{2,1,0:T(8,128)(2,1)}, u32[]{:S(2)}, u32[]{:S(2)}) %all-to-all-start.1) | async-done | bytes 1310752 | tf_op jit(solution)/shard_map/all_to_all | solution.py:186
  80.5 1.0 copy-done.3
  81.5 5.6 %shard_map.69 = bf16[640,384]{1,0:T(8,128)(2,1)} custom-call(bf16[640,1024]{1,0:T(8,128)(2,1)} %bitcast.5.got_ref, bf16[8,32,768]{2,1,0:T(8,128)(2,1)S(1)} %all-to-all-done.line_ref.refs_0_, bf16[8,32,768]{2,1,0:T(8,128)(2,1)S(1)} %copy-done.3, bf16[8,32,768]{2,1,0:T(8,128)(2,1)S(1)} %collective-permute-done.1.behind_ref.refs_2_, ...), custom_call_target="tpu_custom_call" | custom-call | flops 2000000000 | bytes 10000000 | tf_op jit(solution)/shard_map/pallas_call | solution.py:188
  87.1 5.8 %all-to-all-start.2 = ((bf16[16,40,384]{2,1,0:T(8,128)(2,1)}), bf16[16,40,384]{2,1,0:T(8,128)(2,1)S(1)}, u32[]{:S(2)}, u32[]{:S(2)}) async-start(bf16[16,40,384]{2,1,0:T(8,128)(2,1)} %bitcast.6), calls=%async_computation.2 | async-start | bytes 983040 | tf_op jit(solution)/shard_map/all_to_all | solution.py:202
  92.9 16.6 %all-to-all-done.2 = bf16[16,40,384]{2,1,0:T(8,128)(2,1)S(1)} async-done(((bf16[16,40,384]{2,1,0:T(8,128)(2,1)}), bf16[16,40,384]{2,1,0:T(8,128)(2,1)S(1)}, u32[]{:S(2)}, u32[]{:S(2)}) %all-to-all-start.2) | async-done | bytes 491552 | tf_op jit(solution)/shard_map/all_to_all | solution.py:202
  109.5 1.4 %shard_map.70 = (bf16[128,1536]{1,0:T(8,128)(2,1)}, bf16[1,128]{1,0:T(2,128)(2,1)}) custom-call(bf16[640,384]{1,0:T(8,128)(2,1)S(1)} %bitcast.20, bf16[128,1536]{1,0:T(8,128)(2,1)S(1)} %bitcast.21, bf16[1,128]{1,0:T(2,128)(2,1)S(1)} %bitcast.22, s32[1,128]{1,0:T(1,128)S(1)} %bitcast_add_fusion.first_ref), custom_call_target="tpu_custom_call" | custom-call | flops 200000000 | bytes 2000000 | tf_op jit(solution)/shard_map/pallas_call | solution.py:206
  (14 shorter events, 0.0 us)
Async XLA Ops:
  0.6 10.7 %copy-start.5 = (s32[128,1]{0,1:T(1,128)S(1)}, s32[128,1]{0,1:T(1,128)}, u32[]{:S(2)}) copy-start(s32[128,1]{0,1:T(1,128)} %param.8) | copy-start | bytes 1540
  0.6 10.9 %copy-start.4 = (bf16[128,4096]{1,0:T(8,128)(2,1)S(1)}, bf16[128,4096]{1,0:T(8,128)(2,1)}, u32[]{:S(2)}) copy-start(bf16[128,4096]{1,0:T(8,128)(2,1)} %param.5) | copy-start | bytes 3145732
  2.3 18.8 %all-to-all-start = ((bf16[8,32,768]{2,1,0:T(8,128)(2,1)}), bf16[8,32,768]{2,1,0:T(8,128)(2,1)S(1)}, u32[]{:S(2)}, u32[]{:S(2)}) async-start(bf16[8,32,768]{2,1,0:T(8,128)(2,1)} %broadcast_in_dim.5), calls=%async_computation | async-start | bytes 786432 | tf_op jit(solution)/shard_map/all_to_all | solution.py:147
  11.5 0.5 copy-start.7
  21.2 27.6 %collective-permute-start.1 = (bf16[8,32,768]{2,1,0:T(8,128)(2,1)S(1)}, bf16[8,32,768]{2,1,0:T(8,128)(2,1)S(1)}, u32[]{:S(2)}, u32[]{:S(2)}) collective-permute-start(bf16[8,32,768]{2,1,0:T(8,128)(2,1)S(1)} %all-to-all-done.line_ref.refs_0_), channel_id=1, source_target_pairs={{0,192},{1,25},{2,194},{3,27},{4,196},{5,29},{6,198},{7,31},{8,200... | collective-permute-start | bytes 1179656 | tf_op jit(solution)/shard_map/ppermute | solution.py:175
  31.5 23.7 %collective-permute-start = (bf16[8,32,768]{2,1,0:T(8,128)(2,1)S(1)}, bf16[8,32,768]{2,1,0:T(8,128)(2,1)S(1)}, u32[]{:S(2)}, u32[]{:S(2)}) collective-permute-start(bf16[8,32,768]{2,1,0:T(8,128)(2,1)S(1)} %all-to-all-done.line_ref.refs_0_), channel_id=1, source_target_pairs={{0,320},{1,41},{2,322},{3,43},{4,324},{5,45},{6,326},{7,47},{8,328... | collective-permute-start | bytes 1179656 | tf_op jit(solution)/shard_map/ppermute | solution.py:174
  38.3 42.2 %all-to-all-start.1 = ((bf16[16,40,1024]{2,1,0:T(8,128)(2,1)}), bf16[16,40,1024]{2,1,0:T(8,128)(2,1)}, u32[]{:S(2)}, u32[]{:S(2)}) async-start(bf16[16,40,1024]{2,1,0:T(8,128)(2,1)} %bitcast.4), calls=%async_computation.1 | async-start | bytes 2621440 | tf_op jit(solution)/shard_map/all_to_all | solution.py:186
  55.2 0.7 copy-start.2
  56.0 16.4 %collective-permute-start.2 = (bf16[20,32,768]{2,1,0:T(8,128)(2,1)S(1)}, bf16[20,32,768]{2,1,0:T(8,128)(2,1)S(1)}, u32[]{:S(2)}, u32[]{:S(2)}) collective-permute-start(bf16[20,32,768]{2,1,0:T(8,128)(2,1)S(1)} %get-tuple-element.10), channel_id=1, source_target_pairs={{0,64},{1,9},{2,66},{3,11},{4,68},{5,13},{6,70},{7,15},{8,72},{9,1... | collective-permute-start | bytes 2949128 | tf_op jit(solution)/shard_map/ppermute | solution.py:185
  57.9 16.4 %collective-permute-start.3 = (bf16[20,32,768]{2,1,0:T(8,128)(2,1)S(1)}, bf16[20,32,768]{2,1,0:T(8,128)(2,1)S(1)}, u32[]{:S(2)}, u32[]{:S(2)}) collective-permute-start(bf16[20,32,768]{2,1,0:T(8,128)(2,1)S(1)} %get-tuple-element.11), channel_id=1, source_target_pairs={{0,448},{1,57},{2,450},{3,59},{4,452},{5,61},{6,454},{7,63},{8,456... | collective-permute-start | bytes 2949128 | tf_op jit(solution)/shard_map/ppermute | solution.py:185
  80.5 1.0 copy-start.3
  81.5 11.4 %copy-start.6 = (s32[128,1]{0,1:T(1,128)S(1)}, s32[128,1]{0,1:T(1,128)}, u32[]{:S(2)}) copy-start(s32[128,1]{0,1:T(1,128)} %param.8) | copy-start | bytes 1540
  81.5 11.4 %copy-start.8 = (s32[128]{0:T(128)S(1)}, s32[128]{0:T(128)}, u32[]{:S(2)}) copy-start(s32[128]{0:T(128)} %copy-done.7) | copy-start | bytes 1540
  81.5 28.0 %copy-start = (bf16[128,1,1536]{2,0,1:T(8,128)(2,1)S(1)}, bf16[128,1,1536]{2,0,1:T(8,128)(2,1)}, u32[]{:S(2)}) copy-start(bf16[128,1,1536]{2,0,1:T(8,128)(2,1)} %param.6) | copy-start | bytes 1179652
  81.5 28.0 %copy-start.1 = (bf16[128,1]{0,1:T(2,128)(2,1)S(1)}, bf16[128,1]{0,1:T(2,128)(2,1)}, u32[]{:S(2)}) copy-start(bf16[128,1]{0,1:T(2,128)(2,1)} %param.7) | copy-start | bytes 772
  87.1 22.4 %all-to-all-start.2 = ((bf16[16,40,384]{2,1,0:T(8,128)(2,1)}), bf16[16,40,384]{2,1,0:T(8,128)(2,1)S(1)}, u32[]{:S(2)}, u32[]{:S(2)}) async-start(bf16[16,40,384]{2,1,0:T(8,128)(2,1)} %bitcast.6), calls=%async_computation.2 | async-start | bytes 983040 | tf_op jit(solution)/shard_map/all_to_all | solution.py:202

commit v12 on v11

--- a/solution.py
+++ b/solution.py
@@ -97,6 +97,11 @@
 
     give = (lax.broadcasted_iota(jnp.int32, (COUNT, COUNT), 0) == order((1, COUNT), 1)).astype(jnp.bfloat16)
     out_ref[...] = jnp.dot(give, back, preferred_element_type=jnp.float32).astype(jnp.bfloat16)
+
+
+def spread(own_ref, out_ref):
+    for i in range(RING):
+        out_ref[i] = own_ref[...]
 
 
 def join(line_ref, ahead_ref, behind_ref, up_ref, down_ref):
@@ -145,7 +150,12 @@
 
     own = down_weight[0]
     line = lax.all_to_all(
-        jnp.broadcast_to(own[None], (RING,) + own.shape),
+        pl.pallas_call(
+            spread,
+            out_shape=jax.ShapeDtypeStruct((RING,) + own.shape, jnp.bfloat16),
+            in_specs=[pl.BlockSpec(memory_space=pltpu.VMEM)],
+            out_specs=pl.BlockSpec(memory_space=pltpu.VMEM),
+        )(own),
         TORUS,
         split_axis=0,
         concat_axis=0,

time: 112 us -> 112 us (level)
  Pallas kernels: 7.14 us -> 8.8 us
  local copies, waits for them, and re-layouts: 3.41 us -> 1.75 us
    broadcast_in_dim x1 -> x0, local copies, waits for them, and re-layouts: 1.66 us -> none  [body(): jnp.broadcast_to(own[None], (RING,) + own.shape)]
    pallas_call x0 -> x1, Pallas kernels: none -> 1.66 us  [body(): pl.pallas_call(spread, out_shape=jax.ShapeDtypeStruct((RING,) + own.shape...]
where the time goes in v12:
time: 112 us; the launch traced here: 111 us
  waiting for transfers between devices  48.7 us (43%)
  starting transfers between devices  47.9 us (43%)
  Pallas kernels  8.8 us (8%)
  other arithmetic  2.29 us (2%)
  local copies, waits for them, and re-layouts  1.75 us (2%)
    all_to_all x1, waiting for transfers between devices, body(): lax.all_to_all(back.reshape(PEERS, 2 * CAP, FFW // 2), SHARE, split_axis=...  16.6 us
    all_to_all x1, starting transfers between devices, body(): got = lax.all_to_all(sent, SHARE, split_axis=0, concat_axis=0, tiled=True)  10.4 us
    ppermute x1, starting transfers between devices, body(): behind = lax.ppermute(line, TORUS, second_shift(3))  10.3 us
    ppermute x1, waiting for transfers between devices, body(): lax.ppermute(up, TORUS, second_shift(1))  9.94 us
    all_to_all x1, starting transfers between devices, body(): lax.all_to_all(pl.pallas_call(spread, out_shape=jax.ShapeDtypeStruct((RIN...  8.11 us
    all_to_all x1, waiting for transfers between devices, body(): lax.all_to_all(pl.pallas_call(spread, out_shape=jax.ShapeDtypeStruct((RIN...  7.58 us
    ppermute x1, starting transfers between devices, body(): ahead = lax.ppermute(line, TORUS, second_shift(-3))  6.77 us
    ppermute x1, waiting for transfers between devices, body(): ahead = lax.ppermute(line, TORUS, second_shift(-3))  6.5 us
  transfers between devices with their start and end apart: 7, of which 6 were waited for; matrix products, arithmetic and copies ran while one was open for 3% of the time, Pallas kernels for 0%

profile of v12, /device:TPU:1, one launch (start us, length us, event | category | flops | bytes accessed | tf_op | source)
XLA Modules:
  0.0 110.9 jit_solution(10880012485792846914)
XLA Ops:
  0.6 0.0 copy-start.5
  0.6 0.0 copy-start.4
  0.7 1.7 %shard_map.68 = bf16[8,32,768]{2,1,0:T(8,128)(2,1)} custom-call(bf16[32,768]{1,0:T(8,128)(2,1)} %bitcast.23), custom_call_target="tpu_custom_call" | custom-call | tf_op jit(solution)/shard_map/pallas_call | solution.py:153
  2.3 8.1 %all-to-all-start = ((bf16[8,32,768]{2,1,0:T(8,128)(2,1)}), bf16[8,32,768]{2,1,0:T(8,128)(2,1)S(1)}, u32[]{:S(2)}, u32[]{:S(2)}) async-start(bf16[8,32,768]{2,1,0:T(8,128)(2,1)} %shard_map.68), calls=%async_computation | async-start | bytes 786432 | tf_op jit(solution)/shard_map/all_to_all | solution.py:152
  10.4 0.7 fusion.10
  11.2 0.2 reduce_window_sum.11
  11.3 0.0 copy-done.5
  11.3 0.2 select_reduce_fusion
  11.5 0.0 copy-start.7
  11.6 0.1 fusion.13
  11.7 0.3 fusion
  12.0 0.0 copy-done.7
  12.0 0.3 fusion.1
  12.4 1.2 %pad_maximum_fusion = bf16[2,320,1024]{2,1,0:T(8,128)(2,1)} fusion(bf16[1,320,1024]{2,1,0:T(8,128)(2,1)S(1)} %fusion.1, bf16[1,320,1024]{2,1,0:T(8,128)(2,1)S(1)} %fusion), kind=kLoop, calls=%fused_computation.2 | loop fusion | flops 655360 | bytes 2621440 | tf_op jit(solution)/shard_map/stack | solution.py:173
  13.6 7.6 %all-to-all-done.line_ref.refs_0_ = bf16[8,32,768]{2,1,0:T(8,128)(2,1)S(1)} async-done(((bf16[8,32,768]{2,1,0:T(8,128)(2,1)}), bf16[8,32,768]{2,1,0:T(8,128)(2,1)S(1)}, u32[]{:S(2)}, u32[]{:S(2)}) %all-to-all-start) | async-done | bytes 393248 | tf_op jit(solution)/shard_map/all_to_all | solution.py:152
  21.2 10.3 %collective-permute-start.1 = (bf16[8,32,768]{2,1,0:T(8,128)(2,1)S(1)}, bf16[8,32,768]{2,1,0:T(8,128)(2,1)S(1)}, u32[]{:S(2)}, u32[]{:S(2)}) collective-permute-start(bf16[8,32,768]{2,1,0:T(8,128)(2,1)S(1)} %all-to-all-done.line_ref.refs_0_), channel_id=1, source_target_pairs={{0,192},{1,25},{2,194},{3,27},{4,196},{5,29},{6,198},{7,31},{8,200... | collective-permute-start | bytes 1179656 | tf_op jit(solution)/shard_map/ppermute | solution.py:185
  31.5 6.8 %collective-permute-start = (bf16[8,32,768]{2,1,0:T(8,128)(2,1)S(1)}, bf16[8,32,768]{2,1,0:T(8,128)(2,1)S(1)}, u32[]{:S(2)}, u32[]{:S(2)}) collective-permute-start(bf16[8,32,768]{2,1,0:T(8,128)(2,1)S(1)} %all-to-all-done.line_ref.refs_0_), channel_id=1, source_target_pairs={{0,320},{1,41},{2,322},{3,43},{4,324},{5,45},{6,326},{7,47},{8,328... | collective-permute-start | bytes 1179656 | tf_op jit(solution)/shard_map/ppermute | solution.py:184
  38.3 10.4 %all-to-all-start.1 = ((bf16[16,40,1024]{2,1,0:T(8,128)(2,1)}), bf16[16,40,1024]{2,1,0:T(8,128)(2,1)}, u32[]{:S(2)}, u32[]{:S(2)}) async-start(bf16[16,40,1024]{2,1,0:T(8,128)(2,1)} %bitcast.4), calls=%async_computation.1 | async-start | bytes 2621440 | tf_op jit(solution)/shard_map/all_to_all | solution.py:196
  48.7 0.0 collective-permute-done.1.behind_ref.refs_2_
  48.7 6.5 %collective-permute-done.ahead_ref.refs_1_ = bf16[8,32,768]{2,1,0:T(8,128)(2,1)S(1)} collective-permute-done((bf16[8,32,768]{2,1,0:T(8,128)(2,1)S(1)}, bf16[8,32,768]{2,1,0:T(8,128)(2,1)S(1)}, u32[]{:S(2)}, u32[]{:S(2)}) %collective-permute-start) | collective-permute-done | bytes 393248 | tf_op jit(solution)/shard_map/ppermute | solution.py:184
  55.2 0.1 shard_map.69
  55.3 0.6 copy-done.2
  56.0 1.9 %collective-permute-start.2 = (bf16[20,32,768]{2,1,0:T(8,128)(2,1)S(1)}, bf16[20,32,768]{2,1,0:T(8,128)(2,1)S(1)}, u32[]{:S(2)}, u32[]{:S(2)}) collective-permute-start(bf16[20,32,768]{2,1,0:T(8,128)(2,1)S(1)} %get-tuple-element.10), channel_id=1, source_target_pairs={{0,64},{1,9},{2,66},{3,11},{4,68},{5,13},{6,70},{7,15},{8,72},{9,1... | collective-permute-start | bytes 2949128 | tf_op jit(solution)/shard_map/ppermute | solution.py:195
  57.9 4.6 %collective-permute-start.3 = (bf16[20,32,768]{2,1,0:T(8,128)(2,1)S(1)}, bf16[20,32,768]{2,1,0:T(8,128)(2,1)S(1)}, u32[]{:S(2)}, u32[]{:S(2)}) collective-permute-start(bf16[20,32,768]{2,1,0:T(8,128)(2,1)S(1)} %get-tuple-element.11), channel_id=1, source_target_pairs={{0,448},{1,57},{2,450},{3,59},{4,452},{5,61},{6,454},{7,63},{8,456... | collective-permute-start | bytes 2949128 | tf_op jit(solution)/shard_map/ppermute | solution.py:195
  62.5 9.9 %collective-permute-done.2.refs_3_ = bf16[20,32,768]{2,1,0:T(8,128)(2,1)S(1)} collective-permute-done((bf16[20,32,768]{2,1,0:T(8,128)(2,1)S(1)}, bf16[20,32,768]{2,1,0:T(8,128)(2,1)S(1)}, u32[]{:S(2)}, u32[]{:S(2)}) %collective-permute-start.2) | collective-permute-done | bytes 983072 | tf_op jit(solution)/shard_map/ppermute | solution.py:195
  72.4 1.9 %collective-permute-done.3.refs_4_ = bf16[20,32,768]{2,1,0:T(8,128)(2,1)S(1)} collective-permute-done((bf16[20,32,768]{2,1,0:T(8,128)(2,1)S(1)}, bf16[20,32,768]{2,1,0:T(8,128)(2,1)S(1)}, u32[]{:S(2)}, u32[]{:S(2)}) %collective-permute-start.3) | collective-permute-done | bytes 983072 | tf_op jit(solution)/shard_map/ppermute | solution.py:195
  74.3 6.2 %all-to-all-done.1 = bf16[16,40,1024]{2,1,0:T(8,128)(2,1)} async-done(((bf16[16,40,1024]{2,1,0:T(8,128)(2,1)}), bf16[16,40,1024]{2,1,0:T(8,128)(2,1)}, u32[]{:S(2)}, u32[]{:S(2)}) %all-to-all-start.1) | async-done | bytes 1310752 | tf_op jit(solution)/shard_map/all_to_all | solution.py:196
  80.5 1.0 copy-done.3
  81.5 5.6 %shard_map.70 = bf16[640,384]{1,0:T(8,128)(2,1)} custom-call(bf16[640,1024]{1,0:T(8,128)(2,1)} %bitcast.5.got_ref, bf16[8,32,768]{2,1,0:T(8,128)(2,1)S(1)} %all-to-all-done.line_ref.refs_0_, bf16[8,32,768]{2,1,0:T(8,128)(2,1)S(1)} %copy-done.3, bf16[8,32,768]{2,1,0:T(8,128)(2,1)S(1)} %collective-permute-done.1.behind_ref.refs_2_, ...), custom_call_target="tpu_custom_call" | custom-call | flops 2000000000 | bytes 10000000 | tf_op jit(solution)/shard_map/pallas_call | solution.py:198
  87.1 5.8 %all-to-all-start.2 = ((bf16[16,40,384]{2,1,0:T(8,128)(2,1)}), bf16[16,40,384]{2,1,0:T(8,128)(2,1)S(1)}, u32[]{:S(2)}, u32[]{:S(2)}) async-start(bf16[16,40,384]{2,1,0:T(8,128)(2,1)} %bitcast.6), calls=%async_computation.2 | async-start | bytes 983040 | tf_op jit(solution)/shard_map/all_to_all | solution.py:212
  92.9 16.6 %all-to-all-done.2 = bf16[16,40,384]{2,1,0:T(8,128)(2,1)S(1)} async-done(((bf16[16,40,384]{2,1,0:T(8,128)(2,1)}), bf16[16,40,384]{2,1,0:T(8,128)(2,1)S(1)}, u32[]{:S(2)}, u32[]{:S(2)}) %all-to-all-start.2) | async-done | bytes 491552 | tf_op jit(solution)/shard_map/all_to_all | solution.py:212
  109.5 1.4 %shard_map.71 = (bf16[128,1536]{1,0:T(8,128)(2,1)}, bf16[1,128]{1,0:T(2,128)(2,1)}) custom-call(bf16[640,384]{1,0:T(8,128)(2,1)S(1)} %bitcast.20, bf16[128,1536]{1,0:T(8,128)(2,1)S(1)} %bitcast.21, bf16[1,128]{1,0:T(2,128)(2,1)S(1)} %bitcast.22, s32[1,128]{1,0:T(1,128)S(1)} %bitcast_add_fusion.first_ref), custom_call_target="tpu_custom_call" | custom-call | flops 200000000 | bytes 2000000 | tf_op jit(solution)/shard_map/pallas_call | solution.py:216
  (14 shorter events, 0.0 us)
Async XLA Ops:
  0.6 10.7 %copy-start.5 = (s32[128,1]{0,1:T(1,128)S(1)}, s32[128,1]{0,1:T(1,128)}, u32[]{:S(2)}) copy-start(s32[128,1]{0,1:T(1,128)} %param.8) | copy-start | bytes 1540
  0.6 10.9 %copy-start.4 = (bf16[128,4096]{1,0:T(8,128)(2,1)S(1)}, bf16[128,4096]{1,0:T(8,128)(2,1)}, u32[]{:S(2)}) copy-start(bf16[128,4096]{1,0:T(8,128)(2,1)} %param.5) | copy-start | bytes 3145732
  2.3 18.8 %all-to-all-start = ((bf16[8,32,768]{2,1,0:T(8,128)(2,1)}), bf16[8,32,768]{2,1,0:T(8,128)(2,1)S(1)}, u32[]{:S(2)}, u32[]{:S(2)}) async-start(bf16[8,32,768]{2,1,0:T(8,128)(2,1)} %shard_map.68), calls=%async_computation | async-start | bytes 786432 | tf_op jit(solution)/shard_map/all_to_all | solution.py:152
  11.5 0.5 copy-start.7
  21.2 27.6 %collective-permute-start.1 = (bf16[8,32,768]{2,1,0:T(8,128)(2,1)S(1)}, bf16[8,32,768]{2,1,0:T(8,128)(2,1)S(1)}, u32[]{:S(2)}, u32[]{:S(2)}) collective-permute-start(bf16[8,32,768]{2,1,0:T(8,128)(2,1)S(1)} %all-to-all-done.line_ref.refs_0_), channel_id=1, source_target_pairs={{0,192},{1,25},{2,194},{3,27},{4,196},{5,29},{6,198},{7,31},{8,200... | collective-permute-start | bytes 1179656 | tf_op jit(solution)/shard_map/ppermute | solution.py:185
  31.5 23.7 %collective-permute-start = (bf16[8,32,768]{2,1,0:T(8,128)(2,1)S(1)}, bf16[8,32,768]{2,1,0:T(8,128)(2,1)S(1)}, u32[]{:S(2)}, u32[]{:S(2)}) collective-permute-start(bf16[8,32,768]{2,1,0:T(8,128)(2,1)S(1)} %all-to-all-done.line_ref.refs_0_), channel_id=1, source_target_pairs={{0,320},{1,41},{2,322},{3,43},{4,324},{5,45},{6,326},{7,47},{8,328... | collective-permute-start | bytes 1179656 | tf_op jit(solution)/shard_map/ppermute | solution.py:184
  38.3 42.2 %all-to-all-start.1 = ((bf16[16,40,1024]{2,1,0:T(8,128)(2,1)}), bf16[16,40,1024]{2,1,0:T(8,128)(2,1)}, u32[]{:S(2)}, u32[]{:S(2)}) async-start(bf16[16,40,1024]{2,1,0:T(8,128)(2,1)} %bitcast.4), calls=%async_computation.1 | async-start | bytes 2621440 | tf_op jit(solution)/shard_map/all_to_all | solution.py:196
  55.2 0.7 copy-start.2
  56.0 16.4 %collective-permute-start.2 = (bf16[20,32,768]{2,1,0:T(8,128)(2,1)S(1)}, bf16[20,32,768]{2,1,0:T(8,128)(2,1)S(1)}, u32[]{:S(2)}, u32[]{:S(2)}) collective-permute-start(bf16[20,32,768]{2,1,0:T(8,128)(2,1)S(1)} %get-tuple-element.10), channel_id=1, source_target_pairs={{0,64},{1,9},{2,66},{3,11},{4,68},{5,13},{6,70},{7,15},{8,72},{9,1... | collective-permute-start | bytes 2949128 | tf_op jit(solution)/shard_map/ppermute | solution.py:195
  57.9 16.4 %collective-permute-start.3 = (bf16[20,32,768]{2,1,0:T(8,128)(2,1)S(1)}, bf16[20,32,768]{2,1,0:T(8,128)(2,1)S(1)}, u32[]{:S(2)}, u32[]{:S(2)}) collective-permute-start(bf16[20,32,768]{2,1,0:T(8,128)(2,1)S(1)} %get-tuple-element.11), channel_id=1, source_target_pairs={{0,448},{1,57},{2,450},{3,59},{4,452},{5,61},{6,454},{7,63},{8,456... | collective-permute-start | bytes 2949128 | tf_op jit(solution)/shard_map/ppermute | solution.py:195
  80.5 1.0 copy-start.3
  81.5 11.4 %copy-start.6 = (s32[128,1]{0,1:T(1,128)S(1)}, s32[128,1]{0,1:T(1,128)}, u32[]{:S(2)}) copy-start(s32[128,1]{0,1:T(1,128)} %param.8) | copy-start | bytes 1540
  81.5 11.4 %copy-start.8 = (s32[128]{0:T(128)S(1)}, s32[128]{0:T(128)}, u32[]{:S(2)}) copy-start(s32[128]{0:T(128)} %copy-done.7) | copy-start | bytes 1540
  81.5 28.0 %copy-start = (bf16[128,1,1536]{2,0,1:T(8,128)(2,1)S(1)}, bf16[128,1,1536]{2,0,1:T(8,128)(2,1)}, u32[]{:S(2)}) copy-start(bf16[128,1,1536]{2,0,1:T(8,128)(2,1)} %param.6) | copy-start | bytes 1179652
  81.5 28.0 %copy-start.1 = (bf16[128,1]{0,1:T(2,128)(2,1)S(1)}, bf16[128,1]{0,1:T(2,128)(2,1)}, u32[]{:S(2)}) copy-start(bf16[128,1]{0,1:T(2,128)(2,1)} %param.7) | copy-start | bytes 772
  87.1 22.4 %all-to-all-start.2 = ((bf16[16,40,384]{2,1,0:T(8,128)(2,1)}), bf16[16,40,384]{2,1,0:T(8,128)(2,1)S(1)}, u32[]{:S(2)}, u32[]{:S(2)}) async-start(bf16[16,40,384]{2,1,0:T(8,128)(2,1)} %bitcast.6), calls=%async_computation.2 | async-start | bytes 983040 | tf_op jit(solution)/shard_map/all_to_all | solution.py:212
